TPU v7x, 32 devices: a whole 2x2x4 slice. The times are simulated.
32 devices in a mesh: grp: 4 (over x, core), dev: 8 (over z, y).
Axes of the slice: x: 2, y: 2, z: 4, core: 2. Of those that a mesh axis runs over, the one named last changes fastest.
Arguments:
- node_latent: bfloat16 [32, 128, 256], P(('grp', 'dev')), may hold values from -6 to 6
- edge_latent: bfloat16 [32, 384, 256], P(('grp', 'dev')), may hold values from -6 to 6
- cut_latent: bfloat16 [32, 5, 64, 256], P(('grp', 'dev')), may hold values from -6 to 6
- node_cotangent: bfloat16 [32, 128, 256], P(('grp', 'dev')), may hold values from -6 to 6
- edge_sender: int32 [32, 384], P(('grp', 'dev')), may hold values from 0 to 127, as said below
- edge_receiver: int32 [32, 384], P(('grp', 'dev')), may hold values from 0 to 127, as said below
- boundary_rows: int32 [32, 5, 16], P(('grp', 'dev')), may hold values from 0 to 127, as said below
- cut_slot: int32 [32, 5, 64], P(('grp', 'dev')), may hold values from 0 to 15
- cut_receiver: int32 [32, 5, 64], P(('grp', 'dev')), may hold values from 0 to 127, as said below
- node_count: int32 [32], P(('grp', 'dev')), may hold values from 64 to 128, as said below
- edge_count: int32 [32], P(('grp', 'dev')), may hold values from 192 to 384, as said below
- edge_first: bfloat16 [768, 256], replicated, may hold values from -0.21875 to 0.21875
- edge_second: bfloat16 [256, 256], replicated, may hold values from -0.375 to 0.375
- edge_gain: float32 [256], replicated, may hold values from 0.1 to 1.9
- node_first: bfloat16 [512, 256], replicated, may hold values from -0.25 to 0.25
- node_second: bfloat16 [256, 256], replicated, may hold values from -0.375 to 0.375
- node_gain: float32 [256], replicated, may hold values from 0.1 to 1.9
Outputs:
- updated_nodes: bfloat16 [32, 128, 256], P(('grp', 'dev'))
- node_gradient: bfloat16 [32, 128, 256], P(('grp', 'dev'))
- edge_gradient: bfloat16 [32, 384, 256], P(('grp', 'dev'))
- cut_gradient: bfloat16 [32, 5, 64, 256], P(('grp', 'dev'))
Inputs may be any that keep to these rules, and one draw needn't show every extreme that they name: Nodes at or beyond a partition's node_count are padding. Inner edges at or beyond a partition's edge_count are padding. `edge_sender`: a node of the partition below its node_count. `edge_receiver`: a node of the partition below its node_count. `boundary_rows`: a node of the partition below its node_count; a node may stand more than once. `cut_receiver`: a node of the partition below its node_count.
All inputs are finite; a program needn't handle non-finite values.
Results may differ from a plain program's by a relative error of at most 0.0095.
Values may be sent and summed in bfloat16 or wider, within the bound.
No kernel may reach another device: no remote copies, remote signals or barrier semaphores. Data moves between devices by JAX's collectives and lax.ppermute only.
A program may use at most 64 MiB of HBM per device.

v0:
```python
import jax
import jax.numpy as jnp
from jax import lax
from jax.sharding import PartitionSpec as P

ROUNDS = 5


epsilon = 1e-05


def partner(shard, axis, apart):
    return lax.ppermute(shard, axis, [(i, i ^ 1 << apart) for i in range(lax.axis_size(axis))])


def layer_norm(values, gain):
    centre = jnp.mean(values, axis=-1, keepdims=True)
    centred = values - centre
    variance = jnp.mean(centred * centred, axis=-1, keepdims=True)
    inverse = 1.0 / jnp.sqrt(variance + epsilon)
    normed = centred * inverse
    return (normed * gain, normed, inverse)


def norm_backward(upstream, gain, normed, inverse):
    scaled = upstream * gain
    first_mean = jnp.mean(scaled, axis=-1, keepdims=True)
    second_mean = jnp.mean(scaled * normed, axis=-1, keepdims=True)
    return inverse * (scaled - first_mean - normed * second_mean)


def silu_slope(values):
    sigmoid = jax.nn.sigmoid(values)
    return sigmoid * (1.0 + values * (1.0 - sigmoid))


def slot_total(slot_ids, values, count):
    table = (slot_ids[None, :] == jnp.arange(count)[:, None]).astype(jnp.float32)
    return jnp.dot(
        table, values, precision=lax.Precision.HIGHEST, preferred_element_type=jnp.float32
    )


def swap_rows(outgoing, round_index):
    if round_index < 2:
        return partner(outgoing, "grp", round_index)
    return partner(outgoing, "dev", round_index - 2)


def swap_slopes(payload, round_index):
    if round_index < 2:
        return partner((payload[0], payload[1]), "grp", round_index)
    return partner((payload[0], payload[1]), "dev", round_index - 2)


def shards(
    node_latent,
    edge_latent,
    cut_latent,
    node_cotangent,
    edge_sender,
    edge_receiver,
    boundary_rows,
    cut_slot,
    cut_receiver,
    node_count,
    edge_count,
    edge_first,
    edge_second,
    edge_gain,
    node_first,
    node_second,
    node_gain,
):
    nodes = node_latent[0]
    edges = edge_latent[0]
    cut_edges = cut_latent[0]
    cotangent = node_cotangent[0]
    senders = edge_sender[0]
    receivers_local = edge_receiver[0]
    boundary = boundary_rows[0]
    slots = cut_slot[0]
    cut_targets = cut_receiver[0]
    width = nodes.shape[1]
    node_rows = nodes.shape[0]
    edge_rows = edges.shape[0]
    send_rows = boundary.shape[1]
    valid = (jnp.arange(node_rows) < node_count[0]).astype(jnp.float32)[:, None]
    used = (jnp.arange(edge_rows) < edge_count[0]).astype(jnp.float32)
    sender_block = edge_first[width : 2 * width]
    other_block = jnp.concatenate([edge_first[:width], edge_first[2 * width :]], 0)
    cut_flat = cut_targets.reshape(-1)
    pieces = []
    for round_index in range(ROUNDS):
        outgoing = nodes[boundary[round_index]]
        arrived = swap_rows(outgoing, round_index)
        pieces.append(
            jnp.concatenate(
                [
                    nodes[cut_targets[round_index]],
                    arrived[slots[round_index]],
                    cut_edges[round_index],
                ],
                1,
            )
        )
    local_input = jnp.concatenate([nodes[receivers_local], nodes[senders], edges], 1)
    pre_local = jnp.dot(local_input, edge_first, preferred_element_type=jnp.float32)
    pre_cut = jnp.dot(jnp.concatenate(pieces, 0), edge_first, preferred_element_type=jnp.float32)
    pre_edge = jnp.concatenate([pre_local, pre_cut], 0)
    receivers = jnp.concatenate([receivers_local, cut_flat])
    mask = jnp.concatenate([used, jnp.ones((cut_flat.shape[0],), jnp.float32)])[:, None]
    act_edge = jax.nn.silu(pre_edge).astype(jnp.bfloat16)
    out_edge = jnp.dot(act_edge, edge_second, preferred_element_type=jnp.float32)
    normed_edge, edge_normed, edge_inverse = layer_norm(out_edge, edge_gain)
    message = normed_edge * mask
    received_sum = jnp.zeros((node_rows, width), jnp.float32).at[receivers].add(message)
    node_input = jnp.concatenate([nodes, received_sum.astype(jnp.bfloat16)], 1)
    pre_node = jnp.dot(node_input, node_first, preferred_element_type=jnp.float32)
    act_node = jax.nn.silu(pre_node).astype(jnp.bfloat16)
    out_node = jnp.dot(act_node, node_second, preferred_element_type=jnp.float32)
    normed_node, node_normed, node_inverse = layer_norm(out_node, node_gain)
    updated = ((nodes.astype(jnp.float32) + normed_node) * valid).astype(jnp.bfloat16)
    masked_cotangent = cotangent.astype(jnp.float32) * valid
    grad_out_node = norm_backward(masked_cotangent, node_gain, node_normed, node_inverse).astype(
        jnp.bfloat16
    )
    grad_act_node = jnp.dot(grad_out_node, node_second.T, preferred_element_type=jnp.float32)
    grad_pre_node = (grad_act_node * silu_slope(pre_node)).astype(jnp.bfloat16)
    grad_node_input = jnp.dot(grad_pre_node, node_first.T, preferred_element_type=jnp.float32)
    grad_message = grad_node_input[:, width:][receivers] * mask
    grad_out_edge = norm_backward(grad_message, edge_gain, edge_normed, edge_inverse).astype(
        jnp.bfloat16
    )
    grad_act_edge = jnp.dot(grad_out_edge, edge_second.T, preferred_element_type=jnp.float32)
    grad_pre_edge = (grad_act_edge * silu_slope(pre_edge)).astype(jnp.bfloat16)
    local_grad = jnp.dot(
        grad_pre_edge[:edge_rows], edge_first.T, preferred_element_type=jnp.float32
    )
    gradient = masked_cotangent + grad_node_input[:, :width]
    gradient = gradient.at[receivers_local].add(local_grad[:, :width])
    gradient = gradient.at[senders].add(local_grad[:, width : 2 * width])
    edge_gradient = local_grad[:, 2 * width :].astype(jnp.bfloat16)
    cut_pre = grad_pre_edge[edge_rows:]
    cut_grad = jnp.dot(cut_pre, other_block.T, preferred_element_type=jnp.float32)
    gradient = gradient.at[cut_flat].add(cut_grad[:, :width])
    cut_gradient = cut_grad[:, width:]
    per_round = cut_pre.reshape(ROUNDS, -1, width)
    for round_index in range(ROUNDS):
        arrived_grad, arrived_slots = swap_slopes(
            (per_round[round_index], slots[round_index]), round_index
        )
        sender_grad = jnp.dot(arrived_grad, sender_block.T, preferred_element_type=jnp.float32)
        gradient = gradient.at[boundary[round_index]].add(
            slot_total(arrived_slots, sender_grad, send_rows)
        )
    cut_gradient = cut_gradient.reshape(ROUNDS, -1, width).astype(jnp.bfloat16)
    return (
        updated[None],
        gradient.astype(jnp.bfloat16)[None],
        edge_gradient[None],
        cut_gradient[None],
    )


def solution(mesh):
    placed = (
        P(("grp", "dev"), None, None),
        P(("grp", "dev"), None, None),
        P(("grp", "dev"), None, None, None),
        P(("grp", "dev"), None, None),
        P(("grp", "dev"), None),
        P(("grp", "dev"), None),
        P(("grp", "dev"), None, None),
        P(("grp", "dev"), None, None),
        P(("grp", "dev"), None, None),
        P(("grp", "dev")),
        P(("grp", "dev")),
        P(),
        P(),
        P(),
        P(),
        P(),
        P(),
    )
    return jax.shard_map(
        shards,
        mesh=mesh,
        in_specs=placed,
        out_specs=(
            P(("grp", "dev"), None, None),
            P(("grp", "dev"), None, None),
            P(("grp", "dev"), None, None),
            P(("grp", "dev"), None, None, None),
        ),
        check_vma=False,
    )
```

profile of v0, /device:TPU:0, one launch (start us, length us, event | category | flops | bytes accessed | tf_op | source)
XLA Modules:
  0.0 85.3 jit_solution(15569808436556546893)
XLA Ops:
  0.7 0.8 fusion.112
  1.5 1.4 %gather_fusion.3 = bf16[16,256]{1,0:T(8,128)(2,1)S(1)} fusion(bf16[128,256]{1,0:T(8,128)(2,1)} %bitcast.128, s32[1024]{0:T(1024)S(1)} %pad_clamp_fusion.14), kind=kCustom, calls=%fused_computation.3 | custom fusion | bytes 16448 | tf_op jit(solution)/shard_map/gather | solution.py:95
  3.4 1.4 %gather_fusion.6 = bf16[16,256]{1,0:T(8,128)(2,1)S(1)} fusion(bf16[128,256]{1,0:T(8,128)(2,1)} %bitcast.129, s32[1024]{0:T(1024)S(1)} %pad_clamp_fusion.11), kind=kCustom, calls=%fused_computation.6 | custom fusion | bytes 16448 | tf_op jit(solution)/shard_map/gather | solution.py:95
  4.8 2.6 %collective-permute-start.1 = (bf16[16,256]{1,0:T(8,128)(2,1)S(1)}, bf16[16,256]{1,0:T(8,128)(2,1)S(1)}, u32[]{:S(2)}, u32[]{:S(2)}) collective-permute-start(bf16[16,256]{1,0:T(8,128)(2,1)S(1)} %gather_fusion.6), channel_id=1, source_target_pairs={{0,16},{8,24},{16,0},{24,8},{1,17},{9,25},{17,1},{25,9},{2,18},{10... | collective-permute-start | bytes 24584 | tf_op jit(solution)/shard_map/ppermute | solution.py:13
  7.4 1.4 %gather_fusion.9 = bf16[16,256]{1,0:T(8,128)(2,1)S(1)} fusion(bf16[128,256]{1,0:T(8,128)(2,1)} %bitcast.130, s32[1024]{0:T(1024)S(1)} %pad_clamp_fusion.8), kind=kCustom, calls=%fused_computation.9 | custom fusion | bytes 16448 | tf_op jit(solution)/shard_map/gather | solution.py:95
  8.8 1.6 %collective-permute-start.2 = (bf16[16,256]{1,0:T(8,128)(2,1)S(1)}, bf16[16,256]{1,0:T(8,128)(2,1)S(1)}, u32[]{:S(2)}, u32[]{:S(2)}) collective-permute-start(bf16[16,256]{1,0:T(8,128)(2,1)S(1)} %gather_fusion.9), channel_id=1, source_target_pairs={{0,1},{1,0},{2,3},{3,2},{4,5},{5,4},{6,7},{7,6},{8,9},{9,8},{10,11... | collective-permute-start | bytes 24584 | tf_op jit(solution)/shard_map/ppermute | solution.py:13
  10.4 1.4 %gather_fusion.12 = bf16[16,256]{1,0:T(8,128)(2,1)S(1)} fusion(bf16[128,256]{1,0:T(8,128)(2,1)} %bitcast.131, s32[1024]{0:T(1024)S(1)} %pad_clamp_fusion.5), kind=kCustom, calls=%fused_computation.12 | custom fusion | bytes 16448 | tf_op jit(solution)/shard_map/gather | solution.py:95
  11.9 1.6 %collective-permute-start.3 = (bf16[16,256]{1,0:T(8,128)(2,1)S(1)}, bf16[16,256]{1,0:T(8,128)(2,1)S(1)}, u32[]{:S(2)}, u32[]{:S(2)}) collective-permute-start(bf16[16,256]{1,0:T(8,128)(2,1)S(1)} %gather_fusion.12), channel_id=1, source_target_pairs={{0,2},{1,3},{2,0},{3,1},{4,6},{5,7},{6,4},{7,5},{8,10},{9,11},{10,... | collective-permute-start | bytes 24584 | tf_op jit(solution)/shard_map/ppermute | solution.py:13
  13.5 1.4 %gather_fusion.15 = bf16[16,256]{1,0:T(8,128)(2,1)S(1)} fusion(bf16[128,256]{1,0:T(8,128)(2,1)} %bitcast.132, s32[1024]{0:T(1024)S(1)} %pad_clamp_fusion.2), kind=kCustom, calls=%fused_computation.15 | custom fusion | bytes 16448 | tf_op jit(solution)/shard_map/gather | solution.py:95
  14.9 2.7 %collective-permute-start.4 = (bf16[16,256]{1,0:T(8,128)(2,1)S(1)}, bf16[16,256]{1,0:T(8,128)(2,1)S(1)}, u32[]{:S(2)}, u32[]{:S(2)}) collective-permute-start(bf16[16,256]{1,0:T(8,128)(2,1)S(1)} %gather_fusion.15), channel_id=1, source_target_pairs={{0,4},{1,5},{2,6},{3,7},{4,0},{5,1},{6,2},{7,3},{8,12},{9,13},{10,... | collective-permute-start | bytes 24584 | tf_op jit(solution)/shard_map/ppermute | solution.py:13
  22.6 0.8 slice_bitcast_fusion
  24.2 2.1 %gather_fusion.1 = bf16[384,256]{1,0:T(8,128)(2,1)S(1)} fusion(bf16[128,256]{1,0:T(8,128)(2,1)S(1)} %bitcast.133, s32[1024]{0:T(1024)S(1)} %get-tuple-element.48), kind=kCustom, calls=%fused_computation.1 | custom fusion | bytes 394752 | tf_op jit(solution)/shard_map/gather | solution.py:107
  26.3 2.1 %gather_fusion = bf16[384,256]{1,0:T(8,128)(2,1)S(1)} fusion(bf16[128,256]{1,0:T(8,128)(2,1)S(1)} %bitcast.134, s32[1024]{0:T(1024)S(1)} %pad_clamp_fusion.17), kind=kCustom, calls=%fused_computation | custom fusion | bytes 394752 | tf_op jit(solution)/shard_map/gather | solution.py:107
  39.5 6.7 %scatter_custom_fusion = f32[128,256]{1,0:T(8,128)S(1)} fusion(s32[704]{0:T(1024)S(1)} %fusion.95, f32[704,256]{1,0:T(8,128)S(1)} %get-tuple-element.44, f32[704]{0:T(1024)S(1)} %pad_convert_fusion, f32[256]{0:T(256)S(1)} %copy-done.4, f32[704]{0:T(1024)S(1)} %add_rsqrt_fusion, f32[704]{0:T(1024)S(1)} %broadcast_multiply_fusion.2, f32[]{:T(128)} %constant.11.clone.1), kind=kCustom, calls=%fused_computation.36 | custom fusion | flops 901120 | bytes 865284 | tf_op jit(solution)/shard_map/scatter-add | solution.py:117
  47.0 0.8 fusion.45
  48.2 2.2 %gather_fusion.17 = f32[704,256]{1,0:T(8,128)S(1)} fusion(f32[128,256]{1,0:T(8,128)S(1)} %get-tuple-element.15, s32[1024]{0:T(1024)S(1)} %get-tuple-element.47), kind=kCustom, calls=%fused_computation.17 | custom fusion | bytes 1444608 | tf_op jit(solution)/shard_map/gather | solution.py:131
  51.5 1.0 %fusion = bf16[704,256]{1,0:T(8,128)(2,1)S(1)} fusion(bf16[256,256]{1,0:T(8,128)(2,1)S(1)} %copy-done.8, f32[320,256]{1,0:T(8,128)S(1)} %fusion.126, f32[384,256]{1,0:T(8,128)S(1)} %copy-done.10, f32[704,256]{1,0:T(8,128)S(1)} %get-tuple-element.44, f32[704,256]{1,0:T(8,128)S(1)} %gather_fusion.17, f32[704]{0:T(1024)S(1)} %broadcast_multiply_fusion, ...), kind=kOutput, calls=%fused_computation.28 | convolution fusion | flops 95698944 | bytes 2669312 | tf_op jit(solution)/shard_map/dot_general | solution.py:135
  53.9 2.9 %scatter_custom_fusion.1 = f32[128,256]{1,0:T(8,128)S(1)} fusion(f32[128,256]{1,0:T(8,128)S(1)} %get-tuple-element.16, s32[384]{0:T(512)S(1)} %fusion.96, f32[384,768]{1,0:T(8,128)S(1)} %fusion.35), kind=kCustom, calls=%fused_computation.53 | custom fusion | flops 98304 | bytes 524288 | tf_op jit(solution)/shard_map/scatter-add | solution.py:141
  56.8 2.7 %scatter_custom_fusion.2 = f32[128,256]{1,0:T(8,128)S(1)} fusion(f32[128,256]{1,0:T(8,128)S(1)} %scatter_custom_fusion.1, s32[384]{0:T(512)S(1)} %fusion.97, f32[384,768]{1,0:T(8,128)S(1)} %fusion.35), kind=kCustom, calls=%fused_computation.51 | custom fusion | flops 98304 | bytes 524288 | tf_op jit(solution)/shard_map/scatter-add | solution.py:142
  60.2 2.4 %scatter_custom_fusion.3 = f32[128,256]{1,0:T(8,128)S(1)} fusion(f32[128,256]{1,0:T(8,128)S(1)} %scatter_custom_fusion.2, s32[320]{0:T(512)S(1)} %fusion.98, f32[320,512]{1,0:T(8,128)S(1)} %fusion.30), kind=kCustom, calls=%fused_computation.67 | custom fusion | flops 81920 | bytes 458752 | tf_op jit(solution)/shard_map/scatter-add | solution.py:146
  62.7 1.6 %collective-permute-start.8 = (bf16[64,256]{1,0:T(8,128)(2,1)S(1)}, bf16[64,256]{1,0:T(8,128)(2,1)S(1)}, u32[]{:S(2)}, u32[]{:S(2)}) collective-permute-start(bf16[64,256]{1,0:T(8,128)(2,1)S(1)} %get-tuple-element.13), channel_id=1, source_target_pairs={{0,16},{8,24},{16,0},{24,8},{1,17},{9,25},{17,1},{25,9},{2,18},{10... | collective-permute-start | bytes 98312 | tf_op jit(solution)/shard_map/ppermute | solution.py:13
  64.4 2.3 %collective-permute-done.8 = bf16[64,256]{1,0:T(8,128)(2,1)S(1)} collective-permute-done((bf16[64,256]{1,0:T(8,128)(2,1)S(1)}, bf16[64,256]{1,0:T(8,128)(2,1)S(1)}, u32[]{:S(2)}, u32[]{:S(2)}) %collective-permute-start.8) | collective-permute-done | bytes 32800 | tf_op jit(solution)/shard_map/ppermute | solution.py:13
  66.6 1.5 %collective-permute-start.10 = (bf16[64,256]{1,0:T(8,128)(2,1)S(1)}, bf16[64,256]{1,0:T(8,128)(2,1)S(1)}, u32[]{:S(2)}, u32[]{:S(2)}) collective-permute-start(bf16[64,256]{1,0:T(8,128)(2,1)S(1)} %get-tuple-element.12), channel_id=1, source_target_pairs={{0,1},{1,0},{2,3},{3,2},{4,5},{5,4},{6,7},{7,6},{8,9},{9,8},{10,11... | collective-permute-start | bytes 98312 | tf_op jit(solution)/shard_map/ppermute | solution.py:13
  68.3 2.2 %collective-permute-done.10 = bf16[64,256]{1,0:T(8,128)(2,1)S(1)} collective-permute-done((bf16[64,256]{1,0:T(8,128)(2,1)S(1)}, bf16[64,256]{1,0:T(8,128)(2,1)S(1)}, u32[]{:S(2)}, u32[]{:S(2)}) %collective-permute-start.10) | collective-permute-done | bytes 32800 | tf_op jit(solution)/shard_map/ppermute | solution.py:13
  70.5 1.6 %collective-permute-start.12 = (bf16[64,256]{1,0:T(8,128)(2,1)S(1)}, bf16[64,256]{1,0:T(8,128)(2,1)S(1)}, u32[]{:S(2)}, u32[]{:S(2)}) collective-permute-start(bf16[64,256]{1,0:T(8,128)(2,1)S(1)} %get-tuple-element.11), channel_id=1, source_target_pairs={{0,2},{1,3},{2,0},{3,1},{4,6},{5,7},{6,4},{7,5},{8,10},{9,11},{10,... | collective-permute-start | bytes 98312 | tf_op jit(solution)/shard_map/ppermute | solution.py:13
  72.3 2.2 %collective-permute-done.12 = bf16[64,256]{1,0:T(8,128)(2,1)S(1)} collective-permute-done((bf16[64,256]{1,0:T(8,128)(2,1)S(1)}, bf16[64,256]{1,0:T(8,128)(2,1)S(1)}, u32[]{:S(2)}, u32[]{:S(2)}) %collective-permute-start.12) | collective-permute-done | bytes 32800 | tf_op jit(solution)/shard_map/ppermute | solution.py:13
  74.6 4.6 %collective-permute-done.14 = bf16[64,256]{1,0:T(8,128)(2,1)S(1)} collective-permute-done((bf16[64,256]{1,0:T(8,128)(2,1)S(1)}, bf16[64,256]{1,0:T(8,128)(2,1)S(1)}, u32[]{:S(2)}, u32[]{:S(2)}) %collective-permute-start.14) | collective-permute-done | bytes 32800 | tf_op jit(solution)/shard_map/ppermute | solution.py:13
  80.1 0.8 scatter_fusion
  80.9 0.8 scatter_fusion.1
  81.6 0.8 scatter_fusion.2
  82.4 0.8 scatter_fusion.3
  83.9 0.8 scatter_fusion.4
  (116 shorter events, 22.8 us)
Async XLA Ops:
  0.6 45.6 %copy-start = (bf16[512,256]{1,0:T(8,128)(2,1)S(1)}, bf16[512,256]{1,0:T(8,128)(2,1)}, u32[]{:S(2)}) copy-start(bf16[512,256]{1,0:T(8,128)(2,1)} %param.31) | copy-start | bytes 786436
  0.6 23.5 %copy-start.1 = (bf16[1,128,256]{2,1,0:T(8,128)(2,1)S(1)}, bf16[1,128,256]{2,1,0:T(8,128)(2,1)}, u32[]{:S(2)}) copy-start(bf16[1,128,256]{2,1,0:T(8,128)(2,1)} %param.17) | copy-start | bytes 196612
  2.9 30.1 %collective-permute-start = (bf16[16,256]{1,0:T(8,128)(2,1)S(1)}, bf16[16,256]{1,0:T(8,128)(2,1)S(1)}, u32[]{:S(2)}, u32[]{:S(2)}) collective-permute-start(bf16[16,256]{1,0:T(8,128)(2,1)S(1)} %gather_fusion.3), channel_id=1, source_target_pairs={{0,8},{8,0},{16,24},{24,16},{1,9},{9,1},{17,25},{25,17},{2,10},{10... | collective-permute-start | bytes 24584 | tf_op jit(solution)/shard_map/ppermute | solution.py:13
  4.8 29.0 %collective-permute-start.1 = (bf16[16,256]{1,0:T(8,128)(2,1)S(1)}, bf16[16,256]{1,0:T(8,128)(2,1)S(1)}, u32[]{:S(2)}, u32[]{:S(2)}) collective-permute-start(bf16[16,256]{1,0:T(8,128)(2,1)S(1)} %gather_fusion.6), channel_id=1, source_target_pairs={{0,16},{8,24},{16,0},{24,8},{1,17},{9,25},{17,1},{25,9},{2,18},{10... | collective-permute-start | bytes 24584 | tf_op jit(solution)/shard_map/ppermute | solution.py:13
  8.8 26.3 %collective-permute-start.2 = (bf16[16,256]{1,0:T(8,128)(2,1)S(1)}, bf16[16,256]{1,0:T(8,128)(2,1)S(1)}, u32[]{:S(2)}, u32[]{:S(2)}) collective-permute-start(bf16[16,256]{1,0:T(8,128)(2,1)S(1)} %gather_fusion.9), channel_id=1, source_target_pairs={{0,1},{1,0},{2,3},{3,2},{4,5},{5,4},{6,7},{7,6},{8,9},{9,8},{10,11... | collective-permute-start | bytes 24584 | tf_op jit(solution)/shard_map/ppermute | solution.py:13
  11.9 24.6 %collective-permute-start.3 = (bf16[16,256]{1,0:T(8,128)(2,1)S(1)}, bf16[16,256]{1,0:T(8,128)(2,1)S(1)}, u32[]{:S(2)}, u32[]{:S(2)}) collective-permute-start(bf16[16,256]{1,0:T(8,128)(2,1)S(1)} %gather_fusion.12), channel_id=1, source_target_pairs={{0,2},{1,3},{2,0},{3,1},{4,6},{5,7},{6,4},{7,5},{8,10},{9,11},{10,... | collective-permute-start | bytes 24584 | tf_op jit(solution)/shard_map/ppermute | solution.py:13
  14.9 22.7 %collective-permute-start.4 = (bf16[16,256]{1,0:T(8,128)(2,1)S(1)}, bf16[16,256]{1,0:T(8,128)(2,1)S(1)}, u32[]{:S(2)}, u32[]{:S(2)}) collective-permute-start(bf16[16,256]{1,0:T(8,128)(2,1)S(1)} %gather_fusion.15), channel_id=1, source_target_pairs={{0,4},{1,5},{2,6},{3,7},{4,0},{5,1},{6,2},{7,3},{8,12},{9,13},{10,... | collective-permute-start | bytes 24584 | tf_op jit(solution)/shard_map/ppermute | solution.py:13
  26.2 2.8 %copy-start.2 = (bf16[768,256]{1,0:T(8,128)(2,1)S(1)}, bf16[768,256]{1,0:T(8,128)(2,1)}, u32[]{:S(2)}) copy-start(bf16[768,256]{1,0:T(8,128)(2,1)} %param.28) | copy-start | bytes 1179652
  26.3 2.9 %copy-start.6 = (bf16[1,384,256]{2,1,0:T(8,128)(2,1)S(1)}, bf16[1,384,256]{2,1,0:T(8,128)(2,1)}, u32[]{:S(2)}) copy-start(bf16[1,384,256]{2,1,0:T(8,128)(2,1)} %param.18) | copy-start | bytes 589828
  29.5 9.3 %copy-start.9 = (f32[384,256]{1,0:T(8,128)}, f32[384,256]{1,0:T(8,128)S(1)}, u32[]{:S(2)}) copy-start(f32[384,256]{1,0:T(8,128)S(1)} %fusion.6) | copy-start | bytes 1179652
  33.0 46.5 %collective-permute-start.5 = (s32[64]{0:T(128)S(1)}, s32[64]{0:T(128)S(1)}, u32[]{:S(2)}, u32[]{:S(2)}) collective-permute-start(s32[64]{0:T(128)S(1)} %get-tuple-element.24), channel_id=1, source_target_pairs={{0,8},{8,0},{16,24},{24,16},{1,9},{9,1},{17,25},{25,17},{2,10},{10... | collective-permute-start | bytes 776 | tf_op jit(solution)/shard_map/ppermute | solution.py:13
  33.8 45.8 %collective-permute-start.7 = (s32[64]{0:T(128)S(1)}, s32[64]{0:T(128)S(1)}, u32[]{:S(2)}, u32[]{:S(2)}) collective-permute-start(s32[64]{0:T(128)S(1)} %get-tuple-element.25), channel_id=1, source_target_pairs={{0,16},{8,24},{16,0},{24,8},{1,17},{9,25},{17,1},{25,9},{2,18},{10... | collective-permute-start | bytes 776 | tf_op jit(solution)/shard_map/ppermute | solution.py:13
  35.1 44.7 %collective-permute-start.9 = (s32[64]{0:T(128)S(1)}, s32[64]{0:T(128)S(1)}, u32[]{:S(2)}, u32[]{:S(2)}) collective-permute-start(s32[64]{0:T(128)S(1)} %get-tuple-element.26), channel_id=1, source_target_pairs={{0,1},{1,0},{2,3},{3,2},{4,5},{5,4},{6,7},{7,6},{8,9},{9,8},{10,11... | collective-permute-start | bytes 776 | tf_op jit(solution)/shard_map/ppermute | solution.py:13
  36.4 2.3 %copy-start.8 = (bf16[256,256]{1,0:T(8,128)(2,1)S(1)}, bf16[256,256]{1,0:T(8,128)(2,1)}, u32[]{:S(2)}) copy-start(bf16[256,256]{1,0:T(8,128)(2,1)} %param.29) | copy-start | bytes 393220
  36.4 43.5 %collective-permute-start.11 = (s32[64]{0:T(128)S(1)}, s32[64]{0:T(128)S(1)}, u32[]{:S(2)}, u32[]{:S(2)}) collective-permute-start(s32[64]{0:T(128)S(1)} %get-tuple-element.27), channel_id=1, source_target_pairs={{0,2},{1,3},{2,0},{3,1},{4,6},{5,7},{6,4},{7,5},{8,10},{9,11},{10,... | collective-permute-start | bytes 776 | tf_op jit(solution)/shard_map/ppermute | solution.py:13
  38.7 0.8 copy-start.4
  39.2 7.3 %copy-start.7 = (bf16[256,256]{1,0:T(8,128)(2,1)S(1)}, bf16[256,256]{1,0:T(8,128)(2,1)}, u32[]{:S(2)}) copy-start(bf16[256,256]{1,0:T(8,128)(2,1)} %param.32) | copy-start | bytes 393220
  39.5 7.4 %copy-start.3 = (bf16[1,128,256]{2,1,0:T(8,128)(2,1)S(1)}, bf16[1,128,256]{2,1,0:T(8,128)(2,1)}, u32[]{:S(2)}) copy-start(bf16[1,128,256]{2,1,0:T(8,128)(2,1)} %param.20) | copy-start | bytes 196612
  39.5 7.4 %copy-start.5 = (f32[256]{0:T(256)S(1)}, f32[256]{0:T(256)}, u32[]{:S(2)}) copy-start(f32[256]{0:T(256)} %param.33) | copy-start | bytes 3076
  50.5 1.0 %copy-start.10 = (f32[384,256]{1,0:T(8,128)S(1)}, f32[384,256]{1,0:T(8,128)}, u32[]{:S(2)}) copy-start(f32[384,256]{1,0:T(8,128)} %copy-done.9) | copy-start | bytes 1179652
  52.8 9.8 %collective-permute-start.6 = (bf16[64,256]{1,0:T(8,128)(2,1)S(1)}, bf16[64,256]{1,0:T(8,128)(2,1)S(1)}, u32[]{:S(2)}, u32[]{:S(2)}) collective-permute-start(bf16[64,256]{1,0:T(8,128)(2,1)S(1)} %get-tuple-element.14), channel_id=1, source_target_pairs={{0,8},{8,0},{16,24},{24,16},{1,9},{9,1},{17,25},{25,17},{2,10},{10... | collective-permute-start | bytes 98312 | tf_op jit(solution)/shard_map/ppermute | solution.py:13
  62.7 4.0 %collective-permute-start.8 = (bf16[64,256]{1,0:T(8,128)(2,1)S(1)}, bf16[64,256]{1,0:T(8,128)(2,1)S(1)}, u32[]{:S(2)}, u32[]{:S(2)}) collective-permute-start(bf16[64,256]{1,0:T(8,128)(2,1)S(1)} %get-tuple-element.13), channel_id=1, source_target_pairs={{0,16},{8,24},{16,0},{24,8},{1,17},{9,25},{17,1},{25,9},{2,18},{10... | collective-permute-start | bytes 98312 | tf_op jit(solution)/shard_map/ppermute | solution.py:13
  66.6 3.9 %collective-permute-start.10 = (bf16[64,256]{1,0:T(8,128)(2,1)S(1)}, bf16[64,256]{1,0:T(8,128)(2,1)S(1)}, u32[]{:S(2)}, u32[]{:S(2)}) collective-permute-start(bf16[64,256]{1,0:T(8,128)(2,1)S(1)} %get-tuple-element.12), channel_id=1, source_target_pairs={{0,1},{1,0},{2,3},{3,2},{4,5},{5,4},{6,7},{7,6},{8,9},{9,8},{10,11... | collective-permute-start | bytes 98312 | tf_op jit(solution)/shard_map/ppermute | solution.py:13
  70.5 3.9 %collective-permute-start.12 = (bf16[64,256]{1,0:T(8,128)(2,1)S(1)}, bf16[64,256]{1,0:T(8,128)(2,1)S(1)}, u32[]{:S(2)}, u32[]{:S(2)}) collective-permute-start(bf16[64,256]{1,0:T(8,128)(2,1)S(1)} %get-tuple-element.11), channel_id=1, source_target_pairs={{0,2},{1,3},{2,0},{3,1},{4,6},{5,7},{6,4},{7,5},{8,10},{9,11},{10,... | collective-permute-start | bytes 98312 | tf_op jit(solution)/shard_map/ppermute | solution.py:13
  74.5 4.8 %collective-permute-start.14 = (bf16[64,256]{1,0:T(8,128)(2,1)S(1)}, bf16[64,256]{1,0:T(8,128)(2,1)S(1)}, u32[]{:S(2)}, u32[]{:S(2)}) collective-permute-start(bf16[64,256]{1,0:T(8,128)(2,1)S(1)} %get-tuple-element.10), channel_id=1, source_target_pairs={{0,4},{1,5},{2,6},{3,7},{4,0},{5,1},{6,2},{7,3},{8,12},{9,13},{10,... | collective-permute-start | bytes 98312 | tf_op jit(solution)/shard_map/ppermute | solution.py:13
  79.3 4.4 %collective-permute-start.13 = (s32[64]{0:T(128)S(1)}, s32[64]{0:T(128)S(1)}, u32[]{:S(2)}, u32[]{:S(2)}) collective-permute-start(s32[64]{0:T(128)S(1)} %get-tuple-element.23), channel_id=1, source_target_pairs={{0,4},{1,5},{2,6},{3,7},{4,0},{5,1},{6,2},{7,3},{8,12},{9,13},{10,... | collective-permute-start | bytes 776 | tf_op jit(solution)/shard_map/ppermute | solution.py:13
where the time goes:
time: 85.9 us; the launch traced here: 85.3 us
  other arithmetic  26.3 us (31%)
  local copies, waits for them, and re-layouts  24 us (28%)
  starting transfers between devices  15.5 us (18%)
  waiting for transfers between devices  11.9 us (14%)
  matrix products  4.95 us (6%)
  between operations  2.6 us (3%)
    ppermute x15, starting transfers between devices, partner(): lax.ppermute(shard, axis, [(i, i ^ 1 << apart) for i in range(lax.axis_si...  15.5 us
    ppermute x15, waiting for transfers between devices, partner(): lax.ppermute(shard, axis, [(i, i ^ 1 << apart) for i in range(lax.axis_si...  11.9 us
    gather x5, local copies, waits for them, and re-layouts, shards(): outgoing = nodes[boundary[round_index]]  7.12 us
    scatter-add x1, other arithmetic, shards(): jnp.zeros((node_rows, width), jnp.float32).at[receivers].add(message)  6.69 us
    scatter-add x5, other arithmetic, shards(): gradient.at[boundary[round_index]]  3.82 us
    gather x5, local copies, waits for them, and re-layouts, shards(): nodes[cut_targets[round_index]]  3.5 us
    gather x5, local copies, waits for them, and re-layouts, shards(): arrived[slots[round_index]]  3.49 us
    scatter-add x1, other arithmetic, shards(): gradient = gradient.at[receivers_local].add(local_grad[:, :width])  2.91 us
  transfers between devices with their start and end apart: 15, of which 5 were waited for; matrix products, arithmetic and copies ran while one was open for 60% of the time, Pallas kernels for 0%

commit v1 on v0

v1 whole, which is shorter than its diff:
```python
import functools

import jax
import jax.numpy as jnp
from jax import lax
from jax.experimental import pallas as pl
from jax.experimental.pallas import tpu as pltpu
from jax.sharding import PartitionSpec as P

ROUNDS = 5
GRP_ROUNDS = 2

epsilon = 1e-05

bf16 = jnp.bfloat16
f32 = jnp.float32


def partner(shard, round_index):
    axis, apart = ("grp", round_index) if round_index < GRP_ROUNDS else ("dev", round_index - GRP_ROUNDS)
    return lax.ppermute(shard, axis, [(i, i ^ 1 << apart) for i in range(lax.axis_size(axis))])


def mm(a, b):
    return jnp.dot(a, b, preferred_element_type=f32)


def mm_t(a, b):
    return lax.dot_general(a, b, (((1,), (1,)), ((), ())), preferred_element_type=f32)


def t_mm(a, b):
    return lax.dot_general(a, b, (((0,), (0,)), ((), ())), preferred_element_type=f32)


def hot(row, count):
    shape = (count, row.shape[1])
    return (lax.broadcasted_iota(jnp.int32, shape, 0) == jnp.broadcast_to(row, shape)).astype(f32)


def lane_mean(values):
    return jnp.mean(values, axis=-1, keepdims=True)


def norm_parts(values):
    centred = values - lane_mean(values)
    inverse = lax.rsqrt(lane_mean(centred * centred) + epsilon)
    return centred * inverse, inverse


def norm_backward(scaled, normed, inverse):
    return inverse * (scaled - lane_mean(scaled) - normed * lane_mean(scaled * normed))


def silu_parts(values):
    sigmoid = jax.nn.sigmoid(values)
    act = values * sigmoid
    return act, sigmoid + act * (1.0 - sigmoid)


def send_kernel(nodes, boundary, *out):
    table = jnp.concatenate([hot(boundary[r], nodes.shape[0]) for r in range(ROUNDS)], 1)
    rows = t_mm(table.astype(bf16), nodes[...]).astype(bf16)
    send = boundary.shape[2]
    for r in range(ROUNDS):
        out[r][...] = rows[r * send : (r + 1) * send]


def main_kernel(
    node_count, edge_count, nodes, edges, cuts, cotangent, sender, receiver, slot, cut_receiver,
    edge_first, edge_second, edge_gain, node_first, node_second, node_gain,
    *rest,
):
    arrived = rest[:ROUNDS]
    updated, base, grad_pre = rest[ROUNDS : ROUNDS + 3]
    back = rest[ROUNDS + 3 :]
    n, width = nodes.shape
    e = edges.shape[0]
    send = arrived[0].shape[0]
    x = nodes[...]
    edge_lane = lax.broadcasted_iota(jnp.int32, (1, e), 1)
    receive_inner = jnp.where(edge_lane < edge_count[0], receiver[...], -1)
    hot_receive = jnp.concatenate(
        [hot(receive_inner, n)] + [hot(cut_receiver[r], n) for r in range(ROUNDS)], 1
    )
    slots = jnp.concatenate([slot[r] + r * send for r in range(ROUNDS)], 1)
    hot_slot = hot(slots, 128)
    hot_send = hot(sender[...], n)
    gather_receive = hot_receive.T.astype(bf16)
    gather_send = jnp.concatenate([hot_send, hot_slot], 1).T.astype(bf16)
    scatter_receive = hot_receive.astype(bf16)

    w1 = edge_first[:width]
    w2 = edge_first[width : 2 * width]
    w3 = edge_first[2 * width :]
    far = jnp.concatenate([a[...] for a in arrived] + [jnp.zeros((128 - ROUNDS * send, width), bf16)], 0)
    by_receiver = mm(x, w1).astype(bf16)
    by_sender = mm(jnp.concatenate([x, far], 0), w2).astype(bf16)
    gather_inner = jnp.concatenate([gather_receive[:e], gather_send[:e]], 1)
    gather_cut = jnp.concatenate([gather_receive[e:], gather_send[e:]], 1)
    pre_inner = mm(gather_inner, jnp.concatenate([by_receiver, by_sender[:n]], 0)) + mm(edges[...], w3)
    pre_cut = mm(gather_cut, jnp.concatenate([by_receiver, by_sender[n:]], 0)) + mm(cuts[...], w3)
    pre = jnp.concatenate([pre_inner, pre_cut], 0)
    act, slope = silu_parts(pre)
    normed, inverse = norm_parts(mm(act.astype(bf16), edge_second[...]))
    received = mm(scatter_receive, normed.astype(bf16)) * edge_gain[...]

    valid = lax.broadcasted_iota(jnp.int32, (n, 1), 0) < node_count[0]
    pre_node = mm(jnp.concatenate([x, received.astype(bf16)], 1), node_first[...])
    act_node, slope_node = silu_parts(pre_node)
    normed_node, inverse_node = norm_parts(mm(act_node.astype(bf16), node_second[...]))
    updated[...] = jnp.where(valid, x.astype(f32) + normed_node * node_gain[...], 0.0).astype(bf16)
    masked = jnp.where(valid, cotangent[...].astype(f32), 0.0)
    grad_out_node = norm_backward(masked * node_gain[...], normed_node, inverse_node).astype(bf16)
    grad_pre_node = (mm_t(grad_out_node, node_second[...]) * slope_node).astype(bf16)
    base[...] = masked + mm_t(grad_pre_node, node_first[:width])
    at_receiver = mm_t(grad_pre_node, node_first[width:]) * edge_gain[...]
    high = at_receiver.astype(bf16)
    low = (at_receiver - high.astype(f32)).astype(bf16)
    scaled = mm(jnp.concatenate([gather_receive, gather_receive], 1), jnp.concatenate([high, low], 0))
    grad_out = norm_backward(scaled, normed, inverse).astype(bf16)
    grad = (mm_t(grad_out, edge_second[...]) * slope).astype(bf16)
    grad_pre[...] = grad
    sums = mm(hot_slot.astype(bf16), grad[e:]).astype(bf16)
    for r in range(ROUNDS):
        back[r][...] = sums[r * send : (r + 1) * send]


def last_kernel(
    base, grad_pre, sender, receiver, cut_receiver, boundary, edge_first, *rest
):
    arrived = rest[:ROUNDS]
    node_gradient, edge_gradient, cut_gradient = rest[ROUNDS:]
    n, width = base.shape
    e = edge_gradient.shape[0]
    grad = grad_pre[...]
    by_edge = mm_t(grad, edge_first[2 * width :]).astype(bf16)
    edge_gradient[...] = by_edge[:e]
    cut_gradient[...] = by_edge[e:]
    hot_receive = jnp.concatenate(
        [hot(receiver[...], n)] + [hot(cut_receiver[r], n) for r in range(ROUNDS)], 1
    ).astype(bf16)
    hot_boundary = jnp.concatenate([hot(boundary[r], n) for r in range(ROUNDS)], 1).astype(bf16)
    at_receiver = mm(hot_receive, grad).astype(bf16)
    far = jnp.concatenate([a[...] for a in arrived], 0)
    at_sender = (mm(hot(sender[...], n).astype(bf16), grad[:e]) + mm(hot_boundary, far)).astype(bf16)
    total = base[...] + mm_t(at_receiver, edge_first[:width]) + mm_t(at_sender, edge_first[width : 2 * width])
    node_gradient[...] = total.astype(bf16)


VMEM = pl.BlockSpec(memory_space=pltpu.VMEM)
SMEM = pl.BlockSpec(memory_space=pltpu.SMEM)


def call(kernel, out_shape, in_specs, args, flops):
    size = sum(a.size * a.dtype.itemsize for a in list(args) + list(out_shape))
    return pl.pallas_call(
        kernel,
        out_shape=out_shape,
        in_specs=in_specs,
        out_specs=[VMEM] * len(out_shape),
        compiler_params=pltpu.CompilerParams(vmem_limit_bytes=32 * 1024 * 1024),
        cost_estimate=pl.CostEstimate(flops=flops, bytes_accessed=size, transcendentals=0),
    )(*args)


def shards(
    node_latent, edge_latent, cut_latent, node_cotangent, edge_sender, edge_receiver, boundary_rows,
    cut_slot, cut_receiver, node_count, edge_count, edge_first, edge_second, edge_gain, node_first,
    node_second, node_gain,
):
    nodes = node_latent[0]
    edges = edge_latent[0]
    cuts = cut_latent[0].reshape(-1, cut_latent.shape[-1])
    n, width = nodes.shape
    e, c = edges.shape[0], cuts.shape[0]
    boundary = boundary_rows.transpose(1, 0, 2)
    slot = cut_slot.transpose(1, 0, 2)
    cut_targets = cut_receiver.transpose(1, 0, 2)
    send = boundary.shape[2]
    shape = jax.ShapeDtypeStruct
    sent = call(
        send_kernel, [shape((send, width), bf16)] * ROUNDS, [VMEM] * 2, (nodes, boundary),
        2 * 128 * n * width,
    )
    arrived = [partner(sent[r], r) for r in range(ROUNDS)]
    outs = call(
        main_kernel,
        [shape((n, width), bf16), shape((n, width), f32), shape((e + c, width), bf16)]
        + [shape((send, width), bf16)] * ROUNDS,
        [SMEM] * 2 + [VMEM] * (14 + ROUNDS),
        (
            node_count, edge_count, nodes, edges, cuts, node_cotangent[0], edge_sender, edge_receiver, slot,
            cut_targets, edge_first, edge_second, edge_gain[None], node_first, node_second, node_gain[None],
            *arrived,
        ),
        2 * (e + c) * width * width * 6,
    )
    updated, base, grad_pre = outs[:3]
    returned = [partner(outs[3 + r], r) for r in range(ROUNDS)]
    node_gradient, edge_gradient, cut_gradient = call(
        last_kernel,
        [shape((n, width), bf16), shape((e, width), bf16), shape((c, width), bf16)],
        [VMEM] * (7 + ROUNDS),
        (base, grad_pre, edge_sender, edge_receiver, cut_targets, boundary, edge_first, *returned),
        2 * (e + c) * width * width * 2,
    )
    return (
        updated[None],
        node_gradient[None],
        edge_gradient[None],
        cut_gradient.reshape(cut_latent.shape),
    )


def solution(mesh):
    part = ("grp", "dev")
    placed = tuple(P(part, *[None] * (d - 1)) for d in (3, 3, 4, 3, 2, 2, 3, 3, 3, 1, 1)) + (P(),) * 6
    return jax.shard_map(
        shards,
        mesh=mesh,
        in_specs=placed,
        out_specs=tuple(P(part, *[None] * (d - 1)) for d in (3, 3, 3, 4)),
        check_vma=False,
    )
```

time: 85.9 us -> 29.8 us (0.35)
  other arithmetic: 26.3 us -> 0 us
  local copies, waits for them, and re-layouts: 24 us -> 7.84 us
  waiting for transfers between devices: 11.9 us -> 2.42 us
  matrix products: 4.95 us -> 0 us
  Pallas kernels: 0 us -> 4.32 us
  starting transfers between devices: 15.5 us -> 12.8 us
    gather x18 -> x0, local copies, waits for them, and re-layouts: 20.5 us -> none  [the longest x5 7.12 us: shards(): outgoing = nodes[boundary[round_index]]]
    scatter-add x9 -> x0, other arithmetic: 18.6 us -> none  [the longest x1 6.69 us: shards(): jnp.zeros((node_rows, width), jnp.float32).at[receivers].add(message)]
    ppermute x15 -> x10, waiting for transfers between devices: 11.9 us -> 2.42 us  [partner(): lax.ppermute(shard, axis, [(i, i ^ 1 << apart) for i in range(lax.axis_si...]
    unnamed x22 -> x32, local copies, waits for them, and re-layouts: 0.45 us -> 7.84 us
    dot_general x19 -> x0, matrix products: 4.95 us -> none  [the longest x1 0.96 us: shards(): jnp.dot(grad_out_edge, edge_second.T, preferred_element_type=jnp.float32)]
    select_n x7 -> x0, other arithmetic: 4.35 us -> none  [the longest x1 0.79 us: shards(): outgoing = nodes[boundary[round_index]]]
    pallas_call x0 -> x3, Pallas kernels: none -> 4.32 us  [call(): pl.pallas_call(kernel, out_shape=out_shape, in_specs=in_specs, out_specs=...]
    ppermute x15 -> x10, starting transfers between devices: 15.5 us -> 12.8 us  [partner(): lax.ppermute(shard, axis, [(i, i ^ 1 << apart) for i in range(lax.axis_si...]
  transfers between devices with their start and end apart: 15 -> 10, of which waited for: 5 -> 4; matrix products, arithmetic and copies ran while one was open for 60% -> 0% of each run, Pallas kernels for 0% -> 0%
where the time goes in v1:
time: 29.8 us; the launch traced here: 29.4 us
  starting transfers between devices  12.8 us (43%)
  local copies, waits for them, and re-layouts  7.84 us (26%)
  Pallas kernels  4.32 us (14%)
  waiting for transfers between devices  2.42 us (8%)
  between operations  2.03 us (7%)
    ppermute x10, starting transfers between devices, partner(): lax.ppermute(shard, axis, [(i, i ^ 1 << apart) for i in range(lax.axis_si...  12.8 us
    unnamed x32, local copies, waits for them, and re-layouts  7.84 us
    pallas_call x3, Pallas kernels, call(): pl.pallas_call(kernel, out_shape=out_shape, in_specs=in_specs, out_specs=...  4.32 us
    ppermute x10, waiting for transfers between devices, partner(): lax.ppermute(shard, axis, [(i, i ^ 1 << apart) for i in range(lax.axis_si...  2.42 us
  transfers between devices with their start and end apart: 10, of which 4 were waited for; matrix products, arithmetic and copies ran while one was open for 0% of the time, Pallas kernels for 0%

profile of v1, /device:TPU:0, one launch (start us, length us, event | category | flops | bytes accessed | tf_op | source)
XLA Modules:
  0.0 29.4 jit_solution(14121948087551148784)
XLA Ops:
  0.6 0.7 %copy-done.3 = s32[1,5,16]{2,0,1:T(1,128)S(1)} copy-done((s32[1,5,16]{2,0,1:T(1,128)S(1)}, s32[1,5,16]{2,0,1:T(1,128)}, u32[]{:S(2)}) %copy-start.3) | copy-done | bytes 344
  1.3 0.8 %copy-done.2 = bf16[1,128,256]{2,1,0:T(8,128)(2,1)S(1)} copy-done((bf16[1,128,256]{2,1,0:T(8,128)(2,1)S(1)}, bf16[1,128,256]{2,1,0:T(8,128)(2,1)}, u32[]{:S(2)}) %copy-start.2) | copy-done | bytes 65560
  2.2 0.3 shard_map.192
  2.4 0.5 %collective-permute-start = (bf16[16,256]{1,0:T(8,128)(2,1)S(1)}, bf16[16,256]{1,0:T(8,128)(2,1)S(1)}, u32[]{:S(2)}, u32[]{:S(2)}) collective-permute-start(bf16[16,256]{1,0:T(8,128)(2,1)S(1)} %get-tuple-element.20), channel_id=1, source_target_pairs={{0,8},{8,0},{16,24},{24,16},{1,9},{9,1},{17,25},{25,17},{2,10},{10... | collective-permute-start | bytes 24584 | tf_op jit(solution)/shard_map/ppermute | solution.py:21
  3.0 2.6 %collective-permute-start.1 = (bf16[16,256]{1,0:T(8,128)(2,1)S(1)}, bf16[16,256]{1,0:T(8,128)(2,1)S(1)}, u32[]{:S(2)}, u32[]{:S(2)}) collective-permute-start(bf16[16,256]{1,0:T(8,128)(2,1)S(1)} %get-tuple-element.21), channel_id=1, source_target_pairs={{0,16},{8,24},{16,0},{24,8},{1,17},{9,25},{17,1},{25,9},{2,18},{10... | collective-permute-start | bytes 24584 | tf_op jit(solution)/shard_map/ppermute | solution.py:21
  5.5 1.5 %collective-permute-start.2 = (bf16[16,256]{1,0:T(8,128)(2,1)S(1)}, bf16[16,256]{1,0:T(8,128)(2,1)S(1)}, u32[]{:S(2)}, u32[]{:S(2)}) collective-permute-start(bf16[16,256]{1,0:T(8,128)(2,1)S(1)} %get-tuple-element.22), channel_id=1, source_target_pairs={{0,1},{1,0},{2,3},{3,2},{4,5},{5,4},{6,7},{7,6},{8,9},{9,8},{10,11... | collective-permute-start | bytes 24584 | tf_op jit(solution)/shard_map/ppermute | solution.py:21
  7.0 1.6 %collective-permute-start.3 = (bf16[16,256]{1,0:T(8,128)(2,1)S(1)}, bf16[16,256]{1,0:T(8,128)(2,1)S(1)}, u32[]{:S(2)}, u32[]{:S(2)}) collective-permute-start(bf16[16,256]{1,0:T(8,128)(2,1)S(1)} %get-tuple-element.23), channel_id=1, source_target_pairs={{0,2},{1,3},{2,0},{3,1},{4,6},{5,7},{6,4},{7,5},{8,10},{9,11},{10,... | collective-permute-start | bytes 24584 | tf_op jit(solution)/shard_map/ppermute | solution.py:21
  8.6 2.6 %collective-permute-start.4 = (bf16[16,256]{1,0:T(8,128)(2,1)S(1)}, bf16[16,256]{1,0:T(8,128)(2,1)S(1)}, u32[]{:S(2)}, u32[]{:S(2)}) collective-permute-start(bf16[16,256]{1,0:T(8,128)(2,1)S(1)} %get-tuple-element.24), channel_id=1, source_target_pairs={{0,4},{1,5},{2,6},{3,7},{4,0},{5,1},{6,2},{7,3},{8,12},{9,13},{10,... | collective-permute-start | bytes 24584 | tf_op jit(solution)/shard_map/ppermute | solution.py:21
  12.5 0.6 %collective-permute-done.4.rest_4_ = bf16[16,256]{1,0:T(8,128)(2,1)S(1)} collective-permute-done((bf16[16,256]{1,0:T(8,128)(2,1)S(1)}, bf16[16,256]{1,0:T(8,128)(2,1)S(1)}, u32[]{:S(2)}, u32[]{:S(2)}) %collective-permute-start.4) | collective-permute-done | bytes 8224 | tf_op jit(solution)/shard_map/ppermute | solution.py:21
  13.2 0.0 copy-start.5
  13.2 0.0 copy-start.6
  13.2 0.6 %copy-done.15 = f32[256]{0:T(256)S(1)} copy-done((f32[256]{0:T(256)S(1)}, f32[256]{0:T(256)}, u32[]{:S(2)}) %copy-start.15) | copy-done | bytes 1048
  13.8 0.0 copy-done.13
  13.9 0.0 copy-done.14
  13.9 0.0 copy-done.4
  13.9 0.0 copy-done.5
  13.9 0.0 copy-done.6
  13.9 1.0 %copy-done = bf16[768,256]{1,0:T(8,128)(2,1)S(1)} copy-done((bf16[768,256]{1,0:T(8,128)(2,1)S(1)}, bf16[768,256]{1,0:T(8,128)(2,1)}, u32[]{:S(2)}) %copy-start) | copy-done | bytes 393240
  14.9 0.9 %copy-done.7 = bf16[512,256]{1,0:T(8,128)(2,1)S(1)} copy-done((bf16[512,256]{1,0:T(8,128)(2,1)S(1)}, bf16[512,256]{1,0:T(8,128)(2,1)}, u32[]{:S(2)}) %copy-start.7) | copy-done | bytes 262168
  15.9 0.9 %copy-done.8 = bf16[1,384,256]{2,1,0:T(8,128)(2,1)S(1)} copy-done((bf16[1,384,256]{2,1,0:T(8,128)(2,1)S(1)}, bf16[1,384,256]{2,1,0:T(8,128)(2,1)}, u32[]{:S(2)}) %copy-start.8) | copy-done | bytes 196632
  16.8 0.9 %copy-done.9 = bf16[1,5,64,256]{3,2,1,0:T(8,128)(2,1)S(1)} copy-done((bf16[1,5,64,256]{3,2,1,0:T(8,128)(2,1)S(1)}, bf16[1,5,64,256]{3,2,1,0:T(8,128)(2,1)}, u32[]{:S(2)}) %copy-start.9) | copy-done | bytes 163864
  17.7 0.9 %copy-done.10 = bf16[256,256]{1,0:T(8,128)(2,1)S(1)} copy-done((bf16[256,256]{1,0:T(8,128)(2,1)S(1)}, bf16[256,256]{1,0:T(8,128)(2,1)}, u32[]{:S(2)}) %copy-start.10) | copy-done | bytes 131096
  18.6 0.9 %copy-done.11 = bf16[256,256]{1,0:T(8,128)(2,1)S(1)} copy-done((bf16[256,256]{1,0:T(8,128)(2,1)S(1)}, bf16[256,256]{1,0:T(8,128)(2,1)}, u32[]{:S(2)}) %copy-start.11) | copy-done | bytes 131096
  19.5 2.9 %shard_map.193 = (bf16[128,256]{1,0:T(8,128)(2,1)}, f32[128,256]{1,0:T(8,128)S(1)}, bf16[704,256]{1,0:T(8,128)(2,1)S(1)}, bf16[16,256]{1,0:T(8,128)(2,1)S(1)}, b...) custom-call(s32[1]{0:T(128)S(6)} %copy.21.node_count, ...), custom_call_target="tpu_custom_call" | custom-call | flops 553648128 | bytes 2055688 | tf_op jit(solution)/shard_map/pallas_call | solution.py:157
  22.5 0.5 %collective-permute-start.6 = (bf16[16,256]{1,0:T(8,128)(2,1)S(1)}, bf16[16,256]{1,0:T(8,128)(2,1)S(1)}, u32[]{:S(2)}, u32[]{:S(2)}) collective-permute-start(bf16[16,256]{1,0:T(8,128)(2,1)S(1)} %get-tuple-element.29), channel_id=1, source_target_pairs={{0,16},{8,24},{16,0},{24,8},{1,17},{9,25},{17,1},{25,9},{2,18},{10... | collective-permute-start | bytes 24584 | tf_op jit(solution)/shard_map/ppermute | solution.py:21
  23.0 0.5 %collective-permute-start.7 = (bf16[16,256]{1,0:T(8,128)(2,1)S(1)}, bf16[16,256]{1,0:T(8,128)(2,1)S(1)}, u32[]{:S(2)}, u32[]{:S(2)}) collective-permute-start(bf16[16,256]{1,0:T(8,128)(2,1)S(1)} %get-tuple-element.30), channel_id=1, source_target_pairs={{0,1},{1,0},{2,3},{3,2},{4,5},{5,4},{6,7},{7,6},{8,9},{9,8},{10,11... | collective-permute-start | bytes 24584 | tf_op jit(solution)/shard_map/ppermute | solution.py:21
  23.5 0.2 collective-permute-start.8
  23.7 2.8 %collective-permute-start.9 = (bf16[16,256]{1,0:T(8,128)(2,1)S(1)}, bf16[16,256]{1,0:T(8,128)(2,1)S(1)}, u32[]{:S(2)}, u32[]{:S(2)}) collective-permute-start(bf16[16,256]{1,0:T(8,128)(2,1)S(1)} %get-tuple-element.32), channel_id=1, source_target_pairs={{0,4},{1,5},{2,6},{3,7},{4,0},{5,1},{6,2},{7,3},{8,12},{9,13},{10,... | collective-permute-start | bytes 24584 | tf_op jit(solution)/shard_map/ppermute | solution.py:21
  26.5 0.1 collective-permute-done.7.rest_2_
  26.6 0.6 %collective-permute-done.8.rest_3_ = bf16[16,256]{1,0:T(8,128)(2,1)S(1)} collective-permute-done((bf16[16,256]{1,0:T(8,128)(2,1)S(1)}, bf16[16,256]{1,0:T(8,128)(2,1)S(1)}, u32[]{:S(2)}, u32[]{:S(2)}) %collective-permute-start.8) | collective-permute-done | bytes 8224 | tf_op jit(solution)/shard_map/ppermute | solution.py:21
  27.2 1.1 %collective-permute-done.9.rest_4_ = bf16[16,256]{1,0:T(8,128)(2,1)S(1)} collective-permute-done((bf16[16,256]{1,0:T(8,128)(2,1)S(1)}, bf16[16,256]{1,0:T(8,128)(2,1)S(1)}, u32[]{:S(2)}, u32[]{:S(2)}) %collective-permute-start.9) | collective-permute-done | bytes 8224 | tf_op jit(solution)/shard_map/ppermute | solution.py:21
  28.3 1.1 %shard_map.194 = (bf16[128,256]{1,0:T(8,128)(2,1)}, bf16[384,256]{1,0:T(8,128)(2,1)}, bf16[320,256]{1,0:T(8,128)(2,1)}) custom-call(f32[128,256]{1,0:T(8,128)S(1)} %get-tuple-element.26.base, bf16[704,256]{1,0:T(8,128)(2,1)S(1)} %get-tuple-element.27.grad_pre, s32[1,384]{1,0:T(1,128)S(1)} %copy-done.5, s32[1,384]{1,0:T(1,128)S(1)} %copy-done.6, ...), custom_call_target="tpu_custom_call" | custom-call | flops 184549376 | bytes 1356352 | tf_op jit(solution)/shard_map/pallas_call | solution.py:157
  (23 shorter events, 0.0 us)
Async XLA Ops:
  0.6 0.7 %copy-start.3 = (s32[1,5,16]{2,0,1:T(1,128)S(1)}, s32[1,5,16]{2,0,1:T(1,128)}, u32[]{:S(2)}) copy-start(s32[1,5,16]{2,0,1:T(1,128)} %param.23) | copy-start | bytes 964
  1.3 0.8 %copy-start.2 = (bf16[1,128,256]{2,1,0:T(8,128)(2,1)S(1)}, bf16[1,128,256]{2,1,0:T(8,128)(2,1)}, u32[]{:S(2)}) copy-start(bf16[1,128,256]{2,1,0:T(8,128)(2,1)} %param.17) | copy-start | bytes 196612
  2.2 11.0 %copy-start.12 = (bf16[1,128,256]{2,1,0:T(8,128)(2,1)S(1)}, bf16[1,128,256]{2,1,0:T(8,128)(2,1)}, u32[]{:S(2)}) copy-start(bf16[1,128,256]{2,1,0:T(8,128)(2,1)} %param.20) | copy-start | bytes 196612
  2.4 10.1 %collective-permute-start = (bf16[16,256]{1,0:T(8,128)(2,1)S(1)}, bf16[16,256]{1,0:T(8,128)(2,1)S(1)}, u32[]{:S(2)}, u32[]{:S(2)}) collective-permute-start(bf16[16,256]{1,0:T(8,128)(2,1)S(1)} %get-tuple-element.20), channel_id=1, source_target_pairs={{0,8},{8,0},{16,24},{24,16},{1,9},{9,1},{17,25},{25,17},{2,10},{10... | collective-permute-start | bytes 24584 | tf_op jit(solution)/shard_map/ppermute | solution.py:21
  3.0 9.6 %collective-permute-start.1 = (bf16[16,256]{1,0:T(8,128)(2,1)S(1)}, bf16[16,256]{1,0:T(8,128)(2,1)S(1)}, u32[]{:S(2)}, u32[]{:S(2)}) collective-permute-start(bf16[16,256]{1,0:T(8,128)(2,1)S(1)} %get-tuple-element.21), channel_id=1, source_target_pairs={{0,16},{8,24},{16,0},{24,8},{1,17},{9,25},{17,1},{25,9},{2,18},{10... | collective-permute-start | bytes 24584 | tf_op jit(solution)/shard_map/ppermute | solution.py:21
  5.5 7.0 %collective-permute-start.2 = (bf16[16,256]{1,0:T(8,128)(2,1)S(1)}, bf16[16,256]{1,0:T(8,128)(2,1)S(1)}, u32[]{:S(2)}, u32[]{:S(2)}) collective-permute-start(bf16[16,256]{1,0:T(8,128)(2,1)S(1)} %get-tuple-element.22), channel_id=1, source_target_pairs={{0,1},{1,0},{2,3},{3,2},{4,5},{5,4},{6,7},{7,6},{8,9},{9,8},{10,11... | collective-permute-start | bytes 24584 | tf_op jit(solution)/shard_map/ppermute | solution.py:21
  7.0 5.5 %collective-permute-start.3 = (bf16[16,256]{1,0:T(8,128)(2,1)S(1)}, bf16[16,256]{1,0:T(8,128)(2,1)S(1)}, u32[]{:S(2)}, u32[]{:S(2)}) collective-permute-start(bf16[16,256]{1,0:T(8,128)(2,1)S(1)} %get-tuple-element.23), channel_id=1, source_target_pairs={{0,2},{1,3},{2,0},{3,1},{4,6},{5,7},{6,4},{7,5},{8,10},{9,11},{10,... | collective-permute-start | bytes 24584 | tf_op jit(solution)/shard_map/ppermute | solution.py:21
  8.6 4.5 %collective-permute-start.4 = (bf16[16,256]{1,0:T(8,128)(2,1)S(1)}, bf16[16,256]{1,0:T(8,128)(2,1)S(1)}, u32[]{:S(2)}, u32[]{:S(2)}) collective-permute-start(bf16[16,256]{1,0:T(8,128)(2,1)S(1)} %get-tuple-element.24), channel_id=1, source_target_pairs={{0,4},{1,5},{2,6},{3,7},{4,0},{5,1},{6,2},{7,3},{8,12},{9,13},{10,... | collective-permute-start | bytes 24584 | tf_op jit(solution)/shard_map/ppermute | solution.py:21
  13.2 0.7 %copy-start.15 = (f32[256]{0:T(256)S(1)}, f32[256]{0:T(256)}, u32[]{:S(2)}) copy-start(f32[256]{0:T(256)} %param.33) | copy-start | bytes 3076
  13.2 0.7 %copy-start.13 = (s32[1,5,64]{2,0,1:T(1,128)S(1)}, s32[1,5,64]{2,0,1:T(1,128)}, u32[]{:S(2)}) copy-start(s32[1,5,64]{2,0,1:T(1,128)} %param.24) | copy-start | bytes 3844
  13.2 0.7 %copy-start.14 = (f32[256]{0:T(256)S(1)}, f32[256]{0:T(256)}, u32[]{:S(2)}) copy-start(f32[256]{0:T(256)} %param.30) | copy-start | bytes 3076
  13.2 0.7 %copy-start.4 = (s32[1,5,64]{2,0,1:T(1,128)S(1)}, s32[1,5,64]{2,0,1:T(1,128)}, u32[]{:S(2)}) copy-start(s32[1,5,64]{2,0,1:T(1,128)} %param.25) | copy-start | bytes 3844
  13.2 0.7 %copy-start.5 = (s32[1,384]{1,0:T(1,128)S(1)}, s32[1,384]{1,0:T(1,128)}, u32[]{:S(2)}) copy-start(s32[1,384]{1,0:T(1,128)} %sender.3) | copy-start | bytes 4612
  13.2 0.7 %copy-start.6 = (s32[1,384]{1,0:T(1,128)S(1)}, s32[1,384]{1,0:T(1,128)}, u32[]{:S(2)}) copy-start(s32[1,384]{1,0:T(1,128)} %receiver.3) | copy-start | bytes 4612
  13.9 1.0 %copy-start = (bf16[768,256]{1,0:T(8,128)(2,1)S(1)}, bf16[768,256]{1,0:T(8,128)(2,1)}, u32[]{:S(2)}) copy-start(bf16[768,256]{1,0:T(8,128)(2,1)} %edge_first.3) | copy-start | bytes 1179652
  14.9 0.9 %copy-start.7 = (bf16[512,256]{1,0:T(8,128)(2,1)S(1)}, bf16[512,256]{1,0:T(8,128)(2,1)}, u32[]{:S(2)}) copy-start(bf16[512,256]{1,0:T(8,128)(2,1)} %node_first.1) | copy-start | bytes 786436
  15.9 0.9 %copy-start.8 = (bf16[1,384,256]{2,1,0:T(8,128)(2,1)S(1)}, bf16[1,384,256]{2,1,0:T(8,128)(2,1)}, u32[]{:S(2)}) copy-start(bf16[1,384,256]{2,1,0:T(8,128)(2,1)} %param.18) | copy-start | bytes 589828
  16.8 0.9 %copy-start.9 = (bf16[1,5,64,256]{3,2,1,0:T(8,128)(2,1)S(1)}, bf16[1,5,64,256]{3,2,1,0:T(8,128)(2,1)}, u32[]{:S(2)}) copy-start(bf16[1,5,64,256]{3,2,1,0:T(8,128)(2,1)} %param.19) | copy-start | bytes 491524
  17.7 0.9 %copy-start.10 = (bf16[256,256]{1,0:T(8,128)(2,1)S(1)}, bf16[256,256]{1,0:T(8,128)(2,1)}, u32[]{:S(2)}) copy-start(bf16[256,256]{1,0:T(8,128)(2,1)} %edge_second.1) | copy-start | bytes 393220
  18.6 0.9 %copy-start.11 = (bf16[256,256]{1,0:T(8,128)(2,1)S(1)}, bf16[256,256]{1,0:T(8,128)(2,1)}, u32[]{:S(2)}) copy-start(bf16[256,256]{1,0:T(8,128)(2,1)} %node_second.1) | copy-start | bytes 393220
  19.5 8.8 %copy-start.1 = (bf16[768,256]{1,0:T(8,128)(2,1)S(1)}, bf16[768,256]{1,0:T(8,128)(2,1)}, u32[]{:S(2)}) copy-start(bf16[768,256]{1,0:T(8,128)(2,1)} %edge_first.3) | copy-start | bytes 1179652
  22.5 4.1 %collective-permute-start.5 = (bf16[16,256]{1,0:T(8,128)(2,1)S(1)}, bf16[16,256]{1,0:T(8,128)(2,1)S(1)}, u32[]{:S(2)}, u32[]{:S(2)}) collective-permute-start(bf16[16,256]{1,0:T(8,128)(2,1)S(1)} %get-tuple-element.28), channel_id=1, source_target_pairs={{0,8},{8,0},{16,24},{24,16},{1,9},{9,1},{17,25},{25,17},{2,10},{10... | collective-permute-start | bytes 24584 | tf_op jit(solution)/shard_map/ppermute | solution.py:21
  22.5 4.1 %collective-permute-start.6 = (bf16[16,256]{1,0:T(8,128)(2,1)S(1)}, bf16[16,256]{1,0:T(8,128)(2,1)S(1)}, u32[]{:S(2)}, u32[]{:S(2)}) collective-permute-start(bf16[16,256]{1,0:T(8,128)(2,1)S(1)} %get-tuple-element.29), channel_id=1, source_target_pairs={{0,16},{8,24},{16,0},{24,8},{1,17},{9,25},{17,1},{25,9},{2,18},{10... | collective-permute-start | bytes 24584 | tf_op jit(solution)/shard_map/ppermute | solution.py:21
  23.0 3.7 %collective-permute-start.7 = (bf16[16,256]{1,0:T(8,128)(2,1)S(1)}, bf16[16,256]{1,0:T(8,128)(2,1)S(1)}, u32[]{:S(2)}, u32[]{:S(2)}) collective-permute-start(bf16[16,256]{1,0:T(8,128)(2,1)S(1)} %get-tuple-element.30), channel_id=1, source_target_pairs={{0,1},{1,0},{2,3},{3,2},{4,5},{5,4},{6,7},{7,6},{8,9},{9,8},{10,11... | collective-permute-start | bytes 24584 | tf_op jit(solution)/shard_map/ppermute | solution.py:21
  23.5 3.7 %collective-permute-start.8 = (bf16[16,256]{1,0:T(8,128)(2,1)S(1)}, bf16[16,256]{1,0:T(8,128)(2,1)S(1)}, u32[]{:S(2)}, u32[]{:S(2)}) collective-permute-start(bf16[16,256]{1,0:T(8,128)(2,1)S(1)} %get-tuple-element.31), channel_id=1, source_target_pairs={{0,2},{1,3},{2,0},{3,1},{4,6},{5,7},{6,4},{7,5},{8,10},{9,11},{10,... | collective-permute-start | bytes 24584 | tf_op jit(solution)/shard_map/ppermute | solution.py:21
  23.7 4.6 %collective-permute-start.9 = (bf16[16,256]{1,0:T(8,128)(2,1)S(1)}, bf16[16,256]{1,0:T(8,128)(2,1)S(1)}, u32[]{:S(2)}, u32[]{:S(2)}) collective-permute-start(bf16[16,256]{1,0:T(8,128)(2,1)S(1)} %get-tuple-element.32), channel_id=1, source_target_pairs={{0,4},{1,5},{2,6},{3,7},{4,0},{5,1},{6,2},{7,3},{8,12},{9,13},{10,... | collective-permute-start | bytes 24584 | tf_op jit(solution)/shard_map/ppermute | solution.py:21

commit v2 on v1

v2 whole, which is shorter than its diff:
```python
import functools

import jax
import jax.numpy as jnp
from jax import lax
from jax.experimental import pallas as pl
from jax.experimental.pallas import tpu as pltpu
from jax.sharding import PartitionSpec as P

ROUNDS = 5
GRP_ROUNDS = 2

epsilon = 1e-05

bf16 = jnp.bfloat16
f32 = jnp.float32


def partner(shard, round_index):
    axis, apart = ("grp", round_index) if round_index < GRP_ROUNDS else ("dev", round_index - GRP_ROUNDS)
    return lax.ppermute(shard, axis, [(i, i ^ 1 << apart) for i in range(lax.axis_size(axis))])


def exchange(rows):
    got = lax.optimization_barrier([partner(rows[r], r) for r in reversed(range(ROUNDS))])
    return got[::-1]


def mm(a, b):
    return jnp.dot(a, b, preferred_element_type=f32)


def mm_t(a, b):
    return lax.dot_general(a, b, (((1,), (1,)), ((), ())), preferred_element_type=f32)


def t_mm(a, b):
    return lax.dot_general(a, b, (((0,), (0,)), ((), ())), preferred_element_type=f32)


def hot(row, count):
    shape = (count, row.shape[1])
    return (lax.broadcasted_iota(jnp.int32, shape, 0) == jnp.broadcast_to(row, shape)).astype(f32)


def lane_mean(values):
    return jnp.mean(values, axis=-1, keepdims=True)


def norm_parts(values):
    centred = values - lane_mean(values)
    inverse = lax.rsqrt(lane_mean(centred * centred) + epsilon)
    return centred * inverse, inverse


def norm_backward(scaled, normed, inverse):
    return inverse * (scaled - lane_mean(scaled) - normed * lane_mean(scaled * normed))


def silu_parts(values):
    sigmoid = jax.nn.sigmoid(values)
    act = values * sigmoid
    return act, sigmoid + act * (1.0 - sigmoid)


def load(held, loaded, done):
    copies = [pltpu.make_async_copy(h, v, done.at[i]) for i, (h, v) in enumerate(zip(held, loaded))]
    for copy in copies:
        copy.start()
    return copies


def send_kernel(count, *rest):
    held, loaded, out, done = rest[:count], rest[count : 2 * count], rest[2 * count : -1], rest[-1]
    copies = load(held, loaded, done)
    for copy in copies[:2]:
        copy.wait()
    nodes, boundary = loaded[:2]
    table = jnp.concatenate([hot(boundary[r], nodes.shape[0]) for r in range(ROUNDS)], 1)
    rows = t_mm(table.astype(bf16), nodes[...]).astype(bf16)
    send = boundary.shape[2]
    for r in range(ROUNDS):
        out[r][...] = rows[r * send : (r + 1) * send]
    for copy in copies[2:]:
        copy.wait()


def inner_kernel(*rest):
    counts, nodes, edges, sender, receiver, edge_first, edge_second = rest[:7]
    by_receiver, gather_out, normed_out, inverse_out, slope_out, received = rest[7:]
    n, width = nodes.shape
    e = edges.shape[0]
    used = lax.broadcasted_iota(jnp.int32, (1, e), 1) < counts[1:, :e]
    hot_receive = hot(jnp.where(used, receiver[...], -1), n)
    gather = jnp.concatenate([hot_receive, hot(sender[...], n)], 0).T.astype(bf16)
    first = mm(nodes[...], edge_first[:width]).astype(bf16)
    second = mm(nodes[...], edge_first[width : 2 * width]).astype(bf16)
    pre = mm(gather, jnp.concatenate([first, second], 0)) + mm(edges[...], edge_first[2 * width :])
    act, slope = silu_parts(pre)
    normed, inverse = norm_parts(mm(act.astype(bf16), edge_second[...]))
    by_receiver[...] = first
    gather_out[...] = gather[:, :n]
    normed_out[...] = normed
    inverse_out[...] = inverse
    slope_out[...] = slope
    received[...] = mm(hot_receive.astype(bf16), normed.astype(bf16))


def main_kernel(
    counts, nodes, cuts, cotangent, slot, cut_receiver, edge_first, edge_second, edge_gain, node_first, node_second,
    node_gain, by_receiver, received_inner, *rest,
):
    arrived = rest[:ROUNDS]
    updated, base, gained, grad_cut = rest[ROUNDS : ROUNDS + 4]
    back = rest[ROUNDS + 4 :]
    n, width = nodes.shape
    send = arrived[0].shape[0]
    x = nodes[...]
    hot_receive = jnp.concatenate([hot(cut_receiver[r], n) for r in range(ROUNDS)], 1)
    hot_slot = hot(jnp.concatenate([slot[r] + r * send for r in range(ROUNDS)], 1), 128)
    gather = jnp.concatenate([hot_receive, hot_slot], 0).T.astype(bf16)
    far = jnp.concatenate([a[...] for a in arrived] + [jnp.zeros((128 - ROUNDS * send, width), bf16)], 0)
    by_sender = mm(far, edge_first[width : 2 * width]).astype(bf16)
    pre = mm(gather, jnp.concatenate([by_receiver[...], by_sender], 0)) + mm(cuts[...], edge_first[2 * width :])
    act, slope = silu_parts(pre)
    normed, inverse = norm_parts(mm(act.astype(bf16), edge_second[...]))
    received = (received_inner[...] + mm(hot_receive.astype(bf16), normed.astype(bf16))) * edge_gain[...]

    valid = lax.broadcasted_iota(jnp.int32, (n, width), 0) < counts[:1, :width]
    pre_node = mm(jnp.concatenate([x, received.astype(bf16)], 1), node_first[...])
    act_node, slope_node = silu_parts(pre_node)
    normed_node, inverse_node = norm_parts(mm(act_node.astype(bf16), node_second[...]))
    updated[...] = jnp.where(valid, x.astype(f32) + normed_node * node_gain[...], 0.0).astype(bf16)
    masked = jnp.where(valid, cotangent[...].astype(f32), 0.0)
    grad_out_node = norm_backward(masked * node_gain[...], normed_node, inverse_node).astype(bf16)
    grad_pre_node = (mm_t(grad_out_node, node_second[...]) * slope_node).astype(bf16)
    at_receiver = mm_t(grad_pre_node, node_first[width:]) * edge_gain[...]
    high = at_receiver.astype(bf16)
    low = (at_receiver - high.astype(f32)).astype(bf16)
    parts = jnp.concatenate([high, low], 0)
    twice = jnp.concatenate([gather[:, :n], gather[:, :n]], 1)
    grad_out = norm_backward(mm(twice, parts), normed, inverse).astype(bf16)
    grad = (mm_t(grad_out, edge_second[...]) * slope).astype(bf16)
    sums = mm(hot_slot.astype(bf16), grad).astype(bf16)
    for r in range(ROUNDS):
        back[r][...] = sums[r * send : (r + 1) * send]
    grad_cut[...] = grad
    gained[...] = parts
    base[...] = masked + mm_t(grad_pre_node, node_first[:width])


def outer_kernel(
    gained, gather, normed, inverse, slope, edge_first, edge_second, sender, receiver, cut_receiver, grad_cut, base,
    updated_in, updated, edge_gradient, cut_gradient, total,
):
    n, width = base.shape
    updated[...] = updated_in[...]
    cut = grad_cut[...]
    cut_gradient[...] = mm_t(cut, edge_first[2 * width :]).astype(bf16)
    twice = jnp.concatenate([gather[...], gather[...]], 1)
    grad_out = norm_backward(mm(twice, gained[...]), normed[...], inverse[...]).astype(bf16)
    grad = (mm_t(grad_out, edge_second[...]) * slope[...]).astype(bf16)
    edge_gradient[...] = mm_t(grad, edge_first[2 * width :]).astype(bf16)
    hot_cut = jnp.concatenate([hot(cut_receiver[r], n) for r in range(ROUNDS)], 1).astype(bf16)
    at_receiver = mm(hot(receiver[...], n).astype(bf16), grad) + mm(hot_cut, cut)
    at_sender = mm(hot(sender[...], n).astype(bf16), grad)
    total[...] = (
        base[...]
        + mm_t(at_receiver.astype(bf16), edge_first[:width])
        + mm_t(at_sender.astype(bf16), edge_first[width : 2 * width])
    )


def last_kernel(total, boundary, edge_first, *rest):
    arrived, node_gradient = rest[:ROUNDS], rest[ROUNDS]
    n, width = total.shape
    table = jnp.concatenate([hot(boundary[r], n) for r in range(ROUNDS)], 1).astype(bf16)
    at_sender = mm(table, jnp.concatenate([a[...] for a in arrived], 0)).astype(bf16)
    node_gradient[...] = (total[...] + mm_t(at_sender, edge_first[width : 2 * width])).astype(bf16)


VMEM = pl.BlockSpec(memory_space=pltpu.VMEM)
HBM = pl.BlockSpec(memory_space=pltpu.HBM)


def call(kernel, out_shape, args, flops, held=(), scratch=()):
    size = sum(a.size * a.dtype.itemsize for a in args + tuple(held))
    return pl.pallas_call(
        kernel,
        out_shape=out_shape,
        in_specs=[VMEM] * len(args) + [HBM] * len(held),
        out_specs=[VMEM] * len(out_shape),
        scratch_shapes=scratch,
        compiler_params=pltpu.CompilerParams(vmem_limit_bytes=32 * 1024 * 1024),
        cost_estimate=pl.CostEstimate(flops=flops, bytes_accessed=size, transcendentals=0),
    )(*args, *(pltpu.with_memory_space_constraint(a, pltpu.HBM) for a in held))


def shards(
    node_latent, edge_latent, cut_latent, node_cotangent, edge_sender, edge_receiver, boundary_rows,
    cut_slot, cut_receiver, node_count, edge_count, edge_first, edge_second, edge_gain, node_first,
    node_second, node_gain,
):
    nodes = node_latent[0]
    edges = edge_latent[0]
    cuts = cut_latent[0].reshape(-1, cut_latent.shape[-1])
    n, width = nodes.shape
    e, c = edges.shape[0], cuts.shape[0]
    boundary = boundary_rows.transpose(1, 0, 2)
    slot = cut_slot.transpose(1, 0, 2)
    cut_targets = cut_receiver.transpose(1, 0, 2)
    send = boundary.shape[2]
    shape = jax.ShapeDtypeStruct
    kept = pltpu.VMEM

    def copies(arrays):
        return [kept(a.shape, a.dtype) for a in arrays]

    held = (
        nodes, boundary, edge_receiver, edge_sender, edge_first, edges, edge_second, slot,
        cut_targets, edge_gain[None], node_gain[None],
    )
    outs = call(
        functools.partial(send_kernel, len(held)),
        copies(held) + [kept((send, width), bf16)] * ROUNDS,
        (),
        2 * 128 * n * width,
        held,
        [pltpu.SemaphoreType.DMA((len(held),))],
    )
    (
        nodes, boundary, edge_receiver, edge_sender, edge_first, edges, edge_second, slot,
        cut_targets, edge_gain, node_gain,
    ) = outs[: len(held)]
    sent = outs[len(held) :]
    counts = lax.broadcast_in_dim(jnp.concatenate([node_count, edge_count]), (2, max(e, width)), (0,))
    arrived = exchange(sent)
    outs = call(
        inner_kernel,
        [
            kept((n, width), bf16), kept((e, n), bf16), kept((e, width), f32), kept((e, 1), f32),
            kept((e, width), f32), kept((n, width), f32),
        ],
        (counts, nodes, edges, edge_sender, edge_receiver, edge_first, edge_second),
        2 * e * width * width * 4,
    )
    by_receiver, gather, normed, inverse, slope, received = outs
    outs = call(
        main_kernel,
        [kept((n, width), bf16), kept((n, width), f32), kept((2 * n, width), bf16), kept((c, width), bf16)]
        + [kept((send, width), bf16)] * ROUNDS,
        (
            counts, nodes, cuts, node_cotangent[0], slot, cut_targets, edge_first, edge_second, edge_gain, node_first,
            node_second, node_gain, by_receiver, received, *arrived,
        ),
        2 * c * width * width * 6,
    )
    updated, base, gained, grad_cut = outs[:4]
    returned = exchange(outs[4:])
    updated, edge_gradient, cut_gradient, total = call(
        outer_kernel,
        [shape((n, width), bf16), shape((e, width), bf16), shape((c, width), bf16), kept((n, width), f32)],
        (
            gained, gather, normed, inverse, slope, edge_first, edge_second, edge_sender, edge_receiver,
            cut_targets, grad_cut, base, updated,
        ),
        2 * (e + c) * width * width * 3,
    )
    (node_gradient,) = call(
        last_kernel,
        [shape((n, width), bf16)],
        (total, boundary, edge_first, *returned),
        2 * 2 * n * width * width,
    )
    return (
        updated[None],
        node_gradient[None],
        edge_gradient[None],
        cut_gradient.reshape(cut_latent.shape),
    )


def solution(mesh):
    part = ("grp", "dev")
    placed = tuple(P(part, *[None] * (d - 1)) for d in (3, 3, 4, 3, 2, 2, 3, 3, 3, 1, 1)) + (P(),) * 6
    return jax.shard_map(
        shards,
        mesh=mesh,
        in_specs=placed,
        out_specs=tuple(P(part, *[None] * (d - 1)) for d in (3, 3, 3, 4)),
        check_vma=False,
    )
```

time: 29.8 us -> 21.5 us (0.72)
  local copies, waits for them, and re-layouts: 7.84 us -> 0.2 us
  Pallas kernels: 4.32 us -> 6.96 us
  starting transfers between devices: 12.8 us -> 11.2 us
  waiting for transfers between devices: 2.42 us -> 0.88 us
    unnamed x32 -> x8, local copies, waits for them, and re-layouts: 7.84 us -> 0.13 us
    pallas_call x3 -> x5, Pallas kernels: 4.32 us -> 6.96 us  [call(): pl.pallas_call(kernel, out_shape=out_shape, in_specs=[VMEM] * len(args) +...]
    ppermute x10, starting transfers between devices: 12.8 us -> 11.2 us  [partner(): lax.ppermute(shard, axis, [(i, i ^ 1 << apart) for i in range(lax.axis_si...]
    ppermute x10, waiting for transfers between devices: 2.42 us -> 0.88 us  [partner(): lax.ppermute(shard, axis, [(i, i ^ 1 << apart) for i in range(lax.axis_si...]
  transfers between devices with their start and end apart: 10 -> 10, of which waited for: 4 -> 2; matrix products, arithmetic and copies ran while one was open for 0% -> 1% of each run, Pallas kernels for 0% -> 12%
where the time goes in v2:
time: 21.5 us; the launch traced here: 21.4 us
  starting transfers between devices  11.2 us (52%)
  Pallas kernels  6.96 us (32%)
  between operations  2.01 us (9%)
  waiting for transfers between devices  0.88 us (4%)
    ppermute x10, starting transfers between devices, partner(): lax.ppermute(shard, axis, [(i, i ^ 1 << apart) for i in range(lax.axis_si...  11.2 us
    pallas_call x5, Pallas kernels, call(): pl.pallas_call(kernel, out_shape=out_shape, in_specs=[VMEM] * len(args) +...  6.96 us
    ppermute x10, waiting for transfers between devices, partner(): lax.ppermute(shard, axis, [(i, i ^ 1 << apart) for i in range(lax.axis_si...  0.88 us
  transfers between devices with their start and end apart: 10, of which 2 were waited for; matrix products, arithmetic and copies ran while one was open for 1% of the time, Pallas kernels for 12%

profile of v2, /device:TPU:0, one launch (start us, length us, event | category | flops | bytes accessed | tf_op | source)
XLA Modules:
  0.0 21.4 jit_solution(1962767882475153641)
XLA Ops:
  0.6 1.3 %shard_map.192 = (bf16[128,256]{1,0:T(8,128)(2,1)S(1)}, s32[5,1,16]{2,1,0:T(1,128)S(1)}, s32[1,384]{1,0:T(1,128)S(1)}, s32[1,384]{1,0:T(1,128)S(1)}, bf16[768,25...) custom-call(bf16[128,256]{1,0:T(8,128)(2,1)} %bitcast.17, ...), custom_call_target="tpu_custom_call" | custom-call | flops 8388608 | bytes 794432 | tf_op jit(solution)/shard_map/pallas_call | solution.py:188
  2.0 4.1 %collective-permute-start = (bf16[16,256]{1,0:T(8,128)(2,1)S(1)}, bf16[16,256]{1,0:T(8,128)(2,1)S(1)}, u32[]{:S(2)}, u32[]{:S(2)}) collective-permute-start(bf16[16,256]{1,0:T(8,128)(2,1)S(1)} %get-tuple-element.61), channel_id=1, source_target_pairs={{0,4},{1,5},{2,6},{3,7},{4,0},{5,1},{6,2},{7,3},{8,12},{9,13},{10,... | collective-permute-start | bytes 24584 | tf_op jit(solution)/shard_map/ppermute | solution.py:21
  6.1 1.6 %collective-permute-start.1 = (bf16[16,256]{1,0:T(8,128)(2,1)S(1)}, bf16[16,256]{1,0:T(8,128)(2,1)S(1)}, u32[]{:S(2)}, u32[]{:S(2)}) collective-permute-start(bf16[16,256]{1,0:T(8,128)(2,1)S(1)} %get-tuple-element.62), channel_id=1, source_target_pairs={{0,2},{1,3},{2,0},{3,1},{4,6},{5,7},{6,4},{7,5},{8,10},{9,11},{10,... | collective-permute-start | bytes 24584 | tf_op jit(solution)/shard_map/ppermute | solution.py:21
  7.6 1.5 %collective-permute-start.2 = (bf16[16,256]{1,0:T(8,128)(2,1)S(1)}, bf16[16,256]{1,0:T(8,128)(2,1)S(1)}, u32[]{:S(2)}, u32[]{:S(2)}) collective-permute-start(bf16[16,256]{1,0:T(8,128)(2,1)S(1)} %get-tuple-element.63), channel_id=1, source_target_pairs={{0,1},{1,0},{2,3},{3,2},{4,5},{5,4},{6,7},{7,6},{8,9},{9,8},{10,11... | collective-permute-start | bytes 24584 | tf_op jit(solution)/shard_map/ppermute | solution.py:21
  9.2 1.5 %collective-permute-start.3 = (bf16[16,256]{1,0:T(8,128)(2,1)S(1)}, bf16[16,256]{1,0:T(8,128)(2,1)S(1)}, u32[]{:S(2)}, u32[]{:S(2)}) collective-permute-start(bf16[16,256]{1,0:T(8,128)(2,1)S(1)} %get-tuple-element.64), channel_id=1, source_target_pairs={{0,16},{8,24},{16,0},{24,8},{1,17},{9,25},{17,1},{25,9},{2,18},{10... | collective-permute-start | bytes 24584 | tf_op jit(solution)/shard_map/ppermute | solution.py:21
  10.7 0.0 collective-permute-start.4
  12.0 0.1 pad_add_fusion
  12.0 0.1 broadcast_in_dim.18.rest_0_.counts
  12.1 0.0 copy-start
  12.1 0.9 %shard_map.193 = (bf16[128,256]{1,0:T(8,128)(2,1)S(1)}, bf16[384,128]{1,0:T(8,128)(2,1)S(1)}, f32[384,256]{1,0:T(8,128)S(1)}, f32[384,1]{1,0:T(8,128)S(1)}, f32[...) custom-call(s32[2,384]{1,0:T(2,128)S(1)} %broadcast_in_dim.18.rest_0_.counts, ...), custom_call_target="tpu_custom_call" | custom-call | flops 201326592 | bytes 792576 | tf_op jit(solution)/shard_map/pallas_call | solution.py:188
  13.0 0.0 collective-permute-done.rest_4_
  13.0 0.0 collective-permute-done.1.rest_3_
  13.0 0.0 collective-permute-done.2.rest_2_
  13.0 0.0 collective-permute-done.3.rest_1_
  13.0 0.0 collective-permute-done.4.rest_0_
  13.0 0.0 copy-done
  13.1 0.0 copy-done.1
  13.1 0.1 copy-done.2
  13.2 0.0 copy-done.3
  13.2 2.2 %shard_map.194 = (bf16[128,256]{1,0:T(8,128)(2,1)S(1)}, f32[128,256]{1,0:T(8,128)S(1)}, bf16[256,256]{1,0:T(8,128)(2,1)S(1)}, bf16[320,256]{1,0:T(8,128)(2,1)S(1...) custom-call(s32[2,384]{1,0:T(2,128)S(1)} %broadcast_in_dim.18.rest_0, ...), custom_call_target="tpu_custom_call" | custom-call | flops 251658240 | bytes 1457664 | tf_op jit(solution)/shard_map/pallas_call | solution.py:188
  15.4 0.4 %collective-permute-start.5 = (bf16[16,256]{1,0:T(8,128)(2,1)S(1)}, bf16[16,256]{1,0:T(8,128)(2,1)S(1)}, u32[]{:S(2)}, u32[]{:S(2)}) collective-permute-start(bf16[16,256]{1,0:T(8,128)(2,1)S(1)} %get-tuple-element.82), channel_id=1, source_target_pairs={{0,4},{1,5},{2,6},{3,7},{4,0},{5,1},{6,2},{7,3},{8,12},{9,13},{10,... | collective-permute-start | bytes 24584 | tf_op jit(solution)/shard_map/ppermute | solution.py:21
  15.8 0.4 %collective-permute-start.6 = (bf16[16,256]{1,0:T(8,128)(2,1)S(1)}, bf16[16,256]{1,0:T(8,128)(2,1)S(1)}, u32[]{:S(2)}, u32[]{:S(2)}) collective-permute-start(bf16[16,256]{1,0:T(8,128)(2,1)S(1)} %get-tuple-element.83), channel_id=1, source_target_pairs={{0,2},{1,3},{2,0},{3,1},{4,6},{5,7},{6,4},{7,5},{8,10},{9,11},{10,... | collective-permute-start | bytes 24584 | tf_op jit(solution)/shard_map/ppermute | solution.py:21
  16.2 0.5 %collective-permute-start.7 = (bf16[16,256]{1,0:T(8,128)(2,1)S(1)}, bf16[16,256]{1,0:T(8,128)(2,1)S(1)}, u32[]{:S(2)}, u32[]{:S(2)}) collective-permute-start(bf16[16,256]{1,0:T(8,128)(2,1)S(1)} %get-tuple-element.84), channel_id=1, source_target_pairs={{0,1},{1,0},{2,3},{3,2},{4,5},{5,4},{6,7},{7,6},{8,9},{9,8},{10,11... | collective-permute-start | bytes 24584 | tf_op jit(solution)/shard_map/ppermute | solution.py:21
  16.7 1.2 %collective-permute-start.8 = (bf16[16,256]{1,0:T(8,128)(2,1)S(1)}, bf16[16,256]{1,0:T(8,128)(2,1)S(1)}, u32[]{:S(2)}, u32[]{:S(2)}) collective-permute-start(bf16[16,256]{1,0:T(8,128)(2,1)S(1)} %get-tuple-element.85), channel_id=1, source_target_pairs={{0,16},{8,24},{16,0},{24,8},{1,17},{9,25},{17,1},{25,9},{2,18},{10... | collective-permute-start | bytes 24584 | tf_op jit(solution)/shard_map/ppermute | solution.py:21
  17.9 0.0 collective-permute-start.9
  17.9 1.6 %shard_map.195 = (bf16[128,256]{1,0:T(8,128)(2,1)}, bf16[384,256]{1,0:T(8,128)(2,1)}, bf16[320,256]{1,0:T(8,128)(2,1)}, f32[128,256]{1,0:T(8,128)S(1)}) custom-call(bf16[256,256]{1,0:T(8,128)(2,1)S(1)} %get-tuple-element.71.gained, bf16[384,128]{1,0:T(8,128)(2,1)S(1)} %get-tuple-element.72.gather, f32[384,256]{1,0:T(8,128)S(1)} %get-tuple-element.73.normed, ...), custom_call_target="tpu_custom_call" | custom-call | flops 276824064 | bytes 1906432 | tf_op jit(solution)/shard_map/pallas_call | solution.py:188
  19.5 0.5 %collective-permute-done.5.rest_4_ = bf16[16,256]{1,0:T(8,128)(2,1)S(1)} collective-permute-done((bf16[16,256]{1,0:T(8,128)(2,1)S(1)}, bf16[16,256]{1,0:T(8,128)(2,1)S(1)}, u32[]{:S(2)}, u32[]{:S(2)}) %collective-permute-start.5) | collective-permute-done | bytes 8224 | tf_op jit(solution)/shard_map/ppermute | solution.py:21
  20.0 0.0 collective-permute-done.6.rest_3_
  20.0 0.0 collective-permute-done.7.rest_2_
  20.0 0.4 %collective-permute-done.8.rest_1_ = bf16[16,256]{1,0:T(8,128)(2,1)S(1)} collective-permute-done((bf16[16,256]{1,0:T(8,128)(2,1)S(1)}, bf16[16,256]{1,0:T(8,128)(2,1)S(1)}, u32[]{:S(2)}, u32[]{:S(2)}) %collective-permute-start.8) | collective-permute-done | bytes 8224 | tf_op jit(solution)/shard_map/ppermute | solution.py:21
  20.4 0.0 collective-permute-done.9.rest_0_
  20.4 1.0 %shard_map.196 = bf16[128,256]{1,0:T(8,128)(2,1)} custom-call(f32[128,256]{1,0:T(8,128)S(1)} %get-tuple-element.80.total, s32[5,1,16]{2,1,0:T(1,128)S(1)} %get-tuple-element.81.boundary, bf16[768,256]{1,0:T(8,128)(2,1)S(1)} %get-tuple-element.52.rest_5_.edge_first, bf16[16,256]{1,0:T(8,128)(2,1)S(1)} %collective-permute-done.9.rest_0_, ...), custom_call_target="tpu_custom_call" | custom-call | flops 33554432 | bytes 565568 | tf_op jit(solution)/shard_map/pallas_call | solution.py:188
  (3 shorter events, 0.0 us)
Async XLA Ops:
  2.0 11.0 %collective-permute-start = (bf16[16,256]{1,0:T(8,128)(2,1)S(1)}, bf16[16,256]{1,0:T(8,128)(2,1)S(1)}, u32[]{:S(2)}, u32[]{:S(2)}) collective-permute-start(bf16[16,256]{1,0:T(8,128)(2,1)S(1)} %get-tuple-element.61), channel_id=1, source_target_pairs={{0,4},{1,5},{2,6},{3,7},{4,0},{5,1},{6,2},{7,3},{8,12},{9,13},{10,... | collective-permute-start | bytes 24584 | tf_op jit(solution)/shard_map/ppermute | solution.py:21
  6.1 6.9 %collective-permute-start.1 = (bf16[16,256]{1,0:T(8,128)(2,1)S(1)}, bf16[16,256]{1,0:T(8,128)(2,1)S(1)}, u32[]{:S(2)}, u32[]{:S(2)}) collective-permute-start(bf16[16,256]{1,0:T(8,128)(2,1)S(1)} %get-tuple-element.62), channel_id=1, source_target_pairs={{0,2},{1,3},{2,0},{3,1},{4,6},{5,7},{6,4},{7,5},{8,10},{9,11},{10,... | collective-permute-start | bytes 24584 | tf_op jit(solution)/shard_map/ppermute | solution.py:21
  7.6 5.4 %collective-permute-start.2 = (bf16[16,256]{1,0:T(8,128)(2,1)S(1)}, bf16[16,256]{1,0:T(8,128)(2,1)S(1)}, u32[]{:S(2)}, u32[]{:S(2)}) collective-permute-start(bf16[16,256]{1,0:T(8,128)(2,1)S(1)} %get-tuple-element.63), channel_id=1, source_target_pairs={{0,1},{1,0},{2,3},{3,2},{4,5},{5,4},{6,7},{7,6},{8,9},{9,8},{10,11... | collective-permute-start | bytes 24584 | tf_op jit(solution)/shard_map/ppermute | solution.py:21
  9.2 3.9 %collective-permute-start.3 = (bf16[16,256]{1,0:T(8,128)(2,1)S(1)}, bf16[16,256]{1,0:T(8,128)(2,1)S(1)}, u32[]{:S(2)}, u32[]{:S(2)}) collective-permute-start(bf16[16,256]{1,0:T(8,128)(2,1)S(1)} %get-tuple-element.64), channel_id=1, source_target_pairs={{0,16},{8,24},{16,0},{24,8},{1,17},{9,25},{17,1},{25,9},{2,18},{10... | collective-permute-start | bytes 24584 | tf_op jit(solution)/shard_map/ppermute | solution.py:21
  10.7 2.4 %collective-permute-start.4 = (bf16[16,256]{1,0:T(8,128)(2,1)S(1)}, bf16[16,256]{1,0:T(8,128)(2,1)S(1)}, u32[]{:S(2)}, u32[]{:S(2)}) collective-permute-start(bf16[16,256]{1,0:T(8,128)(2,1)S(1)} %get-tuple-element.65), channel_id=1, source_target_pairs={{0,8},{8,0},{16,24},{24,16},{1,9},{9,1},{17,25},{25,17},{2,10},{10... | collective-permute-start | bytes 24584 | tf_op jit(solution)/shard_map/ppermute | solution.py:21
  12.1 1.0 %copy-start = (bf16[512,256]{1,0:T(8,128)(2,1)S(1)}, bf16[512,256]{1,0:T(8,128)(2,1)}, u32[]{:S(2)}) copy-start(bf16[512,256]{1,0:T(8,128)(2,1)} %node_first.1) | copy-start | bytes 786436
  12.1 1.0 %copy-start.1 = (bf16[1,5,64,256]{3,2,1,0:T(8,128)(2,1)S(1)}, bf16[1,5,64,256]{3,2,1,0:T(8,128)(2,1)}, u32[]{:S(2)}) copy-start(bf16[1,5,64,256]{3,2,1,0:T(8,128)(2,1)} %param.19) | copy-start | bytes 491524
  12.1 1.1 %copy-start.2 = (bf16[256,256]{1,0:T(8,128)(2,1)S(1)}, bf16[256,256]{1,0:T(8,128)(2,1)}, u32[]{:S(2)}) copy-start(bf16[256,256]{1,0:T(8,128)(2,1)} %node_second.1) | copy-start | bytes 393220
  12.1 1.1 %copy-start.3 = (bf16[1,128,256]{2,1,0:T(8,128)(2,1)S(1)}, bf16[1,128,256]{2,1,0:T(8,128)(2,1)}, u32[]{:S(2)}) copy-start(bf16[1,128,256]{2,1,0:T(8,128)(2,1)} %param.20) | copy-start | bytes 196612
  15.4 4.6 %collective-permute-start.5 = (bf16[16,256]{1,0:T(8,128)(2,1)S(1)}, bf16[16,256]{1,0:T(8,128)(2,1)S(1)}, u32[]{:S(2)}, u32[]{:S(2)}) collective-permute-start(bf16[16,256]{1,0:T(8,128)(2,1)S(1)} %get-tuple-element.82), channel_id=1, source_target_pairs={{0,4},{1,5},{2,6},{3,7},{4,0},{5,1},{6,2},{7,3},{8,12},{9,13},{10,... | collective-permute-start | bytes 24584 | tf_op jit(solution)/shard_map/ppermute | solution.py:21
  15.8 4.2 %collective-permute-start.6 = (bf16[16,256]{1,0:T(8,128)(2,1)S(1)}, bf16[16,256]{1,0:T(8,128)(2,1)S(1)}, u32[]{:S(2)}, u32[]{:S(2)}) collective-permute-start(bf16[16,256]{1,0:T(8,128)(2,1)S(1)} %get-tuple-element.83), channel_id=1, source_target_pairs={{0,2},{1,3},{2,0},{3,1},{4,6},{5,7},{6,4},{7,5},{8,10},{9,11},{10,... | collective-permute-start | bytes 24584 | tf_op jit(solution)/shard_map/ppermute | solution.py:21
  16.2 3.8 %collective-permute-start.7 = (bf16[16,256]{1,0:T(8,128)(2,1)S(1)}, bf16[16,256]{1,0:T(8,128)(2,1)S(1)}, u32[]{:S(2)}, u32[]{:S(2)}) collective-permute-start(bf16[16,256]{1,0:T(8,128)(2,1)S(1)} %get-tuple-element.84), channel_id=1, source_target_pairs={{0,1},{1,0},{2,3},{3,2},{4,5},{5,4},{6,7},{7,6},{8,9},{9,8},{10,11... | collective-permute-start | bytes 24584 | tf_op jit(solution)/shard_map/ppermute | solution.py:21
  16.7 3.7 %collective-permute-start.8 = (bf16[16,256]{1,0:T(8,128)(2,1)S(1)}, bf16[16,256]{1,0:T(8,128)(2,1)S(1)}, u32[]{:S(2)}, u32[]{:S(2)}) collective-permute-start(bf16[16,256]{1,0:T(8,128)(2,1)S(1)} %get-tuple-element.85), channel_id=1, source_target_pairs={{0,16},{8,24},{16,0},{24,8},{1,17},{9,25},{17,1},{25,9},{2,18},{10... | collective-permute-start | bytes 24584 | tf_op jit(solution)/shard_map/ppermute | solution.py:21
  17.9 2.5 %collective-permute-start.9 = (bf16[16,256]{1,0:T(8,128)(2,1)S(1)}, bf16[16,256]{1,0:T(8,128)(2,1)S(1)}, u32[]{:S(2)}, u32[]{:S(2)}) collective-permute-start(bf16[16,256]{1,0:T(8,128)(2,1)S(1)} %get-tuple-element.86), channel_id=1, source_target_pairs={{0,8},{8,0},{16,24},{24,16},{1,9},{9,1},{17,25},{25,17},{2,10},{10... | collective-permute-start | bytes 24584 | tf_op jit(solution)/shard_map/ppermute | solution.py:21

commit v3 on v2

--- a/solution.py
+++ b/solution.py
@@ -8,6 +8,7 @@
 from jax.sharding import PartitionSpec as P
 
 ROUNDS = 5
+LONG = 4 * 10**9
 GRP_ROUNDS = 2
 
 epsilon = 1e-05
@@ -73,11 +74,11 @@
 def send_kernel(count, *rest):
     held, loaded, out, done = rest[:count], rest[count : 2 * count], rest[2 * count : -1], rest[-1]
     copies = load(held, loaded, done)
-    for copy in copies[:2]:
-        copy.wait()
-    nodes, boundary = loaded[:2]
-    table = jnp.concatenate([hot(boundary[r], nodes.shape[0]) for r in range(ROUNDS)], 1)
-    rows = t_mm(table.astype(bf16), nodes[...]).astype(bf16)
+    boundary, nodes = loaded[:2]
+    copies[0].wait()
+    table = jnp.concatenate([hot(boundary[r], nodes.shape[0]) for r in range(ROUNDS)], 1).T.astype(bf16)
+    copies[1].wait()
+    rows = mm(table, nodes[...]).astype(bf16)
     send = boundary.shape[2]
     for r in range(ROUNDS):
         out[r][...] = rows[r * send : (r + 1) * send]
@@ -86,11 +87,11 @@
 
 
 def inner_kernel(*rest):
-    counts, nodes, edges, sender, receiver, edge_first, edge_second = rest[:7]
+    edge_count, nodes, edges, sender, receiver, edge_first, edge_second = rest[:7]
     by_receiver, gather_out, normed_out, inverse_out, slope_out, received = rest[7:]
     n, width = nodes.shape
     e = edges.shape[0]
-    used = lax.broadcasted_iota(jnp.int32, (1, e), 1) < counts[1:, :e]
+    used = lax.broadcasted_iota(jnp.int32, (1, e), 1) < edge_count[0]
     hot_receive = hot(jnp.where(used, receiver[...], -1), n)
     gather = jnp.concatenate([hot_receive, hot(sender[...], n)], 0).T.astype(bf16)
     first = mm(nodes[...], edge_first[:width]).astype(bf16)
@@ -107,7 +108,7 @@
 
 
 def main_kernel(
-    counts, nodes, cuts, cotangent, slot, cut_receiver, edge_first, edge_second, edge_gain, node_first, node_second,
+    node_count, nodes, cuts, cotangent, slot, cut_receiver, edge_first, edge_second, edge_gain, node_first, node_second,
     node_gain, by_receiver, received_inner, *rest,
 ):
     arrived = rest[:ROUNDS]
@@ -126,7 +127,7 @@
     normed, inverse = norm_parts(mm(act.astype(bf16), edge_second[...]))
     received = (received_inner[...] + mm(hot_receive.astype(bf16), normed.astype(bf16))) * edge_gain[...]
 
-    valid = lax.broadcasted_iota(jnp.int32, (n, width), 0) < counts[:1, :width]
+    valid = lax.broadcasted_iota(jnp.int32, (n, width), 0) < node_count[0]
     pre_node = mm(jnp.concatenate([x, received.astype(bf16)], 1), node_first[...])
     act_node, slope_node = silu_parts(pre_node)
     normed_node, inverse_node = norm_parts(mm(act_node.astype(bf16), node_second[...]))
@@ -141,7 +142,7 @@
     twice = jnp.concatenate([gather[:, :n], gather[:, :n]], 1)
     grad_out = norm_backward(mm(twice, parts), normed, inverse).astype(bf16)
     grad = (mm_t(grad_out, edge_second[...]) * slope).astype(bf16)
-    sums = mm(hot_slot.astype(bf16), grad).astype(bf16)
+    sums = mm(hot_slot[:96].astype(bf16), grad).astype(bf16)
     for r in range(ROUNDS):
         back[r][...] = sums[r * send : (r + 1) * send]
     grad_cut[...] = grad
@@ -151,10 +152,12 @@
 
 def outer_kernel(
     gained, gather, normed, inverse, slope, edge_first, edge_second, sender, receiver, cut_receiver, grad_cut, base,
-    updated_in, updated, edge_gradient, cut_gradient, total,
+    updated_in, boundary, updated, edge_gradient, cut_gradient, total, table, second,
 ):
     n, width = base.shape
     updated[...] = updated_in[...]
+    table[...] = jnp.concatenate([hot(boundary[r], n) for r in range(ROUNDS)], 1).astype(bf16)
+    second[...] = edge_first[width : 2 * width].T
     cut = grad_cut[...]
     cut_gradient[...] = mm_t(cut, edge_first[2 * width :]).astype(bf16)
     twice = jnp.concatenate([gather[...], gather[...]], 1)
@@ -171,16 +174,15 @@
     )
 
 
-def last_kernel(total, boundary, edge_first, *rest):
+def last_kernel(total, table, second, *rest):
     arrived, node_gradient = rest[:ROUNDS], rest[ROUNDS]
-    n, width = total.shape
-    table = jnp.concatenate([hot(boundary[r], n) for r in range(ROUNDS)], 1).astype(bf16)
-    at_sender = mm(table, jnp.concatenate([a[...] for a in arrived], 0)).astype(bf16)
-    node_gradient[...] = (total[...] + mm_t(at_sender, edge_first[width : 2 * width])).astype(bf16)
+    at_sender = mm(table[...], jnp.concatenate([a[...] for a in arrived], 0)).astype(bf16)
+    node_gradient[...] = (total[...] + mm(at_sender, second[...])).astype(bf16)
 
 
 VMEM = pl.BlockSpec(memory_space=pltpu.VMEM)
 HBM = pl.BlockSpec(memory_space=pltpu.HBM)
+SMEM = pl.BlockSpec(memory_space=pltpu.SMEM)
 
 
 def call(kernel, out_shape, args, flops, held=(), scratch=()):
@@ -188,7 +190,7 @@
     return pl.pallas_call(
         kernel,
         out_shape=out_shape,
-        in_specs=[VMEM] * len(args) + [HBM] * len(held),
+        in_specs=[SMEM if a.ndim == 1 else VMEM for a in args] + [HBM] * len(held),
         out_specs=[VMEM] * len(out_shape),
         scratch_shapes=scratch,
         compiler_params=pltpu.CompilerParams(vmem_limit_bytes=32 * 1024 * 1024),
@@ -216,24 +218,17 @@
     def copies(arrays):
         return [kept(a.shape, a.dtype) for a in arrays]
 
-    held = (
-        nodes, boundary, edge_receiver, edge_sender, edge_first, edges, edge_second, slot,
-        cut_targets, edge_gain[None], node_gain[None],
-    )
+    held = (boundary, nodes, edge_receiver, edge_sender, slot, cut_targets, edge_gain[None], node_gain[None])
     outs = call(
         functools.partial(send_kernel, len(held)),
         copies(held) + [kept((send, width), bf16)] * ROUNDS,
         (),
-        2 * 128 * n * width,
+        LONG,
         held,
         [pltpu.SemaphoreType.DMA((len(held),))],
     )
-    (
-        nodes, boundary, edge_receiver, edge_sender, edge_first, edges, edge_second, slot,
-        cut_targets, edge_gain, node_gain,
-    ) = outs[: len(held)]
+    boundary, nodes, edge_receiver, edge_sender, slot, cut_targets, edge_gain, node_gain = outs[: len(held)]
     sent = outs[len(held) :]
-    counts = lax.broadcast_in_dim(jnp.concatenate([node_count, edge_count]), (2, max(e, width)), (0,))
     arrived = exchange(sent)
     outs = call(
         inner_kernel,
@@ -241,8 +236,8 @@
             kept((n, width), bf16), kept((e, n), bf16), kept((e, width), f32), kept((e, 1), f32),
             kept((e, width), f32), kept((n, width), f32),
         ],
-        (counts, nodes, edges, edge_sender, edge_receiver, edge_first, edge_second),
-        2 * e * width * width * 4,
+        (edge_count, nodes, edges, edge_sender, edge_receiver, edge_first, edge_second),
+        LONG,
     )
     by_receiver, gather, normed, inverse, slope, received = outs
     outs = call(
@@ -250,26 +245,29 @@
         [kept((n, width), bf16), kept((n, width), f32), kept((2 * n, width), bf16), kept((c, width), bf16)]
         + [kept((send, width), bf16)] * ROUNDS,
         (
-            counts, nodes, cuts, node_cotangent[0], slot, cut_targets, edge_first, edge_second, edge_gain, node_first,
+            node_count, nodes, cuts, node_cotangent[0], slot, cut_targets, edge_first, edge_second, edge_gain, node_first,
             node_second, node_gain, by_receiver, received, *arrived,
         ),
         2 * c * width * width * 6,
     )
     updated, base, gained, grad_cut = outs[:4]
     returned = exchange(outs[4:])
-    updated, edge_gradient, cut_gradient, total = call(
+    updated, edge_gradient, cut_gradient, total, table, second = call(
         outer_kernel,
-        [shape((n, width), bf16), shape((e, width), bf16), shape((c, width), bf16), kept((n, width), f32)],
+        [
+            shape((n, width), bf16), shape((e, width), bf16), shape((c, width), bf16), kept((n, width), f32),
+            kept((n, ROUNDS * send), bf16), kept((width, width), bf16),
+        ],
         (
             gained, gather, normed, inverse, slope, edge_first, edge_second, edge_sender, edge_receiver,
-            cut_targets, grad_cut, base, updated,
+            cut_targets, grad_cut, base, updated, boundary,
         ),
         2 * (e + c) * width * width * 3,
     )
     (node_gradient,) = call(
         last_kernel,
         [shape((n, width), bf16)],
-        (total, boundary, edge_first, *returned),
+        (total, table, second, *returned),
         2 * 2 * n * width * width,
     )
     return (

time: 21.5 us -> 21.1 us (0.981)
  Pallas kernels: 6.96 us -> 6.68 us
    pallas_call x5, Pallas kernels: 6.96 us -> 6.68 us  [call(): pl.pallas_call(kernel, out_shape=out_shape, in_specs=[SMEM if a.ndim == 1...]
  transfers between devices with their start and end apart: 10 -> 10, of which waited for: 2 -> 2; matrix products, arithmetic and copies ran while one was open for 1% -> 0% of each run, Pallas kernels for 12% -> 12%
where the time goes in v3:
time: 21.1 us; the launch traced here: 21 us
  starting transfers between devices  11.4 us (54%)
  Pallas kernels  6.68 us (32%)
  between operations  2.12 us (10%)
  waiting for transfers between devices  0.76 us (4%)
    ppermute x10, starting transfers between devices, partner(): lax.ppermute(shard, axis, [(i, i ^ 1 << apart) for i in range(lax.axis_si...  11.4 us
    pallas_call x5, Pallas kernels, call(): pl.pallas_call(kernel, out_shape=out_shape, in_specs=[SMEM if a.ndim == 1...  6.68 us
    ppermute x10, waiting for transfers between devices, partner(): lax.ppermute(shard, axis, [(i, i ^ 1 << apart) for i in range(lax.axis_si...  0.76 us
  transfers between devices with their start and end apart: 10, of which 2 were waited for; matrix products, arithmetic and copies ran while one was open for 0% of the time, Pallas kernels for 12%

profile of v3, /device:TPU:0, one launch (start us, length us, event | category | flops | bytes accessed | tf_op | source)
XLA Modules:
  0.0 21.0 jit_solution(10079805508660363007)
XLA Ops:
  0.6 0.0 copy-start
  0.6 0.0 copy-start.1
  0.7 0.0 copy-start.6
  0.7 1.1 %shard_map.192 = (s32[5,1,16]{2,1,0:T(1,128)S(1)}, bf16[128,256]{1,0:T(8,128)(2,1)S(1)}, s32[1,384]{1,0:T(1,128)S(1)}, s32[1,384]{1,0:T(1,128)S(1)}, s32[5,1,64]...) custom-call(s32[5,1,16]{2,1,0:T(1,128)} %bitcast.21, ...), custom_call_target="tpu_custom_call" | custom-call | flops 4000000000 | bytes 73536 | tf_op jit(solution)/shard_map/pallas_call | solution.py:190
  1.8 4.1 %collective-permute-start = (bf16[16,256]{1,0:T(8,128)(2,1)S(1)}, bf16[16,256]{1,0:T(8,128)(2,1)S(1)}, u32[]{:S(2)}, u32[]{:S(2)}) collective-permute-start(bf16[16,256]{1,0:T(8,128)(2,1)S(1)} %get-tuple-element.57), channel_id=1, source_target_pairs={{0,4},{1,5},{2,6},{3,7},{4,0},{5,1},{6,2},{7,3},{8,12},{9,13},{10,... | collective-permute-start | bytes 24584 | tf_op jit(solution)/shard_map/ppermute | solution.py:22
  5.9 1.6 %collective-permute-start.1 = (bf16[16,256]{1,0:T(8,128)(2,1)S(1)}, bf16[16,256]{1,0:T(8,128)(2,1)S(1)}, u32[]{:S(2)}, u32[]{:S(2)}) collective-permute-start(bf16[16,256]{1,0:T(8,128)(2,1)S(1)} %get-tuple-element.58), channel_id=1, source_target_pairs={{0,2},{1,3},{2,0},{3,1},{4,6},{5,7},{6,4},{7,5},{8,10},{9,11},{10,... | collective-permute-start | bytes 24584 | tf_op jit(solution)/shard_map/ppermute | solution.py:22
  7.5 1.5 %collective-permute-start.2 = (bf16[16,256]{1,0:T(8,128)(2,1)S(1)}, bf16[16,256]{1,0:T(8,128)(2,1)S(1)}, u32[]{:S(2)}, u32[]{:S(2)}) collective-permute-start(bf16[16,256]{1,0:T(8,128)(2,1)S(1)} %get-tuple-element.59), channel_id=1, source_target_pairs={{0,1},{1,0},{2,3},{3,2},{4,5},{5,4},{6,7},{7,6},{8,9},{9,8},{10,11... | collective-permute-start | bytes 24584 | tf_op jit(solution)/shard_map/ppermute | solution.py:22
  9.0 1.5 %collective-permute-start.3 = (bf16[16,256]{1,0:T(8,128)(2,1)S(1)}, bf16[16,256]{1,0:T(8,128)(2,1)S(1)}, u32[]{:S(2)}, u32[]{:S(2)}) collective-permute-start(bf16[16,256]{1,0:T(8,128)(2,1)S(1)} %get-tuple-element.60), channel_id=1, source_target_pairs={{0,16},{8,24},{16,0},{24,8},{1,17},{9,25},{17,1},{25,9},{2,18},{10... | collective-permute-start | bytes 24584 | tf_op jit(solution)/shard_map/ppermute | solution.py:22
  10.5 0.0 collective-permute-start.4
  11.2 0.0 copy-start.2
  11.2 0.0 copy-start.3
  11.2 0.0 copy-start.4
  11.2 0.0 copy-start.5
  11.2 0.9 %shard_map.193 = (bf16[128,256]{1,0:T(8,128)(2,1)S(1)}, bf16[384,128]{1,0:T(8,128)(2,1)S(1)}, f32[384,256]{1,0:T(8,128)S(1)}, f32[384,1]{1,0:T(8,128)S(1)}, f32[...) custom-call(s32[1]{0:T(128)S(6)} %copy.22.rest_0_, bf16[128,256]{1,0:T(8,128)(2,1)S(1)} %get-tuple-element.48.rest_1_.nodes, ...), custom_call_target="tpu_custom_call" | custom-call | flops 4000000000 | bytes 789508 | tf_op jit(solution)/shard_map/pallas_call | solution.py:190
  12.8 0.0 collective-permute-done.rest_4_
  12.8 0.0 collective-permute-done.1.rest_3_
  12.8 0.0 collective-permute-done.2.rest_2_
  12.8 0.0 collective-permute-done.3.rest_1_
  12.8 0.0 collective-permute-done.4.rest_0_
  12.9 2.2 %shard_map.194 = (bf16[128,256]{1,0:T(8,128)(2,1)S(1)}, f32[128,256]{1,0:T(8,128)S(1)}, bf16[256,256]{1,0:T(8,128)(2,1)S(1)}, bf16[320,256]{1,0:T(8,128)(2,1)S(1...) custom-call(s32[1]{0:T(128)S(6)} %copy.21.node_count, ...), custom_call_target="tpu_custom_call" | custom-call | flops 251658240 | bytes 1454596 | tf_op jit(solution)/shard_map/pallas_call | solution.py:190
  15.1 0.4 %collective-permute-start.5 = (bf16[16,256]{1,0:T(8,128)(2,1)S(1)}, bf16[16,256]{1,0:T(8,128)(2,1)S(1)}, u32[]{:S(2)}, u32[]{:S(2)}) collective-permute-start(bf16[16,256]{1,0:T(8,128)(2,1)S(1)} %get-tuple-element.80), channel_id=1, source_target_pairs={{0,4},{1,5},{2,6},{3,7},{4,0},{5,1},{6,2},{7,3},{8,12},{9,13},{10,... | collective-permute-start | bytes 24584 | tf_op jit(solution)/shard_map/ppermute | solution.py:22
  15.5 0.5 %collective-permute-start.6 = (bf16[16,256]{1,0:T(8,128)(2,1)S(1)}, bf16[16,256]{1,0:T(8,128)(2,1)S(1)}, u32[]{:S(2)}, u32[]{:S(2)}) collective-permute-start(bf16[16,256]{1,0:T(8,128)(2,1)S(1)} %get-tuple-element.81), channel_id=1, source_target_pairs={{0,2},{1,3},{2,0},{3,1},{4,6},{5,7},{6,4},{7,5},{8,10},{9,11},{10,... | collective-permute-start | bytes 24584 | tf_op jit(solution)/shard_map/ppermute | solution.py:22
  15.9 0.5 %collective-permute-start.7 = (bf16[16,256]{1,0:T(8,128)(2,1)S(1)}, bf16[16,256]{1,0:T(8,128)(2,1)S(1)}, u32[]{:S(2)}, u32[]{:S(2)}) collective-permute-start(bf16[16,256]{1,0:T(8,128)(2,1)S(1)} %get-tuple-element.82), channel_id=1, source_target_pairs={{0,1},{1,0},{2,3},{3,2},{4,5},{5,4},{6,7},{7,6},{8,9},{9,8},{10,11... | collective-permute-start | bytes 24584 | tf_op jit(solution)/shard_map/ppermute | solution.py:22
  16.4 1.3 %collective-permute-start.8 = (bf16[16,256]{1,0:T(8,128)(2,1)S(1)}, bf16[16,256]{1,0:T(8,128)(2,1)S(1)}, u32[]{:S(2)}, u32[]{:S(2)}) collective-permute-start(bf16[16,256]{1,0:T(8,128)(2,1)S(1)} %get-tuple-element.83), channel_id=1, source_target_pairs={{0,16},{8,24},{16,0},{24,8},{1,17},{9,25},{17,1},{25,9},{2,18},{10... | collective-permute-start | bytes 24584 | tf_op jit(solution)/shard_map/ppermute | solution.py:22
  17.7 0.0 collective-permute-start.9
  17.7 1.6 %shard_map.195 = (bf16[128,256]{1,0:T(8,128)(2,1)}, bf16[384,256]{1,0:T(8,128)(2,1)}, bf16[320,256]{1,0:T(8,128)(2,1)}, f32[128,256]{1,0:T(8,128)S(1)}, bf16[128...) custom-call(bf16[256,256]{1,0:T(8,128)(2,1)S(1)} %get-tuple-element.67.gained, ...), custom_call_target="tpu_custom_call" | custom-call | flops 276824064 | bytes 1906752 | tf_op jit(solution)/shard_map/pallas_call | solution.py:190
  19.3 0.4 %collective-permute-done.5.rest_4_ = bf16[16,256]{1,0:T(8,128)(2,1)S(1)} collective-permute-done((bf16[16,256]{1,0:T(8,128)(2,1)S(1)}, bf16[16,256]{1,0:T(8,128)(2,1)S(1)}, u32[]{:S(2)}, u32[]{:S(2)}) %collective-permute-start.5) | collective-permute-done | bytes 8224 | tf_op jit(solution)/shard_map/ppermute | solution.py:22
  19.7 0.0 collective-permute-done.6.rest_3_
  19.7 0.0 collective-permute-done.7.rest_2_
  19.7 0.4 %collective-permute-done.8.rest_1_ = bf16[16,256]{1,0:T(8,128)(2,1)S(1)} collective-permute-done((bf16[16,256]{1,0:T(8,128)(2,1)S(1)}, bf16[16,256]{1,0:T(8,128)(2,1)S(1)}, u32[]{:S(2)}, u32[]{:S(2)}) %collective-permute-start.8) | collective-permute-done | bytes 8224 | tf_op jit(solution)/shard_map/ppermute | solution.py:22
  20.1 0.0 collective-permute-done.9.rest_0_
  20.1 0.9 %shard_map.196 = bf16[128,256]{1,0:T(8,128)(2,1)} custom-call(f32[128,256]{1,0:T(8,128)S(1)} %get-tuple-element.77.total, bf16[128,80]{1,0:T(8,128)(2,1)S(1)} %get-tuple-element.78.table, bf16[256,256]{1,0:T(8,128)(2,1)S(1)} %get-tuple-element.79.second, bf16[16,256]{1,0:T(8,128)(2,1)S(1)} %collective-permute-done.9.rest_0_, ...), custom_call_target="tpu_custom_call" | custom-call | flops 33554432 | bytes 323584 | tf_op jit(solution)/shard_map/pallas_call | solution.py:190
  (7 shorter events, 0.0 us)
Async XLA Ops:
  0.6 10.5 %copy-start = (bf16[768,256]{1,0:T(8,128)(2,1)S(1)}, bf16[768,256]{1,0:T(8,128)(2,1)}, u32[]{:S(2)}) copy-start(bf16[768,256]{1,0:T(8,128)(2,1)} %edge_first.3) | copy-start | bytes 1179652
  0.6 10.5 %copy-start.1 = (bf16[256,256]{1,0:T(8,128)(2,1)S(1)}, bf16[256,256]{1,0:T(8,128)(2,1)}, u32[]{:S(2)}) copy-start(bf16[256,256]{1,0:T(8,128)(2,1)} %edge_second.3) | copy-start | bytes 393220
  0.7 10.5 %copy-start.6 = (bf16[1,384,256]{2,1,0:T(8,128)(2,1)S(1)}, bf16[1,384,256]{2,1,0:T(8,128)(2,1)}, u32[]{:S(2)}) copy-start(bf16[1,384,256]{2,1,0:T(8,128)(2,1)} %param.18) | copy-start | bytes 589828
  1.8 11.0 %collective-permute-start = (bf16[16,256]{1,0:T(8,128)(2,1)S(1)}, bf16[16,256]{1,0:T(8,128)(2,1)S(1)}, u32[]{:S(2)}, u32[]{:S(2)}) collective-permute-start(bf16[16,256]{1,0:T(8,128)(2,1)S(1)} %get-tuple-element.57), channel_id=1, source_target_pairs={{0,4},{1,5},{2,6},{3,7},{4,0},{5,1},{6,2},{7,3},{8,12},{9,13},{10,... | collective-permute-start | bytes 24584 | tf_op jit(solution)/shard_map/ppermute | solution.py:22
  5.9 6.9 %collective-permute-start.1 = (bf16[16,256]{1,0:T(8,128)(2,1)S(1)}, bf16[16,256]{1,0:T(8,128)(2,1)S(1)}, u32[]{:S(2)}, u32[]{:S(2)}) collective-permute-start(bf16[16,256]{1,0:T(8,128)(2,1)S(1)} %get-tuple-element.58), channel_id=1, source_target_pairs={{0,2},{1,3},{2,0},{3,1},{4,6},{5,7},{6,4},{7,5},{8,10},{9,11},{10,... | collective-permute-start | bytes 24584 | tf_op jit(solution)/shard_map/ppermute | solution.py:22
  7.5 5.3 %collective-permute-start.2 = (bf16[16,256]{1,0:T(8,128)(2,1)S(1)}, bf16[16,256]{1,0:T(8,128)(2,1)S(1)}, u32[]{:S(2)}, u32[]{:S(2)}) collective-permute-start(bf16[16,256]{1,0:T(8,128)(2,1)S(1)} %get-tuple-element.59), channel_id=1, source_target_pairs={{0,1},{1,0},{2,3},{3,2},{4,5},{5,4},{6,7},{7,6},{8,9},{9,8},{10,11... | collective-permute-start | bytes 24584 | tf_op jit(solution)/shard_map/ppermute | solution.py:22
  9.0 3.8 %collective-permute-start.3 = (bf16[16,256]{1,0:T(8,128)(2,1)S(1)}, bf16[16,256]{1,0:T(8,128)(2,1)S(1)}, u32[]{:S(2)}, u32[]{:S(2)}) collective-permute-start(bf16[16,256]{1,0:T(8,128)(2,1)S(1)} %get-tuple-element.60), channel_id=1, source_target_pairs={{0,16},{8,24},{16,0},{24,8},{1,17},{9,25},{17,1},{25,9},{2,18},{10... | collective-permute-start | bytes 24584 | tf_op jit(solution)/shard_map/ppermute | solution.py:22
  10.5 2.3 %collective-permute-start.4 = (bf16[16,256]{1,0:T(8,128)(2,1)S(1)}, bf16[16,256]{1,0:T(8,128)(2,1)S(1)}, u32[]{:S(2)}, u32[]{:S(2)}) collective-permute-start(bf16[16,256]{1,0:T(8,128)(2,1)S(1)} %get-tuple-element.61), channel_id=1, source_target_pairs={{0,8},{8,0},{16,24},{24,16},{1,9},{9,1},{17,25},{25,17},{2,10},{10... | collective-permute-start | bytes 24584 | tf_op jit(solution)/shard_map/ppermute | solution.py:22
  11.2 1.6 %copy-start.2 = (bf16[512,256]{1,0:T(8,128)(2,1)S(1)}, bf16[512,256]{1,0:T(8,128)(2,1)}, u32[]{:S(2)}) copy-start(bf16[512,256]{1,0:T(8,128)(2,1)} %node_first.1) | copy-start | bytes 786436
  11.2 1.6 %copy-start.3 = (bf16[1,5,64,256]{3,2,1,0:T(8,128)(2,1)S(1)}, bf16[1,5,64,256]{3,2,1,0:T(8,128)(2,1)}, u32[]{:S(2)}) copy-start(bf16[1,5,64,256]{3,2,1,0:T(8,128)(2,1)} %param.19) | copy-start | bytes 491524
  11.2 1.6 %copy-start.4 = (bf16[256,256]{1,0:T(8,128)(2,1)S(1)}, bf16[256,256]{1,0:T(8,128)(2,1)}, u32[]{:S(2)}) copy-start(bf16[256,256]{1,0:T(8,128)(2,1)} %node_second.1) | copy-start | bytes 393220
  11.2 1.6 %copy-start.5 = (bf16[1,128,256]{2,1,0:T(8,128)(2,1)S(1)}, bf16[1,128,256]{2,1,0:T(8,128)(2,1)}, u32[]{:S(2)}) copy-start(bf16[1,128,256]{2,1,0:T(8,128)(2,1)} %param.20) | copy-start | bytes 196612
  15.1 4.6 %collective-permute-start.5 = (bf16[16,256]{1,0:T(8,128)(2,1)S(1)}, bf16[16,256]{1,0:T(8,128)(2,1)S(1)}, u32[]{:S(2)}, u32[]{:S(2)}) collective-permute-start(bf16[16,256]{1,0:T(8,128)(2,1)S(1)} %get-tuple-element.80), channel_id=1, source_target_pairs={{0,4},{1,5},{2,6},{3,7},{4,0},{5,1},{6,2},{7,3},{8,12},{9,13},{10,... | collective-permute-start | bytes 24584 | tf_op jit(solution)/shard_map/ppermute | solution.py:22
  15.5 4.2 %collective-permute-start.6 = (bf16[16,256]{1,0:T(8,128)(2,1)S(1)}, bf16[16,256]{1,0:T(8,128)(2,1)S(1)}, u32[]{:S(2)}, u32[]{:S(2)}) collective-permute-start(bf16[16,256]{1,0:T(8,128)(2,1)S(1)} %get-tuple-element.81), channel_id=1, source_target_pairs={{0,2},{1,3},{2,0},{3,1},{4,6},{5,7},{6,4},{7,5},{8,10},{9,11},{10,... | collective-permute-start | bytes 24584 | tf_op jit(solution)/shard_map/ppermute | solution.py:22
  15.9 3.8 %collective-permute-start.7 = (bf16[16,256]{1,0:T(8,128)(2,1)S(1)}, bf16[16,256]{1,0:T(8,128)(2,1)S(1)}, u32[]{:S(2)}, u32[]{:S(2)}) collective-permute-start(bf16[16,256]{1,0:T(8,128)(2,1)S(1)} %get-tuple-element.82), channel_id=1, source_target_pairs={{0,1},{1,0},{2,3},{3,2},{4,5},{5,4},{6,7},{7,6},{8,9},{9,8},{10,11... | collective-permute-start | bytes 24584 | tf_op jit(solution)/shard_map/ppermute | solution.py:22
  16.4 3.7 %collective-permute-start.8 = (bf16[16,256]{1,0:T(8,128)(2,1)S(1)}, bf16[16,256]{1,0:T(8,128)(2,1)S(1)}, u32[]{:S(2)}, u32[]{:S(2)}) collective-permute-start(bf16[16,256]{1,0:T(8,128)(2,1)S(1)} %get-tuple-element.83), channel_id=1, source_target_pairs={{0,16},{8,24},{16,0},{24,8},{1,17},{9,25},{17,1},{25,9},{2,18},{10... | collective-permute-start | bytes 24584 | tf_op jit(solution)/shard_map/ppermute | solution.py:22
  17.7 2.3 %collective-permute-start.9 = (bf16[16,256]{1,0:T(8,128)(2,1)S(1)}, bf16[16,256]{1,0:T(8,128)(2,1)S(1)}, u32[]{:S(2)}, u32[]{:S(2)}) collective-permute-start(bf16[16,256]{1,0:T(8,128)(2,1)S(1)} %get-tuple-element.84), channel_id=1, source_target_pairs={{0,8},{8,0},{16,24},{24,16},{1,9},{9,1},{17,25},{25,17},{2,10},{10... | collective-permute-start | bytes 24584 | tf_op jit(solution)/shard_map/ppermute | solution.py:22

commit v4 on v3

--- a/solution.py
+++ b/solution.py
@@ -8,8 +8,8 @@
 from jax.sharding import PartitionSpec as P
 
 ROUNDS = 5
+GRP_ROUNDS = 2
 LONG = 4 * 10**9
-GRP_ROUNDS = 2
 
 epsilon = 1e-05
 
@@ -35,13 +35,18 @@
     return lax.dot_general(a, b, (((1,), (1,)), ((), ())), preferred_element_type=f32)
 
 
-def t_mm(a, b):
-    return lax.dot_general(a, b, (((0,), (0,)), ((), ())), preferred_element_type=f32)
-
-
 def hot(row, count):
     shape = (count, row.shape[1])
     return (lax.broadcasted_iota(jnp.int32, shape, 0) == jnp.broadcast_to(row, shape)).astype(f32)
+
+
+def split(values):
+    high = values.astype(bf16)
+    return high, (values - high.astype(f32)).astype(bf16)
+
+
+def add_rows(table, values):
+    return mm(jnp.concatenate([table, table], 1), jnp.concatenate(split(values), 0))
 
 
 def lane_mean(values):
@@ -94,17 +99,17 @@
     used = lax.broadcasted_iota(jnp.int32, (1, e), 1) < edge_count[0]
     hot_receive = hot(jnp.where(used, receiver[...], -1), n)
     gather = jnp.concatenate([hot_receive, hot(sender[...], n)], 0).T.astype(bf16)
-    first = mm(nodes[...], edge_first[:width]).astype(bf16)
-    second = mm(nodes[...], edge_first[width : 2 * width]).astype(bf16)
-    pre = mm(gather, jnp.concatenate([first, second], 0)) + mm(edges[...], edge_first[2 * width :])
+    first = mm(nodes[...], edge_first[:width])
+    second = mm(nodes[...], edge_first[width : 2 * width])
+    pre = add_rows(gather, jnp.concatenate([first, second], 0)) + mm(edges[...], edge_first[2 * width :])
     act, slope = silu_parts(pre)
     normed, inverse = norm_parts(mm(act.astype(bf16), edge_second[...]))
-    by_receiver[...] = first
+    by_receiver[...] = jnp.concatenate(split(first), 0)
     gather_out[...] = gather[:, :n]
     normed_out[...] = normed
     inverse_out[...] = inverse
     slope_out[...] = slope
-    received[...] = mm(hot_receive.astype(bf16), normed.astype(bf16))
+    received[...] = add_rows(hot_receive.astype(bf16), normed)
 
 
 def main_kernel(
@@ -119,13 +124,14 @@
     x = nodes[...]
     hot_receive = jnp.concatenate([hot(cut_receiver[r], n) for r in range(ROUNDS)], 1)
     hot_slot = hot(jnp.concatenate([slot[r] + r * send for r in range(ROUNDS)], 1), 128)
-    gather = jnp.concatenate([hot_receive, hot_slot], 0).T.astype(bf16)
+    gather = hot_receive.T.astype(bf16)
+    twice = jnp.concatenate([gather, gather], 1)
+    near = mm(twice, by_receiver[...]) + mm(cuts[...], edge_first[2 * width :])
     far = jnp.concatenate([a[...] for a in arrived] + [jnp.zeros((128 - ROUNDS * send, width), bf16)], 0)
-    by_sender = mm(far, edge_first[width : 2 * width]).astype(bf16)
-    pre = mm(gather, jnp.concatenate([by_receiver[...], by_sender], 0)) + mm(cuts[...], edge_first[2 * width :])
+    pre = near + add_rows(hot_slot.T.astype(bf16), mm(far, edge_first[width : 2 * width]))
     act, slope = silu_parts(pre)
     normed, inverse = norm_parts(mm(act.astype(bf16), edge_second[...]))
-    received = (received_inner[...] + mm(hot_receive.astype(bf16), normed.astype(bf16))) * edge_gain[...]
+    received = (received_inner[...] + add_rows(hot_receive.astype(bf16), normed)) * edge_gain[...]
 
     valid = lax.broadcasted_iota(jnp.int32, (n, width), 0) < node_count[0]
     pre_node = mm(jnp.concatenate([x, received.astype(bf16)], 1), node_first[...])
@@ -136,10 +142,7 @@
     grad_out_node = norm_backward(masked * node_gain[...], normed_node, inverse_node).astype(bf16)
     grad_pre_node = (mm_t(grad_out_node, node_second[...]) * slope_node).astype(bf16)
     at_receiver = mm_t(grad_pre_node, node_first[width:]) * edge_gain[...]
-    high = at_receiver.astype(bf16)
-    low = (at_receiver - high.astype(f32)).astype(bf16)
-    parts = jnp.concatenate([high, low], 0)
-    twice = jnp.concatenate([gather[:, :n], gather[:, :n]], 1)
+    parts = jnp.concatenate(split(at_receiver), 0)
     grad_out = norm_backward(mm(twice, parts), normed, inverse).astype(bf16)
     grad = (mm_t(grad_out, edge_second[...]) * slope).astype(bf16)
     sums = mm(hot_slot[:96].astype(bf16), grad).astype(bf16)
@@ -233,7 +236,7 @@
     outs = call(
         inner_kernel,
         [
-            kept((n, width), bf16), kept((e, n), bf16), kept((e, width), f32), kept((e, 1), f32),
+            kept((2 * n, width), bf16), kept((e, n), bf16), kept((e, width), f32), kept((e, 1), f32),
             kept((e, width), f32), kept((n, width), f32),
         ],
         (edge_count, nodes, edges, edge_sender, edge_receiver, edge_first, edge_second),

time: 21.1 us -> 21.4 us (1.014)
  Pallas kernels: 6.68 us -> 6.94 us
    pallas_call x5, Pallas kernels: 6.68 us -> 6.94 us  [call(): pl.pallas_call(kernel, out_shape=out_shape, in_specs=[SMEM if a.ndim == 1...]
where the time goes in v4:
time: 21.4 us; the launch traced here: 21.2 us
  starting transfers between devices  11.2 us (52%)
  Pallas kernels  6.94 us (32%)
  between operations  2.12 us (10%)
  waiting for transfers between devices  0.92 us (4%)
    ppermute x10, starting transfers between devices, partner(): lax.ppermute(shard, axis, [(i, i ^ 1 << apart) for i in range(lax.axis_si...  11.2 us
    pallas_call x5, Pallas kernels, call(): pl.pallas_call(kernel, out_shape=out_shape, in_specs=[SMEM if a.ndim == 1...  6.94 us
    ppermute x10, waiting for transfers between devices, partner(): lax.ppermute(shard, axis, [(i, i ^ 1 << apart) for i in range(lax.axis_si...  0.92 us
  transfers between devices with their start and end apart: 10, of which 2 were waited for; matrix products, arithmetic and copies ran while one was open for 0% of the time, Pallas kernels for 12%

profile of v4, /device:TPU:0, one launch (start us, length us, event | category | flops | bytes accessed | tf_op | source)
XLA Modules:
  0.0 21.2 jit_solution(14828387784879707451)
XLA Ops:
  0.7 1.1 %shard_map.192 = (s32[5,1,16]{2,1,0:T(1,128)S(1)}, bf16[128,256]{1,0:T(8,128)(2,1)S(1)}, s32[1,384]{1,0:T(1,128)S(1)}, s32[1,384]{1,0:T(1,128)S(1)}, s32[5,1,64]...) custom-call(s32[5,1,16]{2,1,0:T(1,128)} %bitcast.21, ...), custom_call_target="tpu_custom_call" | custom-call | flops 4000000000 | bytes 73536 | tf_op jit(solution)/shard_map/pallas_call | solution.py:193
  1.8 4.1 %collective-permute-start = (bf16[16,256]{1,0:T(8,128)(2,1)S(1)}, bf16[16,256]{1,0:T(8,128)(2,1)S(1)}, u32[]{:S(2)}, u32[]{:S(2)}) collective-permute-start(bf16[16,256]{1,0:T(8,128)(2,1)S(1)} %get-tuple-element.57), channel_id=1, source_target_pairs={{0,4},{1,5},{2,6},{3,7},{4,0},{5,1},{6,2},{7,3},{8,12},{9,13},{10,... | collective-permute-start | bytes 24584 | tf_op jit(solution)/shard_map/ppermute | solution.py:22
  5.9 1.6 %collective-permute-start.1 = (bf16[16,256]{1,0:T(8,128)(2,1)S(1)}, bf16[16,256]{1,0:T(8,128)(2,1)S(1)}, u32[]{:S(2)}, u32[]{:S(2)}) collective-permute-start(bf16[16,256]{1,0:T(8,128)(2,1)S(1)} %get-tuple-element.58), channel_id=1, source_target_pairs={{0,2},{1,3},{2,0},{3,1},{4,6},{5,7},{6,4},{7,5},{8,10},{9,11},{10,... | collective-permute-start | bytes 24584 | tf_op jit(solution)/shard_map/ppermute | solution.py:22
  7.5 1.5 %collective-permute-start.2 = (bf16[16,256]{1,0:T(8,128)(2,1)S(1)}, bf16[16,256]{1,0:T(8,128)(2,1)S(1)}, u32[]{:S(2)}, u32[]{:S(2)}) collective-permute-start(bf16[16,256]{1,0:T(8,128)(2,1)S(1)} %get-tuple-element.59), channel_id=1, source_target_pairs={{0,1},{1,0},{2,3},{3,2},{4,5},{5,4},{6,7},{7,6},{8,9},{9,8},{10,11... | collective-permute-start | bytes 24584 | tf_op jit(solution)/shard_map/ppermute | solution.py:22
  9.0 1.5 %collective-permute-start.3 = (bf16[16,256]{1,0:T(8,128)(2,1)S(1)}, bf16[16,256]{1,0:T(8,128)(2,1)S(1)}, u32[]{:S(2)}, u32[]{:S(2)}) collective-permute-start(bf16[16,256]{1,0:T(8,128)(2,1)S(1)} %get-tuple-element.60), channel_id=1, source_target_pairs={{0,16},{8,24},{16,0},{24,8},{1,17},{9,25},{17,1},{25,9},{2,18},{10... | collective-permute-start | bytes 24584 | tf_op jit(solution)/shard_map/ppermute | solution.py:22
  10.5 0.0 collective-permute-start.4
  11.2 0.0 copy-start.2
  11.2 0.0 copy-start.3
  11.2 0.0 copy-start.4
  11.2 0.0 copy-start.5
  11.2 1.0 %shard_map.193 = (bf16[256,256]{1,0:T(8,128)(2,1)S(1)}, bf16[384,128]{1,0:T(8,128)(2,1)S(1)}, f32[384,256]{1,0:T(8,128)S(1)}, f32[384,1]{1,0:T(8,128)S(1)}, f32[...) custom-call(s32[1]{0:T(128)S(6)} %copy.22.rest_0_, bf16[128,256]{1,0:T(8,128)(2,1)S(1)} %get-tuple-element.48.rest_1_.nodes, ...), custom_call_target="tpu_custom_call" | custom-call | flops 4000000000 | bytes 789508 | tf_op jit(solution)/shard_map/pallas_call | solution.py:193
  12.9 0.0 collective-permute-done.rest_4_
  13.0 0.0 collective-permute-done.1.rest_3_
  13.0 0.0 collective-permute-done.2.rest_2_
  13.0 0.0 collective-permute-done.3.rest_1_
  13.0 0.0 collective-permute-done.4.rest_0_
  13.0 0.0 copy-done.2
  13.0 0.0 copy-done.3
  13.0 0.0 copy-done.4
  13.0 2.3 %shard_map.194 = (bf16[128,256]{1,0:T(8,128)(2,1)S(1)}, f32[128,256]{1,0:T(8,128)S(1)}, bf16[256,256]{1,0:T(8,128)(2,1)S(1)}, bf16[320,256]{1,0:T(8,128)(2,1)S(1...) custom-call(s32[1]{0:T(128)S(6)} %copy.21.node_count, ...), custom_call_target="tpu_custom_call" | custom-call | flops 251658240 | bytes 1520132 | tf_op jit(solution)/shard_map/pallas_call | solution.py:193
  15.3 0.4 %collective-permute-start.5 = (bf16[16,256]{1,0:T(8,128)(2,1)S(1)}, bf16[16,256]{1,0:T(8,128)(2,1)S(1)}, u32[]{:S(2)}, u32[]{:S(2)}) collective-permute-start(bf16[16,256]{1,0:T(8,128)(2,1)S(1)} %get-tuple-element.80), channel_id=1, source_target_pairs={{0,4},{1,5},{2,6},{3,7},{4,0},{5,1},{6,2},{7,3},{8,12},{9,13},{10,... | collective-permute-start | bytes 24584 | tf_op jit(solution)/shard_map/ppermute | solution.py:22
  15.7 0.5 %collective-permute-start.6 = (bf16[16,256]{1,0:T(8,128)(2,1)S(1)}, bf16[16,256]{1,0:T(8,128)(2,1)S(1)}, u32[]{:S(2)}, u32[]{:S(2)}) collective-permute-start(bf16[16,256]{1,0:T(8,128)(2,1)S(1)} %get-tuple-element.81), channel_id=1, source_target_pairs={{0,2},{1,3},{2,0},{3,1},{4,6},{5,7},{6,4},{7,5},{8,10},{9,11},{10,... | collective-permute-start | bytes 24584 | tf_op jit(solution)/shard_map/ppermute | solution.py:22
  16.2 0.5 %collective-permute-start.7 = (bf16[16,256]{1,0:T(8,128)(2,1)S(1)}, bf16[16,256]{1,0:T(8,128)(2,1)S(1)}, u32[]{:S(2)}, u32[]{:S(2)}) collective-permute-start(bf16[16,256]{1,0:T(8,128)(2,1)S(1)} %get-tuple-element.82), channel_id=1, source_target_pairs={{0,1},{1,0},{2,3},{3,2},{4,5},{5,4},{6,7},{7,6},{8,9},{9,8},{10,11... | collective-permute-start | bytes 24584 | tf_op jit(solution)/shard_map/ppermute | solution.py:22
  16.7 1.2 %collective-permute-start.8 = (bf16[16,256]{1,0:T(8,128)(2,1)S(1)}, bf16[16,256]{1,0:T(8,128)(2,1)S(1)}, u32[]{:S(2)}, u32[]{:S(2)}) collective-permute-start(bf16[16,256]{1,0:T(8,128)(2,1)S(1)} %get-tuple-element.83), channel_id=1, source_target_pairs={{0,16},{8,24},{16,0},{24,8},{1,17},{9,25},{17,1},{25,9},{2,18},{10... | collective-permute-start | bytes 24584 | tf_op jit(solution)/shard_map/ppermute | solution.py:22
  17.8 0.0 collective-permute-start.9
  17.8 1.6 %shard_map.195 = (bf16[128,256]{1,0:T(8,128)(2,1)}, bf16[384,256]{1,0:T(8,128)(2,1)}, bf16[320,256]{1,0:T(8,128)(2,1)}, f32[128,256]{1,0:T(8,128)S(1)}, bf16[128...) custom-call(bf16[256,256]{1,0:T(8,128)(2,1)S(1)} %get-tuple-element.67.gained, ...), custom_call_target="tpu_custom_call" | custom-call | flops 276824064 | bytes 1906752 | tf_op jit(solution)/shard_map/pallas_call | solution.py:193
  19.4 0.5 %collective-permute-done.5.rest_4_ = bf16[16,256]{1,0:T(8,128)(2,1)S(1)} collective-permute-done((bf16[16,256]{1,0:T(8,128)(2,1)S(1)}, bf16[16,256]{1,0:T(8,128)(2,1)S(1)}, u32[]{:S(2)}, u32[]{:S(2)}) %collective-permute-start.5) | collective-permute-done | bytes 8224 | tf_op jit(solution)/shard_map/ppermute | solution.py:22
  19.9 0.0 collective-permute-done.6.rest_3_
  19.9 0.0 collective-permute-done.7.rest_2_
  19.9 0.4 %collective-permute-done.8.rest_1_ = bf16[16,256]{1,0:T(8,128)(2,1)S(1)} collective-permute-done((bf16[16,256]{1,0:T(8,128)(2,1)S(1)}, bf16[16,256]{1,0:T(8,128)(2,1)S(1)}, u32[]{:S(2)}, u32[]{:S(2)}) %collective-permute-start.8) | collective-permute-done | bytes 8224 | tf_op jit(solution)/shard_map/ppermute | solution.py:22
  20.3 0.0 collective-permute-done.9.rest_0_
  20.3 0.9 %shard_map.196 = bf16[128,256]{1,0:T(8,128)(2,1)} custom-call(f32[128,256]{1,0:T(8,128)S(1)} %get-tuple-element.77.total, bf16[128,80]{1,0:T(8,128)(2,1)S(1)} %get-tuple-element.78.table, bf16[256,256]{1,0:T(8,128)(2,1)S(1)} %get-tuple-element.79.second, bf16[16,256]{1,0:T(8,128)(2,1)S(1)} %collective-permute-done.9.rest_0_, ...), custom_call_target="tpu_custom_call" | custom-call | flops 33554432 | bytes 323584 | tf_op jit(solution)/shard_map/pallas_call | solution.py:193
  (7 shorter events, 0.0 us)
Async XLA Ops:
  0.6 10.5 %copy-start = (bf16[768,256]{1,0:T(8,128)(2,1)S(1)}, bf16[768,256]{1,0:T(8,128)(2,1)}, u32[]{:S(2)}) copy-start(bf16[768,256]{1,0:T(8,128)(2,1)} %edge_first.3) | copy-start | bytes 1179652
  0.6 10.5 %copy-start.1 = (bf16[256,256]{1,0:T(8,128)(2,1)S(1)}, bf16[256,256]{1,0:T(8,128)(2,1)}, u32[]{:S(2)}) copy-start(bf16[256,256]{1,0:T(8,128)(2,1)} %edge_second.3) | copy-start | bytes 393220
  0.7 10.5 %copy-start.6 = (bf16[1,384,256]{2,1,0:T(8,128)(2,1)S(1)}, bf16[1,384,256]{2,1,0:T(8,128)(2,1)}, u32[]{:S(2)}) copy-start(bf16[1,384,256]{2,1,0:T(8,128)(2,1)} %param.18) | copy-start | bytes 589828
  1.8 11.1 %collective-permute-start = (bf16[16,256]{1,0:T(8,128)(2,1)S(1)}, bf16[16,256]{1,0:T(8,128)(2,1)S(1)}, u32[]{:S(2)}, u32[]{:S(2)}) collective-permute-start(bf16[16,256]{1,0:T(8,128)(2,1)S(1)} %get-tuple-element.57), channel_id=1, source_target_pairs={{0,4},{1,5},{2,6},{3,7},{4,0},{5,1},{6,2},{7,3},{8,12},{9,13},{10,... | collective-permute-start | bytes 24584 | tf_op jit(solution)/shard_map/ppermute | solution.py:22
  5.9 7.0 %collective-permute-start.1 = (bf16[16,256]{1,0:T(8,128)(2,1)S(1)}, bf16[16,256]{1,0:T(8,128)(2,1)S(1)}, u32[]{:S(2)}, u32[]{:S(2)}) collective-permute-start(bf16[16,256]{1,0:T(8,128)(2,1)S(1)} %get-tuple-element.58), channel_id=1, source_target_pairs={{0,2},{1,3},{2,0},{3,1},{4,6},{5,7},{6,4},{7,5},{8,10},{9,11},{10,... | collective-permute-start | bytes 24584 | tf_op jit(solution)/shard_map/ppermute | solution.py:22
  7.5 5.5 %collective-permute-start.2 = (bf16[16,256]{1,0:T(8,128)(2,1)S(1)}, bf16[16,256]{1,0:T(8,128)(2,1)S(1)}, u32[]{:S(2)}, u32[]{:S(2)}) collective-permute-start(bf16[16,256]{1,0:T(8,128)(2,1)S(1)} %get-tuple-element.59), channel_id=1, source_target_pairs={{0,1},{1,0},{2,3},{3,2},{4,5},{5,4},{6,7},{7,6},{8,9},{9,8},{10,11... | collective-permute-start | bytes 24584 | tf_op jit(solution)/shard_map/ppermute | solution.py:22
  9.0 4.0 %collective-permute-start.3 = (bf16[16,256]{1,0:T(8,128)(2,1)S(1)}, bf16[16,256]{1,0:T(8,128)(2,1)S(1)}, u32[]{:S(2)}, u32[]{:S(2)}) collective-permute-start(bf16[16,256]{1,0:T(8,128)(2,1)S(1)} %get-tuple-element.60), channel_id=1, source_target_pairs={{0,16},{8,24},{16,0},{24,8},{1,17},{9,25},{17,1},{25,9},{2,18},{10... | collective-permute-start | bytes 24584 | tf_op jit(solution)/shard_map/ppermute | solution.py:22
  10.5 2.5 %collective-permute-start.4 = (bf16[16,256]{1,0:T(8,128)(2,1)S(1)}, bf16[16,256]{1,0:T(8,128)(2,1)S(1)}, u32[]{:S(2)}, u32[]{:S(2)}) collective-permute-start(bf16[16,256]{1,0:T(8,128)(2,1)S(1)} %get-tuple-element.61), channel_id=1, source_target_pairs={{0,8},{8,0},{16,24},{24,16},{1,9},{9,1},{17,25},{25,17},{2,10},{10... | collective-permute-start | bytes 24584 | tf_op jit(solution)/shard_map/ppermute | solution.py:22
  11.2 1.8 %copy-start.2 = (bf16[512,256]{1,0:T(8,128)(2,1)S(1)}, bf16[512,256]{1,0:T(8,128)(2,1)}, u32[]{:S(2)}) copy-start(bf16[512,256]{1,0:T(8,128)(2,1)} %node_first.1) | copy-start | bytes 786436
  11.2 1.8 %copy-start.3 = (bf16[1,5,64,256]{3,2,1,0:T(8,128)(2,1)S(1)}, bf16[1,5,64,256]{3,2,1,0:T(8,128)(2,1)}, u32[]{:S(2)}) copy-start(bf16[1,5,64,256]{3,2,1,0:T(8,128)(2,1)} %param.19) | copy-start | bytes 491524
  11.2 1.8 %copy-start.4 = (bf16[256,256]{1,0:T(8,128)(2,1)S(1)}, bf16[256,256]{1,0:T(8,128)(2,1)}, u32[]{:S(2)}) copy-start(bf16[256,256]{1,0:T(8,128)(2,1)} %node_second.1) | copy-start | bytes 393220
  11.2 1.8 %copy-start.5 = (bf16[1,128,256]{2,1,0:T(8,128)(2,1)S(1)}, bf16[1,128,256]{2,1,0:T(8,128)(2,1)}, u32[]{:S(2)}) copy-start(bf16[1,128,256]{2,1,0:T(8,128)(2,1)} %param.20) | copy-start | bytes 196612
  15.3 4.6 %collective-permute-start.5 = (bf16[16,256]{1,0:T(8,128)(2,1)S(1)}, bf16[16,256]{1,0:T(8,128)(2,1)S(1)}, u32[]{:S(2)}, u32[]{:S(2)}) collective-permute-start(bf16[16,256]{1,0:T(8,128)(2,1)S(1)} %get-tuple-element.80), channel_id=1, source_target_pairs={{0,4},{1,5},{2,6},{3,7},{4,0},{5,1},{6,2},{7,3},{8,12},{9,13},{10,... | collective-permute-start | bytes 24584 | tf_op jit(solution)/shard_map/ppermute | solution.py:22
  15.7 4.2 %collective-permute-start.6 = (bf16[16,256]{1,0:T(8,128)(2,1)S(1)}, bf16[16,256]{1,0:T(8,128)(2,1)S(1)}, u32[]{:S(2)}, u32[]{:S(2)}) collective-permute-start(bf16[16,256]{1,0:T(8,128)(2,1)S(1)} %get-tuple-element.81), channel_id=1, source_target_pairs={{0,2},{1,3},{2,0},{3,1},{4,6},{5,7},{6,4},{7,5},{8,10},{9,11},{10,... | collective-permute-start | bytes 24584 | tf_op jit(solution)/shard_map/ppermute | solution.py:22
  16.2 3.8 %collective-permute-start.7 = (bf16[16,256]{1,0:T(8,128)(2,1)S(1)}, bf16[16,256]{1,0:T(8,128)(2,1)S(1)}, u32[]{:S(2)}, u32[]{:S(2)}) collective-permute-start(bf16[16,256]{1,0:T(8,128)(2,1)S(1)} %get-tuple-element.82), channel_id=1, source_target_pairs={{0,1},{1,0},{2,3},{3,2},{4,5},{5,4},{6,7},{7,6},{8,9},{9,8},{10,11... | collective-permute-start | bytes 24584 | tf_op jit(solution)/shard_map/ppermute | solution.py:22
  16.7 3.7 %collective-permute-start.8 = (bf16[16,256]{1,0:T(8,128)(2,1)S(1)}, bf16[16,256]{1,0:T(8,128)(2,1)S(1)}, u32[]{:S(2)}, u32[]{:S(2)}) collective-permute-start(bf16[16,256]{1,0:T(8,128)(2,1)S(1)} %get-tuple-element.83), channel_id=1, source_target_pairs={{0,16},{8,24},{16,0},{24,8},{1,17},{9,25},{17,1},{25,9},{2,18},{10... | collective-permute-start | bytes 24584 | tf_op jit(solution)/shard_map/ppermute | solution.py:22
  17.8 2.5 %collective-permute-start.9 = (bf16[16,256]{1,0:T(8,128)(2,1)S(1)}, bf16[16,256]{1,0:T(8,128)(2,1)S(1)}, u32[]{:S(2)}, u32[]{:S(2)}) collective-permute-start(bf16[16,256]{1,0:T(8,128)(2,1)S(1)} %get-tuple-element.84), channel_id=1, source_target_pairs={{0,8},{8,0},{16,24},{24,16},{1,9},{9,1},{17,25},{25,17},{2,10},{10... | collective-permute-start | bytes 24584 | tf_op jit(solution)/shard_map/ppermute | solution.py:22

commit v5 on v4

v5 whole, which is shorter than its diff:
```python
import functools

import jax
import jax.numpy as jnp
from jax import lax
from jax.experimental import pallas as pl
from jax.experimental.pallas import tpu as pltpu
from jax.sharding import PartitionSpec as P

ROUNDS = 5
GRP_ROUNDS = 2
LONG = 4 * 10**9

epsilon = 1e-05

bf16 = jnp.bfloat16
f32 = jnp.float32


def partner(shard, round_index):
    axis, apart = ("grp", round_index) if round_index < GRP_ROUNDS else ("dev", round_index - GRP_ROUNDS)
    return lax.ppermute(shard, axis, [(i, i ^ 1 << apart) for i in range(lax.axis_size(axis))])


def exchange(rows):
    got = lax.optimization_barrier([partner(rows[r], r) for r in reversed(range(ROUNDS))])
    return got[::-1]


def mm(a, b):
    return jnp.dot(a, b, preferred_element_type=f32)


def mm_t(a, b):
    return lax.dot_general(a, b, (((1,), (1,)), ((), ())), preferred_element_type=f32)


def hot(row, count):
    shape = (count, row.shape[1])
    return (lax.broadcasted_iota(jnp.int32, shape, 0) == jnp.broadcast_to(row, shape)).astype(f32)


def split(values):
    high = values.astype(bf16)
    return high, (values - high.astype(f32)).astype(bf16)


def add_rows(table, values):
    return mm(jnp.concatenate([table, table], 1), jnp.concatenate(split(values), 0))


def lane_mean(values):
    return jnp.mean(values, axis=-1, keepdims=True)


def norm_parts(values):
    centred = values - lane_mean(values)
    inverse = lax.rsqrt(lane_mean(centred * centred) + epsilon)
    return centred * inverse, inverse


def norm_backward(scaled, normed, inverse):
    return inverse * (scaled - lane_mean(scaled) - normed * lane_mean(scaled * normed))


def silu_parts(values):
    sigmoid = jax.nn.sigmoid(values)
    act = values * sigmoid
    return act, sigmoid + act * (1.0 - sigmoid)


def load(held, loaded, done):
    copies = [pltpu.make_async_copy(h, v, done.at[i]) for i, (h, v) in enumerate(zip(held, loaded))]
    for copy in copies:
        copy.start()
    return copies


def send_kernel(count, *rest):
    held, loaded, out, done = rest[:count], rest[count : 2 * count], rest[2 * count : -1], rest[-1]
    copies = load(held, loaded, done)
    boundary, nodes = loaded[:2]
    copies[0].wait()
    table = jnp.concatenate([hot(boundary[r], nodes.shape[0]) for r in range(ROUNDS)], 1).T.astype(bf16)
    copies[1].wait()
    rows = mm(table, nodes[...]).astype(bf16)
    send = boundary.shape[2]
    for r in range(ROUNDS):
        out[r][...] = rows[r * send : (r + 1) * send]
    for copy in copies[2:]:
        copy.wait()


def inner_kernel(
    edge_count, nodes, edges, cuts, sender, receiver, slot, cut_receiver, boundary, edge_first, edge_second,
    gather_out, normed_out, inverse_out, slope_out, received, near, gather_cut, gather_far,
    scatter_receive, scatter_send, scatter_cut, scatter_far, scatter_boundary, first_t, second_t,
):
    n, width = nodes.shape
    e = edges.shape[0]
    used = lax.broadcasted_iota(jnp.int32, (1, e), 1) < edge_count[0]
    hot_receive = hot(jnp.where(used, receiver[...], -1), n)
    hot_send = hot(sender[...], n)
    gather = jnp.concatenate([hot_receive, hot_send], 0).T.astype(bf16)
    first = mm(nodes[...], edge_first[:width])
    second = mm(nodes[...], edge_first[width : 2 * width])
    pre = add_rows(gather, jnp.concatenate([first, second], 0)) + mm(edges[...], edge_first[2 * width :])
    act, slope = silu_parts(pre)
    normed, inverse = norm_parts(mm(act.astype(bf16), edge_second[...]))
    gather_out[...] = gather[:, :n]
    normed_out[...] = normed
    inverse_out[...] = inverse
    slope_out[...] = slope
    received[...] = add_rows(hot_receive.astype(bf16), normed)
    scatter_receive[...] = hot_receive.astype(bf16)
    scatter_send[...] = hot_send.astype(bf16)

    send = boundary.shape[2]
    hot_cut = jnp.concatenate([hot(cut_receiver[r], n) for r in range(ROUNDS)], 1)
    hot_far = hot(jnp.concatenate([slot[r] + r * send for r in range(ROUNDS)], 1), gather_far.shape[1])
    at_cut = hot_cut.T.astype(bf16)
    near[...] = add_rows(at_cut, first) + mm(cuts[...], edge_first[2 * width :])
    gather_cut[...] = at_cut
    gather_far[...] = hot_far.T.astype(bf16)
    scatter_cut[...] = hot_cut.astype(bf16)
    scatter_far[...] = hot_far[: scatter_far.shape[0]].astype(bf16)
    scatter_boundary[...] = jnp.concatenate([hot(boundary[r], n) for r in range(ROUNDS)], 1).astype(bf16)
    first_t[...] = edge_first[...].T
    second_t[...] = edge_second[...].T


def main_kernel(
    nodes, cotangent, edge_first, edge_second, edge_gain, node_first, node_second, node_gain, received_inner, near,
    gather_cut, gather_far, scatter_cut, scatter_far, second_t, *rest,
):
    arrived = rest[:ROUNDS]
    updated, base, gained, grad_cut = rest[ROUNDS : ROUNDS + 4]
    back = rest[ROUNDS + 4 :]
    n, width = nodes.shape
    send = arrived[0].shape[0]
    x = nodes[...]
    empty = jnp.zeros((gather_far.shape[1] - ROUNDS * send, width), bf16)
    far = jnp.concatenate([a[...] for a in arrived] + [empty], 0)
    pre = near[...] + add_rows(gather_far[...], mm(far, edge_first[width : 2 * width]))
    act, slope = silu_parts(pre)
    normed, inverse = norm_parts(mm(act.astype(bf16), edge_second[...]))
    received = (received_inner[...] + add_rows(scatter_cut[...], normed)) * edge_gain[...]

    pre_node = mm(jnp.concatenate([x, received.astype(bf16)], 1), node_first[...])
    act_node, slope_node = silu_parts(pre_node)
    normed_node, inverse_node = norm_parts(mm(act_node.astype(bf16), node_second[...]))
    updated[...] = (x.astype(f32) + normed_node * node_gain[...]).astype(bf16)
    upstream = cotangent[...].astype(f32)
    grad_out_node = norm_backward(upstream * node_gain[...], normed_node, inverse_node).astype(bf16)
    grad_pre_node = (mm_t(grad_out_node, node_second[...]) * slope_node).astype(bf16)
    at_receiver = mm_t(grad_pre_node, node_first[width:]) * edge_gain[...]
    parts = jnp.concatenate(split(at_receiver), 0)
    twice = jnp.concatenate([gather_cut[...], gather_cut[...]], 1)
    grad_out = norm_backward(mm(twice, parts), normed, inverse).astype(bf16)
    grad = (mm(grad_out, second_t[...]) * slope).astype(bf16)
    sums = mm(scatter_far[...], grad).astype(bf16)
    for r in range(ROUNDS):
        back[r][...] = sums[r * send : (r + 1) * send]
    grad_cut[...] = grad
    gained[...] = parts
    base[...] = upstream + mm_t(grad_pre_node, node_first[:width])


def outer_kernel(
    node_count, gained, gather, normed, inverse, slope, first_t, second_t, scatter_receive, scatter_send, scatter_cut,
    grad_cut, base, updated_in, updated, edge_gradient, cut_gradient, total,
):
    n, width = base.shape
    valid = lax.broadcasted_iota(jnp.int32, (n, width), 0) < node_count[0]
    updated[...] = jnp.where(valid, updated_in[...].astype(f32), 0.0).astype(bf16)
    cut = grad_cut[...]
    cut_gradient[...] = mm(cut, first_t[:, 2 * width :]).astype(bf16)
    twice = jnp.concatenate([gather[...], gather[...]], 1)
    grad_out = norm_backward(mm(twice, gained[...]), normed[...], inverse[...]).astype(bf16)
    grad = (mm(grad_out, second_t[...]) * slope[...]).astype(bf16)
    edge_gradient[...] = mm(grad, first_t[:, 2 * width :]).astype(bf16)
    at_receiver = mm(scatter_receive[...], grad) + mm(scatter_cut[...], cut)
    at_sender = mm(scatter_send[...], grad)
    total[...] = (
        jnp.where(valid, base[...], 0.0)
        + mm(at_receiver.astype(bf16), first_t[:, :width])
        + mm(at_sender.astype(bf16), first_t[:, width : 2 * width])
    )


def last_kernel(total, scatter_boundary, first_t, updated, edge_gradient, cut_gradient, *rest):
    arrived, outs, here, done = rest[:ROUNDS], rest[ROUNDS : ROUNDS + 4], *rest[ROUNDS + 4 :]
    held = (updated, edge_gradient, cut_gradient, here)
    copies = [pltpu.make_async_copy(a, b, done.at[i]) for i, (a, b) in enumerate(zip(held, outs))]
    for copy in copies[:3]:
        copy.start()
    width = total.shape[1]
    at_sender = mm(scatter_boundary[...], jnp.concatenate([a[...] for a in arrived], 0)).astype(bf16)
    here[...] = (total[...] + mm(at_sender, first_t[:, width : 2 * width])).astype(bf16)
    copies[3].start()
    for copy in copies:
        copy.wait()


VMEM = pl.BlockSpec(memory_space=pltpu.VMEM)
HBM = pl.BlockSpec(memory_space=pltpu.HBM)
SMEM = pl.BlockSpec(memory_space=pltpu.SMEM)


def call(kernel, out_shape, args, flops, held=(), scratch=(), written=0):
    size = sum(a.size * a.dtype.itemsize for a in args + tuple(held))
    return pl.pallas_call(
        kernel,
        out_shape=out_shape,
        in_specs=[SMEM if a.ndim == 1 else VMEM for a in args] + [HBM] * len(held),
        out_specs=[VMEM if i >= written else HBM for i in range(len(out_shape))],
        scratch_shapes=scratch,
        compiler_params=pltpu.CompilerParams(vmem_limit_bytes=32 * 1024 * 1024),
        cost_estimate=pl.CostEstimate(flops=flops, bytes_accessed=size if flops else 0, transcendentals=0),
    )(*args, *(pltpu.with_memory_space_constraint(a, pltpu.HBM) for a in held))


def shards(
    node_latent, edge_latent, cut_latent, node_cotangent, edge_sender, edge_receiver, boundary_rows,
    cut_slot, cut_receiver, node_count, edge_count, edge_first, edge_second, edge_gain, node_first,
    node_second, node_gain,
):
    nodes = node_latent[0]
    edges = edge_latent[0]
    cuts = cut_latent[0].reshape(-1, cut_latent.shape[-1])
    n, width = nodes.shape
    e, c = edges.shape[0], cuts.shape[0]
    boundary = boundary_rows.transpose(1, 0, 2)
    slot = cut_slot.transpose(1, 0, 2)
    cut_targets = cut_receiver.transpose(1, 0, 2)
    send = boundary.shape[2]
    shape = jax.ShapeDtypeStruct
    kept = pltpu.VMEM

    def copies(arrays):
        return [kept(a.shape, a.dtype) for a in arrays]

    held = (boundary, nodes, edge_receiver, edge_sender, slot, cut_targets, edge_gain[None], node_gain[None])
    outs = call(
        functools.partial(send_kernel, len(held)),
        copies(held) + [kept((send, width), bf16)] * ROUNDS,
        (),
        LONG,
        held,
        [pltpu.SemaphoreType.DMA((len(held),))],
    )
    boundary, nodes, edge_receiver, edge_sender, slot, cut_targets, edge_gain, node_gain = outs[: len(held)]
    sent = outs[len(held) :]
    arrived = exchange(sent)
    slots = ROUNDS * send
    some = -(-slots // 32) * 32
    all_slots = -(-slots // 128) * 128
    outs = call(
        inner_kernel,
        [
            kept((e, n), bf16), kept((e, width), f32), kept((e, 1), f32), kept((e, width), f32),
            kept((n, width), f32), kept((c, width), f32), kept((c, n), bf16), kept((c, all_slots), bf16),
            kept((n, e), bf16), kept((n, e), bf16), kept((n, c), bf16), kept((some, c), bf16),
            kept((n, slots), bf16), kept((width, 3 * width), bf16), kept((width, width), bf16),
        ],
        (
            edge_count, nodes, edges, cuts, edge_sender, edge_receiver, slot, cut_targets, boundary, edge_first,
            edge_second,
        ),
        LONG,
    )
    gather, normed, inverse, slope, received, near, gather_cut, gather_far = outs[:8]
    scatter_receive, scatter_send, scatter_cut, scatter_far, scatter_boundary, first_t, second_t = outs[8:]
    outs = call(
        main_kernel,
        [kept((n, width), bf16), kept((n, width), f32), kept((2 * n, width), bf16), kept((c, width), bf16)]
        + [kept((send, width), bf16)] * ROUNDS,
        (
            nodes, node_cotangent[0], edge_first, edge_second, edge_gain, node_first, node_second, node_gain,
            received, near, gather_cut, gather_far, scatter_cut, scatter_far, second_t, *arrived,
        ),
        2 * c * width * width * 6,
    )
    updated, base, gained, grad_cut = outs[:4]
    returned = exchange(outs[4:])
    updated, edge_gradient, cut_gradient, total = call(
        outer_kernel,
        [kept((n, width), bf16), kept((e, width), bf16), kept((c, width), bf16), kept((n, width), f32)],
        (
            node_count, gained, gather, normed, inverse, slope, first_t, second_t, scatter_receive, scatter_send,
            scatter_cut, grad_cut, base, updated,
        ),
        0,
    )
    updated, edge_gradient, cut_gradient, node_gradient = call(
        last_kernel,
        [shape((n, width), bf16), shape((e, width), bf16), shape((c, width), bf16), shape((n, width), bf16)],
        (total, scatter_boundary, first_t, updated, edge_gradient, cut_gradient, *returned),
        2 * 2 * n * width * width,
        scratch=[pltpu.VMEM((n, width), bf16), pltpu.SemaphoreType.DMA((4,))],
        written=4,
    )
    return (
        updated[None],
        node_gradient[None],
        edge_gradient[None],
        cut_gradient.reshape(cut_latent.shape),
    )


def solution(mesh):
    part = ("grp", "dev")
    placed = tuple(P(part, *[None] * (d - 1)) for d in (3, 3, 4, 3, 2, 2, 3, 3, 3, 1, 1)) + (P(),) * 6
    return jax.shard_map(
        shards,
        mesh=mesh,
        in_specs=placed,
        out_specs=tuple(P(part, *[None] * (d - 1)) for d in (3, 3, 3, 4)),
        check_vma=False,
    )
```

time: 21.4 us -> 20.9 us (0.977)
  Pallas kernels: 6.94 us -> 6.47 us
  starting transfers between devices: 11.2 us -> 11.5 us
  waiting for transfers between devices: 0.92 us -> 0.63 us
    pallas_call x5, Pallas kernels: 6.94 us -> 6.47 us  [call(): pl.pallas_call(kernel, out_shape=out_shape, in_specs=[SMEM if a.ndim == 1...]
    ppermute x10, starting transfers between devices: 11.2 us -> 11.5 us  [partner(): lax.ppermute(shard, axis, [(i, i ^ 1 << apart) for i in range(lax.axis_si...]
    ppermute x10, waiting for transfers between devices: 0.92 us -> 0.63 us  [partner(): lax.ppermute(shard, axis, [(i, i ^ 1 << apart) for i in range(lax.axis_si...]
  transfers between devices with their start and end apart: 10 -> 10, of which waited for: 2 -> 3; matrix products, arithmetic and copies ran while one was open for 0% -> 0% of each run, Pallas kernels for 12% -> 10%
where the time goes in v5:
time: 20.9 us; the launch traced here: 20.8 us
  starting transfers between devices  11.5 us (55%)
  Pallas kernels  6.47 us (31%)
  between operations  2.1 us (10%)
  waiting for transfers between devices  0.63 us (3%)
    ppermute x10, starting transfers between devices, partner(): lax.ppermute(shard, axis, [(i, i ^ 1 << apart) for i in range(lax.axis_si...  11.5 us
    pallas_call x5, Pallas kernels, call(): pl.pallas_call(kernel, out_shape=out_shape, in_specs=[SMEM if a.ndim == 1...  6.47 us
    ppermute x10, waiting for transfers between devices, partner(): lax.ppermute(shard, axis, [(i, i ^ 1 << apart) for i in range(lax.axis_si...  0.63 us
  transfers between devices with their start and end apart: 10, of which 3 were waited for; matrix products, arithmetic and copies ran while one was open for 0% of the time, Pallas kernels for 10%

profile of v5, /device:TPU:0, one launch (start us, length us, event | category | flops | bytes accessed | tf_op | source)
XLA Modules:
  0.0 20.8 jit_solution(10923374472815144667)
XLA Ops:
  0.6 0.0 copy-start
  0.6 0.0 copy-start.2
  0.7 0.0 copy-start.5
  0.7 1.2 %shard_map.192 = (s32[5,1,16]{2,1,0:T(1,128)S(1)}, bf16[128,256]{1,0:T(8,128)(2,1)S(1)}, s32[1,384]{1,0:T(1,128)S(1)}, s32[1,384]{1,0:T(1,128)S(1)}, s32[5,1,64]...) custom-call(s32[5,1,16]{2,1,0:T(1,128)} %bitcast.21, ...), custom_call_target="tpu_custom_call" | custom-call | flops 4000000000 | bytes 73536 | tf_op jit(solution)/shard_map/pallas_call | solution.py:212
  1.8 4.1 %collective-permute-start = (bf16[16,256]{1,0:T(8,128)(2,1)S(1)}, bf16[16,256]{1,0:T(8,128)(2,1)S(1)}, u32[]{:S(2)}, u32[]{:S(2)}) collective-permute-start(bf16[16,256]{1,0:T(8,128)(2,1)S(1)} %get-tuple-element.74), channel_id=1, source_target_pairs={{0,4},{1,5},{2,6},{3,7},{4,0},{5,1},{6,2},{7,3},{8,12},{9,13},{10,... | collective-permute-start | bytes 24584 | tf_op jit(solution)/shard_map/ppermute | solution.py:22
  5.9 1.6 %collective-permute-start.1 = (bf16[16,256]{1,0:T(8,128)(2,1)S(1)}, bf16[16,256]{1,0:T(8,128)(2,1)S(1)}, u32[]{:S(2)}, u32[]{:S(2)}) collective-permute-start(bf16[16,256]{1,0:T(8,128)(2,1)S(1)} %get-tuple-element.75), channel_id=1, source_target_pairs={{0,2},{1,3},{2,0},{3,1},{4,6},{5,7},{6,4},{7,5},{8,10},{9,11},{10,... | collective-permute-start | bytes 24584 | tf_op jit(solution)/shard_map/ppermute | solution.py:22
  7.5 1.5 %collective-permute-start.2 = (bf16[16,256]{1,0:T(8,128)(2,1)S(1)}, bf16[16,256]{1,0:T(8,128)(2,1)S(1)}, u32[]{:S(2)}, u32[]{:S(2)}) collective-permute-start(bf16[16,256]{1,0:T(8,128)(2,1)S(1)} %get-tuple-element.76), channel_id=1, source_target_pairs={{0,1},{1,0},{2,3},{3,2},{4,5},{5,4},{6,7},{7,6},{8,9},{9,8},{10,11... | collective-permute-start | bytes 24584 | tf_op jit(solution)/shard_map/ppermute | solution.py:22
  9.0 1.5 %collective-permute-start.3 = (bf16[16,256]{1,0:T(8,128)(2,1)S(1)}, bf16[16,256]{1,0:T(8,128)(2,1)S(1)}, u32[]{:S(2)}, u32[]{:S(2)}) collective-permute-start(bf16[16,256]{1,0:T(8,128)(2,1)S(1)} %get-tuple-element.77), channel_id=1, source_target_pairs={{0,16},{8,24},{16,0},{24,8},{1,17},{9,25},{17,1},{25,9},{2,18},{10... | collective-permute-start | bytes 24584 | tf_op jit(solution)/shard_map/ppermute | solution.py:22
  10.5 0.0 collective-permute-start.4
  11.2 0.0 copy-start.1
  11.2 0.0 copy-start.3
  11.2 0.0 copy-start.4
  11.3 1.2 %shard_map.193 = (bf16[384,128]{1,0:T(8,128)(2,1)S(1)}, f32[384,256]{1,0:T(8,128)S(1)}, f32[384,1]{1,0:T(8,128)S(1)}, f32[384,256]{1,0:T(8,128)S(1)}, f32[128,25...) custom-call(s32[1]{0:T(128)S(6)} %copy.22.edge_count, ...), custom_call_target="tpu_custom_call" | custom-call | flops 4000000000 | bytes 956228 | tf_op jit(solution)/shard_map/pallas_call | solution.py:212
  12.5 0.0 collective-permute-done.rest_4_
  12.5 0.0 collective-permute-done.1.rest_3_
  12.5 0.0 collective-permute-done.2.rest_2_
  12.5 0.2 collective-permute-done.3.rest_1_
  12.7 0.0 collective-permute-done.4.rest_0_
  12.7 0.0 copy-done.3
  12.7 2.2 %shard_map.194 = (bf16[128,256]{1,0:T(8,128)(2,1)S(1)}, f32[128,256]{1,0:T(8,128)S(1)}, bf16[256,256]{1,0:T(8,128)(2,1)S(1)}, bf16[320,256]{1,0:T(8,128)(2,1)S(1...) custom-call(bf16[128,256]{1,0:T(8,128)(2,1)S(1)} %get-tuple-element., ...), custom_call_target="tpu_custom_call" | custom-call | flops 251658240 | bytes 1988608 | tf_op jit(solution)/shard_map/pallas_call | solution.py:212
  14.9 0.4 %collective-permute-start.5 = (bf16[16,256]{1,0:T(8,128)(2,1)S(1)}, bf16[16,256]{1,0:T(8,128)(2,1)S(1)}, u32[]{:S(2)}, u32[]{:S(2)}) collective-permute-start(bf16[16,256]{1,0:T(8,128)(2,1)S(1)} %get-tuple-element.100), channel_id=1, source_target_pairs={{0,4},{1,5},{2,6},{3,7},{4,0},{5,1},{6,2},{7,3},{8,12},{9,13},{10,... | collective-permute-start | bytes 24584 | tf_op jit(solution)/shard_map/ppermute | solution.py:22
  15.4 0.4 %collective-permute-start.6 = (bf16[16,256]{1,0:T(8,128)(2,1)S(1)}, bf16[16,256]{1,0:T(8,128)(2,1)S(1)}, u32[]{:S(2)}, u32[]{:S(2)}) collective-permute-start(bf16[16,256]{1,0:T(8,128)(2,1)S(1)} %get-tuple-element.101), channel_id=1, source_target_pairs={{0,2},{1,3},{2,0},{3,1},{4,6},{5,7},{6,4},{7,5},{8,10},{9,11},{10,... | collective-permute-start | bytes 24584 | tf_op jit(solution)/shard_map/ppermute | solution.py:22
  15.8 0.4 %collective-permute-start.7 = (bf16[16,256]{1,0:T(8,128)(2,1)S(1)}, bf16[16,256]{1,0:T(8,128)(2,1)S(1)}, u32[]{:S(2)}, u32[]{:S(2)}) collective-permute-start(bf16[16,256]{1,0:T(8,128)(2,1)S(1)} %get-tuple-element.102), channel_id=1, source_target_pairs={{0,1},{1,0},{2,3},{3,2},{4,5},{5,4},{6,7},{7,6},{8,9},{9,8},{10,11... | collective-permute-start | bytes 24584 | tf_op jit(solution)/shard_map/ppermute | solution.py:22
  16.2 1.6 %collective-permute-start.8 = (bf16[16,256]{1,0:T(8,128)(2,1)S(1)}, bf16[16,256]{1,0:T(8,128)(2,1)S(1)}, u32[]{:S(2)}, u32[]{:S(2)}) collective-permute-start(bf16[16,256]{1,0:T(8,128)(2,1)S(1)} %get-tuple-element.103), channel_id=1, source_target_pairs={{0,16},{8,24},{16,0},{24,8},{1,17},{9,25},{17,1},{25,9},{2,18},{10... | collective-permute-start | bytes 24584 | tf_op jit(solution)/shard_map/ppermute | solution.py:22
  17.8 0.0 collective-permute-start.9
  18.4 0.9 %shard_map.195 = (bf16[128,256]{1,0:T(8,128)(2,1)S(1)}, bf16[384,256]{1,0:T(8,128)(2,1)S(1)}, bf16[320,256]{1,0:T(8,128)(2,1)S(1)}, f32[128,256]{1,0:T(8,128)S(1)}) custom-call(s32[1]{0:T(128)S(6)} %copy.21.node_count, bf16[256,256]{1,0:T(8,128)(2,1)S(1)} %get-tuple-element.84.gained, bf16[384,128]{1,0:T(8,128)(2,1)S(1)} %get-tuple-element.85.gather, ...), custom_call_target="tpu_custom_call" | custom-call | tf_op jit(solution)/shard_map/pallas_call | solution.py:212
  19.4 0.2 %collective-permute-done.5.rest_4_ = bf16[16,256]{1,0:T(8,128)(2,1)S(1)} collective-permute-done((bf16[16,256]{1,0:T(8,128)(2,1)S(1)}, bf16[16,256]{1,0:T(8,128)(2,1)S(1)}, u32[]{:S(2)}, u32[]{:S(2)}) %collective-permute-start.5) | collective-permute-done | bytes 8224 | tf_op jit(solution)/shard_map/ppermute | solution.py:22
  19.6 0.0 collective-permute-done.6.rest_3_
  19.6 0.0 collective-permute-done.7.rest_2_
  19.6 0.2 %collective-permute-done.8.rest_1_ = bf16[16,256]{1,0:T(8,128)(2,1)S(1)} collective-permute-done((bf16[16,256]{1,0:T(8,128)(2,1)S(1)}, bf16[16,256]{1,0:T(8,128)(2,1)S(1)}, u32[]{:S(2)}, u32[]{:S(2)}) %collective-permute-start.8) | collective-permute-done | bytes 8224 | tf_op jit(solution)/shard_map/ppermute | solution.py:22
  19.8 0.0 collective-permute-done.9.rest_0_
  19.8 1.0 %shard_map.196 = (bf16[128,256]{1,0:T(8,128)(2,1)}, bf16[384,256]{1,0:T(8,128)(2,1)}, bf16[320,256]{1,0:T(8,128)(2,1)}, bf16[128,256]{1,0:T(8,128)(2,1)}) custom-call(f32[128,256]{1,0:T(8,128)S(1)} %get-tuple-element.95.total, bf16[128,80]{1,0:T(8,128)(2,1)S(1)} %get-tuple-element.96.scatter_boundary, bf16[256,768]{1,0:T(8,128)(2,1)S(1)} %get-tuple-element.89.first_t, ...), custom_call_target="tpu_custom_call" | custom-call | flops 33554432 | bytes 1011712 | tf_op jit(solution)/shard_map/pallas_call | solution.py:212
  (7 shorter events, 0.0 us)
Async XLA Ops:
  0.6 10.6 %copy-start = (bf16[768,256]{1,0:T(8,128)(2,1)S(1)}, bf16[768,256]{1,0:T(8,128)(2,1)}, u32[]{:S(2)}) copy-start(bf16[768,256]{1,0:T(8,128)(2,1)} %edge_first.3) | copy-start | bytes 1179652
  0.6 10.6 %copy-start.2 = (bf16[256,256]{1,0:T(8,128)(2,1)S(1)}, bf16[256,256]{1,0:T(8,128)(2,1)}, u32[]{:S(2)}) copy-start(bf16[256,256]{1,0:T(8,128)(2,1)} %edge_second.3) | copy-start | bytes 393220
  0.7 10.6 %copy-start.5 = (bf16[1,384,256]{2,1,0:T(8,128)(2,1)S(1)}, bf16[1,384,256]{2,1,0:T(8,128)(2,1)}, u32[]{:S(2)}) copy-start(bf16[1,384,256]{2,1,0:T(8,128)(2,1)} %param.18) | copy-start | bytes 589828
  0.7 10.6 %copy-start.6 = (bf16[1,5,64,256]{3,2,1,0:T(8,128)(2,1)S(1)}, bf16[1,5,64,256]{3,2,1,0:T(8,128)(2,1)}, u32[]{:S(2)}) copy-start(bf16[1,5,64,256]{3,2,1,0:T(8,128)(2,1)} %param.19) | copy-start | bytes 491524
  1.8 10.7 %collective-permute-start = (bf16[16,256]{1,0:T(8,128)(2,1)S(1)}, bf16[16,256]{1,0:T(8,128)(2,1)S(1)}, u32[]{:S(2)}, u32[]{:S(2)}) collective-permute-start(bf16[16,256]{1,0:T(8,128)(2,1)S(1)} %get-tuple-element.74), channel_id=1, source_target_pairs={{0,4},{1,5},{2,6},{3,7},{4,0},{5,1},{6,2},{7,3},{8,12},{9,13},{10,... | collective-permute-start | bytes 24584 | tf_op jit(solution)/shard_map/ppermute | solution.py:22
  5.9 6.6 %collective-permute-start.1 = (bf16[16,256]{1,0:T(8,128)(2,1)S(1)}, bf16[16,256]{1,0:T(8,128)(2,1)S(1)}, u32[]{:S(2)}, u32[]{:S(2)}) collective-permute-start(bf16[16,256]{1,0:T(8,128)(2,1)S(1)} %get-tuple-element.75), channel_id=1, source_target_pairs={{0,2},{1,3},{2,0},{3,1},{4,6},{5,7},{6,4},{7,5},{8,10},{9,11},{10,... | collective-permute-start | bytes 24584 | tf_op jit(solution)/shard_map/ppermute | solution.py:22
  7.5 5.0 %collective-permute-start.2 = (bf16[16,256]{1,0:T(8,128)(2,1)S(1)}, bf16[16,256]{1,0:T(8,128)(2,1)S(1)}, u32[]{:S(2)}, u32[]{:S(2)}) collective-permute-start(bf16[16,256]{1,0:T(8,128)(2,1)S(1)} %get-tuple-element.76), channel_id=1, source_target_pairs={{0,1},{1,0},{2,3},{3,2},{4,5},{5,4},{6,7},{7,6},{8,9},{9,8},{10,11... | collective-permute-start | bytes 24584 | tf_op jit(solution)/shard_map/ppermute | solution.py:22
  9.0 3.7 %collective-permute-start.3 = (bf16[16,256]{1,0:T(8,128)(2,1)S(1)}, bf16[16,256]{1,0:T(8,128)(2,1)S(1)}, u32[]{:S(2)}, u32[]{:S(2)}) collective-permute-start(bf16[16,256]{1,0:T(8,128)(2,1)S(1)} %get-tuple-element.77), channel_id=1, source_target_pairs={{0,16},{8,24},{16,0},{24,8},{1,17},{9,25},{17,1},{25,9},{2,18},{10... | collective-permute-start | bytes 24584 | tf_op jit(solution)/shard_map/ppermute | solution.py:22
  10.5 2.2 %collective-permute-start.4 = (bf16[16,256]{1,0:T(8,128)(2,1)S(1)}, bf16[16,256]{1,0:T(8,128)(2,1)S(1)}, u32[]{:S(2)}, u32[]{:S(2)}) collective-permute-start(bf16[16,256]{1,0:T(8,128)(2,1)S(1)} %get-tuple-element.78), channel_id=1, source_target_pairs={{0,8},{8,0},{16,24},{24,16},{1,9},{9,1},{17,25},{25,17},{2,10},{10... | collective-permute-start | bytes 24584 | tf_op jit(solution)/shard_map/ppermute | solution.py:22
  11.2 1.5 %copy-start.1 = (bf16[512,256]{1,0:T(8,128)(2,1)S(1)}, bf16[512,256]{1,0:T(8,128)(2,1)}, u32[]{:S(2)}) copy-start(bf16[512,256]{1,0:T(8,128)(2,1)} %node_first.1) | copy-start | bytes 786436
  11.2 1.5 %copy-start.3 = (bf16[256,256]{1,0:T(8,128)(2,1)S(1)}, bf16[256,256]{1,0:T(8,128)(2,1)}, u32[]{:S(2)}) copy-start(bf16[256,256]{1,0:T(8,128)(2,1)} %node_second.1) | copy-start | bytes 393220
  11.2 1.5 %copy-start.4 = (bf16[1,128,256]{2,1,0:T(8,128)(2,1)S(1)}, bf16[1,128,256]{2,1,0:T(8,128)(2,1)}, u32[]{:S(2)}) copy-start(bf16[1,128,256]{2,1,0:T(8,128)(2,1)} %param.20) | copy-start | bytes 196612
  14.9 4.6 %collective-permute-start.5 = (bf16[16,256]{1,0:T(8,128)(2,1)S(1)}, bf16[16,256]{1,0:T(8,128)(2,1)S(1)}, u32[]{:S(2)}, u32[]{:S(2)}) collective-permute-start(bf16[16,256]{1,0:T(8,128)(2,1)S(1)} %get-tuple-element.100), channel_id=1, source_target_pairs={{0,4},{1,5},{2,6},{3,7},{4,0},{5,1},{6,2},{7,3},{8,12},{9,13},{10,... | collective-permute-start | bytes 24584 | tf_op jit(solution)/shard_map/ppermute | solution.py:22
  15.4 4.2 %collective-permute-start.6 = (bf16[16,256]{1,0:T(8,128)(2,1)S(1)}, bf16[16,256]{1,0:T(8,128)(2,1)S(1)}, u32[]{:S(2)}, u32[]{:S(2)}) collective-permute-start(bf16[16,256]{1,0:T(8,128)(2,1)S(1)} %get-tuple-element.101), channel_id=1, source_target_pairs={{0,2},{1,3},{2,0},{3,1},{4,6},{5,7},{6,4},{7,5},{8,10},{9,11},{10,... | collective-permute-start | bytes 24584 | tf_op jit(solution)/shard_map/ppermute | solution.py:22
  15.8 3.8 %collective-permute-start.7 = (bf16[16,256]{1,0:T(8,128)(2,1)S(1)}, bf16[16,256]{1,0:T(8,128)(2,1)S(1)}, u32[]{:S(2)}, u32[]{:S(2)}) collective-permute-start(bf16[16,256]{1,0:T(8,128)(2,1)S(1)} %get-tuple-element.102), channel_id=1, source_target_pairs={{0,1},{1,0},{2,3},{3,2},{4,5},{5,4},{6,7},{7,6},{8,9},{9,8},{10,11... | collective-permute-start | bytes 24584 | tf_op jit(solution)/shard_map/ppermute | solution.py:22
  16.2 3.7 %collective-permute-start.8 = (bf16[16,256]{1,0:T(8,128)(2,1)S(1)}, bf16[16,256]{1,0:T(8,128)(2,1)S(1)}, u32[]{:S(2)}, u32[]{:S(2)}) collective-permute-start(bf16[16,256]{1,0:T(8,128)(2,1)S(1)} %get-tuple-element.103), channel_id=1, source_target_pairs={{0,16},{8,24},{16,0},{24,8},{1,17},{9,25},{17,1},{25,9},{2,18},{10... | collective-permute-start | bytes 24584 | tf_op jit(solution)/shard_map/ppermute | solution.py:22
  17.8 2.0 %collective-permute-start.9 = (bf16[16,256]{1,0:T(8,128)(2,1)S(1)}, bf16[16,256]{1,0:T(8,128)(2,1)S(1)}, u32[]{:S(2)}, u32[]{:S(2)}) collective-permute-start(bf16[16,256]{1,0:T(8,128)(2,1)S(1)} %get-tuple-element.104), channel_id=1, source_target_pairs={{0,8},{8,0},{16,24},{24,16},{1,9},{9,1},{17,25},{25,17},{2,10},{10... | collective-permute-start | bytes 24584 | tf_op jit(solution)/shard_map/ppermute | solution.py:22

commit v6 on v5

--- a/solution.py
+++ b/solution.py
@@ -101,13 +101,13 @@
     used = lax.broadcasted_iota(jnp.int32, (1, e), 1) < edge_count[0]
     hot_receive = hot(jnp.where(used, receiver[...], -1), n)
     hot_send = hot(sender[...], n)
-    gather = jnp.concatenate([hot_receive, hot_send], 0).T.astype(bf16)
-    first = mm(nodes[...], edge_first[:width])
-    second = mm(nodes[...], edge_first[width : 2 * width])
-    pre = add_rows(gather, jnp.concatenate([first, second], 0)) + mm(edges[...], edge_first[2 * width :])
+    hot_cut = jnp.concatenate([hot(cut_receiver[r], n) for r in range(ROUNDS)], 1)
+    gather = jnp.concatenate([hot_receive, hot_send, hot_cut], 1).T.astype(bf16)
+    ends = mm(gather, nodes[...]).astype(bf16)
+    pre = mm(jnp.concatenate([ends[:e], ends[e : 2 * e], edges[...]], 1), edge_first[...])
     act, slope = silu_parts(pre)
     normed, inverse = norm_parts(mm(act.astype(bf16), edge_second[...]))
-    gather_out[...] = gather[:, :n]
+    gather_out[...] = gather[:e]
     normed_out[...] = normed
     inverse_out[...] = inverse
     slope_out[...] = slope
@@ -116,11 +116,9 @@
     scatter_send[...] = hot_send.astype(bf16)
 
     send = boundary.shape[2]
-    hot_cut = jnp.concatenate([hot(cut_receiver[r], n) for r in range(ROUNDS)], 1)
     hot_far = hot(jnp.concatenate([slot[r] + r * send for r in range(ROUNDS)], 1), gather_far.shape[1])
-    at_cut = hot_cut.T.astype(bf16)
-    near[...] = add_rows(at_cut, first) + mm(cuts[...], edge_first[2 * width :])
-    gather_cut[...] = at_cut
+    near[...] = mm(ends[2 * e :], edge_first[:width]) + mm(cuts[...], edge_first[2 * width :])
+    gather_cut[...] = gather[2 * e :]
     gather_far[...] = hot_far.T.astype(bf16)
     scatter_cut[...] = hot_cut.astype(bf16)
     scatter_far[...] = hot_far[: scatter_far.shape[0]].astype(bf16)
@@ -141,7 +139,8 @@
     x = nodes[...]
     empty = jnp.zeros((gather_far.shape[1] - ROUNDS * send, width), bf16)
     far = jnp.concatenate([a[...] for a in arrived] + [empty], 0)
-    pre = near[...] + add_rows(gather_far[...], mm(far, edge_first[width : 2 * width]))
+    far_end = mm(gather_far[...], far).astype(bf16)
+    pre = near[...] + mm(far_end, edge_first[width : 2 * width])
     act, slope = silu_parts(pre)
     normed, inverse = norm_parts(mm(act.astype(bf16), edge_second[...]))
     received = (received_inner[...] + add_rows(scatter_cut[...], normed)) * edge_gain[...]

time: 20.9 us -> 20.9 us (level)
  no operation moved by 1% of the time
where the time goes in v6:
time: 20.9 us; the launch traced here: 20.7 us
  starting transfers between devices  11.5 us (55%)
  Pallas kernels  6.41 us (31%)
  between operations  2.1 us (10%)
  waiting for transfers between devices  0.63 us (3%)
    ppermute x10, starting transfers between devices, partner(): lax.ppermute(shard, axis, [(i, i ^ 1 << apart) for i in range(lax.axis_si...  11.5 us
    pallas_call x5, Pallas kernels, call(): pl.pallas_call(kernel, out_shape=out_shape, in_specs=[SMEM if a.ndim == 1...  6.41 us
    ppermute x10, waiting for transfers between devices, partner(): lax.ppermute(shard, axis, [(i, i ^ 1 << apart) for i in range(lax.axis_si...  0.63 us
  transfers between devices with their start and end apart: 10, of which 3 were waited for; matrix products, arithmetic and copies ran while one was open for 0% of the time, Pallas kernels for 10%

profile of v6, /device:TPU:0, one launch (start us, length us, event | category | flops | bytes accessed | tf_op | source)
XLA Modules:
  0.0 20.7 jit_solution(10684711740925831614)
XLA Ops:
  0.6 0.0 copy-start
  0.6 0.0 copy-start.2
  0.7 0.0 copy-start.5
  0.7 0.0 copy-start.6
  0.7 1.2 %shard_map.192 = (s32[5,1,16]{2,1,0:T(1,128)S(1)}, bf16[128,256]{1,0:T(8,128)(2,1)S(1)}, s32[1,384]{1,0:T(1,128)S(1)}, s32[1,384]{1,0:T(1,128)S(1)}, s32[5,1,64]...) custom-call(s32[5,1,16]{2,1,0:T(1,128)} %bitcast.21, ...), custom_call_target="tpu_custom_call" | custom-call | flops 4000000000 | bytes 73536 | tf_op jit(solution)/shard_map/pallas_call | solution.py:211
  1.8 4.1 %collective-permute-start = (bf16[16,256]{1,0:T(8,128)(2,1)S(1)}, bf16[16,256]{1,0:T(8,128)(2,1)S(1)}, u32[]{:S(2)}, u32[]{:S(2)}) collective-permute-start(bf16[16,256]{1,0:T(8,128)(2,1)S(1)} %get-tuple-element.74), channel_id=1, source_target_pairs={{0,4},{1,5},{2,6},{3,7},{4,0},{5,1},{6,2},{7,3},{8,12},{9,13},{10,... | collective-permute-start | bytes 24584 | tf_op jit(solution)/shard_map/ppermute | solution.py:22
  5.9 1.6 %collective-permute-start.1 = (bf16[16,256]{1,0:T(8,128)(2,1)S(1)}, bf16[16,256]{1,0:T(8,128)(2,1)S(1)}, u32[]{:S(2)}, u32[]{:S(2)}) collective-permute-start(bf16[16,256]{1,0:T(8,128)(2,1)S(1)} %get-tuple-element.75), channel_id=1, source_target_pairs={{0,2},{1,3},{2,0},{3,1},{4,6},{5,7},{6,4},{7,5},{8,10},{9,11},{10,... | collective-permute-start | bytes 24584 | tf_op jit(solution)/shard_map/ppermute | solution.py:22
  7.5 1.5 %collective-permute-start.2 = (bf16[16,256]{1,0:T(8,128)(2,1)S(1)}, bf16[16,256]{1,0:T(8,128)(2,1)S(1)}, u32[]{:S(2)}, u32[]{:S(2)}) collective-permute-start(bf16[16,256]{1,0:T(8,128)(2,1)S(1)} %get-tuple-element.76), channel_id=1, source_target_pairs={{0,1},{1,0},{2,3},{3,2},{4,5},{5,4},{6,7},{7,6},{8,9},{9,8},{10,11... | collective-permute-start | bytes 24584 | tf_op jit(solution)/shard_map/ppermute | solution.py:22
  9.0 1.5 %collective-permute-start.3 = (bf16[16,256]{1,0:T(8,128)(2,1)S(1)}, bf16[16,256]{1,0:T(8,128)(2,1)S(1)}, u32[]{:S(2)}, u32[]{:S(2)}) collective-permute-start(bf16[16,256]{1,0:T(8,128)(2,1)S(1)} %get-tuple-element.77), channel_id=1, source_target_pairs={{0,16},{8,24},{16,0},{24,8},{1,17},{9,25},{17,1},{25,9},{2,18},{10... | collective-permute-start | bytes 24584 | tf_op jit(solution)/shard_map/ppermute | solution.py:22
  10.5 0.0 collective-permute-start.4
  11.2 0.0 copy-start.1
  11.2 0.0 copy-start.3
  11.2 0.0 copy-start.4
  11.3 1.2 %shard_map.193 = (bf16[384,128]{1,0:T(8,128)(2,1)S(1)}, f32[384,256]{1,0:T(8,128)S(1)}, f32[384,1]{1,0:T(8,128)S(1)}, f32[384,256]{1,0:T(8,128)S(1)}, f32[128,25...) custom-call(s32[1]{0:T(128)S(6)} %copy.22.edge_count, ...), custom_call_target="tpu_custom_call" | custom-call | flops 4000000000 | bytes 956228 | tf_op jit(solution)/shard_map/pallas_call | solution.py:211
  12.5 0.0 collective-permute-done.rest_4_
  12.5 0.0 collective-permute-done.1.rest_3_
  12.5 0.0 collective-permute-done.2.rest_2_
  12.5 0.2 collective-permute-done.3.rest_1_
  12.7 0.0 collective-permute-done.4.rest_0_
  12.7 2.2 %shard_map.194 = (bf16[128,256]{1,0:T(8,128)(2,1)S(1)}, f32[128,256]{1,0:T(8,128)S(1)}, bf16[256,256]{1,0:T(8,128)(2,1)S(1)}, bf16[320,256]{1,0:T(8,128)(2,1)S(1...) custom-call(bf16[128,256]{1,0:T(8,128)(2,1)S(1)} %get-tuple-element., ...), custom_call_target="tpu_custom_call" | custom-call | flops 251658240 | bytes 1988608 | tf_op jit(solution)/shard_map/pallas_call | solution.py:211
  14.9 0.4 %collective-permute-start.5 = (bf16[16,256]{1,0:T(8,128)(2,1)S(1)}, bf16[16,256]{1,0:T(8,128)(2,1)S(1)}, u32[]{:S(2)}, u32[]{:S(2)}) collective-permute-start(bf16[16,256]{1,0:T(8,128)(2,1)S(1)} %get-tuple-element.100), channel_id=1, source_target_pairs={{0,4},{1,5},{2,6},{3,7},{4,0},{5,1},{6,2},{7,3},{8,12},{9,13},{10,... | collective-permute-start | bytes 24584 | tf_op jit(solution)/shard_map/ppermute | solution.py:22
  15.3 0.4 %collective-permute-start.6 = (bf16[16,256]{1,0:T(8,128)(2,1)S(1)}, bf16[16,256]{1,0:T(8,128)(2,1)S(1)}, u32[]{:S(2)}, u32[]{:S(2)}) collective-permute-start(bf16[16,256]{1,0:T(8,128)(2,1)S(1)} %get-tuple-element.101), channel_id=1, source_target_pairs={{0,2},{1,3},{2,0},{3,1},{4,6},{5,7},{6,4},{7,5},{8,10},{9,11},{10,... | collective-permute-start | bytes 24584 | tf_op jit(solution)/shard_map/ppermute | solution.py:22
  15.7 0.4 %collective-permute-start.7 = (bf16[16,256]{1,0:T(8,128)(2,1)S(1)}, bf16[16,256]{1,0:T(8,128)(2,1)S(1)}, u32[]{:S(2)}, u32[]{:S(2)}) collective-permute-start(bf16[16,256]{1,0:T(8,128)(2,1)S(1)} %get-tuple-element.102), channel_id=1, source_target_pairs={{0,1},{1,0},{2,3},{3,2},{4,5},{5,4},{6,7},{7,6},{8,9},{9,8},{10,11... | collective-permute-start | bytes 24584 | tf_op jit(solution)/shard_map/ppermute | solution.py:22
  16.1 1.6 %collective-permute-start.8 = (bf16[16,256]{1,0:T(8,128)(2,1)S(1)}, bf16[16,256]{1,0:T(8,128)(2,1)S(1)}, u32[]{:S(2)}, u32[]{:S(2)}) collective-permute-start(bf16[16,256]{1,0:T(8,128)(2,1)S(1)} %get-tuple-element.103), channel_id=1, source_target_pairs={{0,16},{8,24},{16,0},{24,8},{1,17},{9,25},{17,1},{25,9},{2,18},{10... | collective-permute-start | bytes 24584 | tf_op jit(solution)/shard_map/ppermute | solution.py:22
  17.7 0.0 collective-permute-start.9
  18.4 0.9 %shard_map.195 = (bf16[128,256]{1,0:T(8,128)(2,1)S(1)}, bf16[384,256]{1,0:T(8,128)(2,1)S(1)}, bf16[320,256]{1,0:T(8,128)(2,1)S(1)}, f32[128,256]{1,0:T(8,128)S(1)}) custom-call(s32[1]{0:T(128)S(6)} %copy.21.node_count, bf16[256,256]{1,0:T(8,128)(2,1)S(1)} %get-tuple-element.84.gained, bf16[384,128]{1,0:T(8,128)(2,1)S(1)} %get-tuple-element.85.gather, ...), custom_call_target="tpu_custom_call" | custom-call | tf_op jit(solution)/shard_map/pallas_call | solution.py:211
  19.3 0.2 %collective-permute-done.5.rest_4_ = bf16[16,256]{1,0:T(8,128)(2,1)S(1)} collective-permute-done((bf16[16,256]{1,0:T(8,128)(2,1)S(1)}, bf16[16,256]{1,0:T(8,128)(2,1)S(1)}, u32[]{:S(2)}, u32[]{:S(2)}) %collective-permute-start.5) | collective-permute-done | bytes 8224 | tf_op jit(solution)/shard_map/ppermute | solution.py:22
  19.5 0.0 collective-permute-done.6.rest_3_
  19.5 0.0 collective-permute-done.7.rest_2_
  19.5 0.2 %collective-permute-done.8.rest_1_ = bf16[16,256]{1,0:T(8,128)(2,1)S(1)} collective-permute-done((bf16[16,256]{1,0:T(8,128)(2,1)S(1)}, bf16[16,256]{1,0:T(8,128)(2,1)S(1)}, u32[]{:S(2)}, u32[]{:S(2)}) %collective-permute-start.8) | collective-permute-done | bytes 8224 | tf_op jit(solution)/shard_map/ppermute | solution.py:22
  19.8 0.0 collective-permute-done.9.rest_0_
  19.8 1.0 %shard_map.196 = (bf16[128,256]{1,0:T(8,128)(2,1)}, bf16[384,256]{1,0:T(8,128)(2,1)}, bf16[320,256]{1,0:T(8,128)(2,1)}, bf16[128,256]{1,0:T(8,128)(2,1)}) custom-call(f32[128,256]{1,0:T(8,128)S(1)} %get-tuple-element.95.total, bf16[128,80]{1,0:T(8,128)(2,1)S(1)} %get-tuple-element.96.scatter_boundary, bf16[256,768]{1,0:T(8,128)(2,1)S(1)} %get-tuple-element.89.first_t, ...), custom_call_target="tpu_custom_call" | custom-call | flops 33554432 | bytes 1011712 | tf_op jit(solution)/shard_map/pallas_call | solution.py:211
  (7 shorter events, 0.0 us)
Async XLA Ops:
  0.6 10.6 %copy-start = (bf16[768,256]{1,0:T(8,128)(2,1)S(1)}, bf16[768,256]{1,0:T(8,128)(2,1)}, u32[]{:S(2)}) copy-start(bf16[768,256]{1,0:T(8,128)(2,1)} %edge_first.3) | copy-start | bytes 1179652
  0.6 10.6 %copy-start.2 = (bf16[256,256]{1,0:T(8,128)(2,1)S(1)}, bf16[256,256]{1,0:T(8,128)(2,1)}, u32[]{:S(2)}) copy-start(bf16[256,256]{1,0:T(8,128)(2,1)} %edge_second.3) | copy-start | bytes 393220
  0.7 10.6 %copy-start.5 = (bf16[1,384,256]{2,1,0:T(8,128)(2,1)S(1)}, bf16[1,384,256]{2,1,0:T(8,128)(2,1)}, u32[]{:S(2)}) copy-start(bf16[1,384,256]{2,1,0:T(8,128)(2,1)} %param.18) | copy-start | bytes 589828
  0.7 10.6 %copy-start.6 = (bf16[1,5,64,256]{3,2,1,0:T(8,128)(2,1)S(1)}, bf16[1,5,64,256]{3,2,1,0:T(8,128)(2,1)}, u32[]{:S(2)}) copy-start(bf16[1,5,64,256]{3,2,1,0:T(8,128)(2,1)} %param.19) | copy-start | bytes 491524
  1.8 10.7 %collective-permute-start = (bf16[16,256]{1,0:T(8,128)(2,1)S(1)}, bf16[16,256]{1,0:T(8,128)(2,1)S(1)}, u32[]{:S(2)}, u32[]{:S(2)}) collective-permute-start(bf16[16,256]{1,0:T(8,128)(2,1)S(1)} %get-tuple-element.74), channel_id=1, source_target_pairs={{0,4},{1,5},{2,6},{3,7},{4,0},{5,1},{6,2},{7,3},{8,12},{9,13},{10,... | collective-permute-start | bytes 24584 | tf_op jit(solution)/shard_map/ppermute | solution.py:22
  5.9 6.6 %collective-permute-start.1 = (bf16[16,256]{1,0:T(8,128)(2,1)S(1)}, bf16[16,256]{1,0:T(8,128)(2,1)S(1)}, u32[]{:S(2)}, u32[]{:S(2)}) collective-permute-start(bf16[16,256]{1,0:T(8,128)(2,1)S(1)} %get-tuple-element.75), channel_id=1, source_target_pairs={{0,2},{1,3},{2,0},{3,1},{4,6},{5,7},{6,4},{7,5},{8,10},{9,11},{10,... | collective-permute-start | bytes 24584 | tf_op jit(solution)/shard_map/ppermute | solution.py:22
  7.5 5.0 %collective-permute-start.2 = (bf16[16,256]{1,0:T(8,128)(2,1)S(1)}, bf16[16,256]{1,0:T(8,128)(2,1)S(1)}, u32[]{:S(2)}, u32[]{:S(2)}) collective-permute-start(bf16[16,256]{1,0:T(8,128)(2,1)S(1)} %get-tuple-element.76), channel_id=1, source_target_pairs={{0,1},{1,0},{2,3},{3,2},{4,5},{5,4},{6,7},{7,6},{8,9},{9,8},{10,11... | collective-permute-start | bytes 24584 | tf_op jit(solution)/shard_map/ppermute | solution.py:22
  9.0 3.7 %collective-permute-start.3 = (bf16[16,256]{1,0:T(8,128)(2,1)S(1)}, bf16[16,256]{1,0:T(8,128)(2,1)S(1)}, u32[]{:S(2)}, u32[]{:S(2)}) collective-permute-start(bf16[16,256]{1,0:T(8,128)(2,1)S(1)} %get-tuple-element.77), channel_id=1, source_target_pairs={{0,16},{8,24},{16,0},{24,8},{1,17},{9,25},{17,1},{25,9},{2,18},{10... | collective-permute-start | bytes 24584 | tf_op jit(solution)/shard_map/ppermute | solution.py:22
  10.5 2.2 %collective-permute-start.4 = (bf16[16,256]{1,0:T(8,128)(2,1)S(1)}, bf16[16,256]{1,0:T(8,128)(2,1)S(1)}, u32[]{:S(2)}, u32[]{:S(2)}) collective-permute-start(bf16[16,256]{1,0:T(8,128)(2,1)S(1)} %get-tuple-element.78), channel_id=1, source_target_pairs={{0,8},{8,0},{16,24},{24,16},{1,9},{9,1},{17,25},{25,17},{2,10},{10... | collective-permute-start | bytes 24584 | tf_op jit(solution)/shard_map/ppermute | solution.py:22
  11.2 1.5 %copy-start.1 = (bf16[512,256]{1,0:T(8,128)(2,1)S(1)}, bf16[512,256]{1,0:T(8,128)(2,1)}, u32[]{:S(2)}) copy-start(bf16[512,256]{1,0:T(8,128)(2,1)} %node_first.1) | copy-start | bytes 786436
  11.2 1.5 %copy-start.3 = (bf16[256,256]{1,0:T(8,128)(2,1)S(1)}, bf16[256,256]{1,0:T(8,128)(2,1)}, u32[]{:S(2)}) copy-start(bf16[256,256]{1,0:T(8,128)(2,1)} %node_second.1) | copy-start | bytes 393220
  11.2 1.5 %copy-start.4 = (bf16[1,128,256]{2,1,0:T(8,128)(2,1)S(1)}, bf16[1,128,256]{2,1,0:T(8,128)(2,1)}, u32[]{:S(2)}) copy-start(bf16[1,128,256]{2,1,0:T(8,128)(2,1)} %param.20) | copy-start | bytes 196612
  14.9 4.6 %collective-permute-start.5 = (bf16[16,256]{1,0:T(8,128)(2,1)S(1)}, bf16[16,256]{1,0:T(8,128)(2,1)S(1)}, u32[]{:S(2)}, u32[]{:S(2)}) collective-permute-start(bf16[16,256]{1,0:T(8,128)(2,1)S(1)} %get-tuple-element.100), channel_id=1, source_target_pairs={{0,4},{1,5},{2,6},{3,7},{4,0},{5,1},{6,2},{7,3},{8,12},{9,13},{10,... | collective-permute-start | bytes 24584 | tf_op jit(solution)/shard_map/ppermute | solution.py:22
  15.3 4.2 %collective-permute-start.6 = (bf16[16,256]{1,0:T(8,128)(2,1)S(1)}, bf16[16,256]{1,0:T(8,128)(2,1)S(1)}, u32[]{:S(2)}, u32[]{:S(2)}) collective-permute-start(bf16[16,256]{1,0:T(8,128)(2,1)S(1)} %get-tuple-element.101), channel_id=1, source_target_pairs={{0,2},{1,3},{2,0},{3,1},{4,6},{5,7},{6,4},{7,5},{8,10},{9,11},{10,... | collective-permute-start | bytes 24584 | tf_op jit(solution)/shard_map/ppermute | solution.py:22
  15.7 3.8 %collective-permute-start.7 = (bf16[16,256]{1,0:T(8,128)(2,1)S(1)}, bf16[16,256]{1,0:T(8,128)(2,1)S(1)}, u32[]{:S(2)}, u32[]{:S(2)}) collective-permute-start(bf16[16,256]{1,0:T(8,128)(2,1)S(1)} %get-tuple-element.102), channel_id=1, source_target_pairs={{0,1},{1,0},{2,3},{3,2},{4,5},{5,4},{6,7},{7,6},{8,9},{9,8},{10,11... | collective-permute-start | bytes 24584 | tf_op jit(solution)/shard_map/ppermute | solution.py:22
  16.1 3.7 %collective-permute-start.8 = (bf16[16,256]{1,0:T(8,128)(2,1)S(1)}, bf16[16,256]{1,0:T(8,128)(2,1)S(1)}, u32[]{:S(2)}, u32[]{:S(2)}) collective-permute-start(bf16[16,256]{1,0:T(8,128)(2,1)S(1)} %get-tuple-element.103), channel_id=1, source_target_pairs={{0,16},{8,24},{16,0},{24,8},{1,17},{9,25},{17,1},{25,9},{2,18},{10... | collective-permute-start | bytes 24584 | tf_op jit(solution)/shard_map/ppermute | solution.py:22
  17.7 2.0 %collective-permute-start.9 = (bf16[16,256]{1,0:T(8,128)(2,1)S(1)}, bf16[16,256]{1,0:T(8,128)(2,1)S(1)}, u32[]{:S(2)}, u32[]{:S(2)}) collective-permute-start(bf16[16,256]{1,0:T(8,128)(2,1)S(1)} %get-tuple-element.104), channel_id=1, source_target_pairs={{0,8},{8,0},{16,24},{24,16},{1,9},{9,1},{17,25},{25,17},{2,10},{10... | collective-permute-start | bytes 24584 | tf_op jit(solution)/shard_map/ppermute | solution.py:22

commit v7 on v6

--- a/solution.py
+++ b/solution.py
@@ -55,6 +55,17 @@
 
 def norm_parts(values):
     centred = values - lane_mean(values)
+    inverse = lax.rsqrt(lane_mean(centred * centred) + epsilon)
+    return centred * inverse, inverse
+
+
+def centred_parts(weights):
+    values = weights.astype(f32)
+    return jnp.concatenate(split(values - lane_mean(values)), 0)
+
+
+def norm_centred(act, parts):
+    centred = mm(jnp.concatenate([act, act], 1), parts)
     inverse = lax.rsqrt(lane_mean(centred * centred) + epsilon)
     return centred * inverse, inverse
 
@@ -95,6 +106,7 @@
     edge_count, nodes, edges, cuts, sender, receiver, slot, cut_receiver, boundary, edge_first, edge_second,
     gather_out, normed_out, inverse_out, slope_out, received, near, gather_cut, gather_far,
     scatter_receive, scatter_send, scatter_cut, scatter_far, scatter_boundary, first_t, second_t,
+    second_centred,
 ):
     n, width = nodes.shape
     e = edges.shape[0]
@@ -125,14 +137,15 @@
     scatter_boundary[...] = jnp.concatenate([hot(boundary[r], n) for r in range(ROUNDS)], 1).astype(bf16)
     first_t[...] = edge_first[...].T
     second_t[...] = edge_second[...].T
+    second_centred[...] = centred_parts(edge_second[...])
 
 
 def main_kernel(
-    nodes, cotangent, edge_first, edge_second, edge_gain, node_first, node_second, node_gain, received_inner, near,
+    nodes, cotangent, edge_first, second_centred, edge_gain, node_first, node_second, node_gain, received_inner, near,
     gather_cut, gather_far, scatter_cut, scatter_far, second_t, *rest,
 ):
     arrived = rest[:ROUNDS]
-    updated, base, gained, grad_cut = rest[ROUNDS : ROUNDS + 4]
+    updated, base, grad_nodes, grad_cut = rest[ROUNDS : ROUNDS + 4]
     back = rest[ROUNDS + 4 :]
     n, width = nodes.shape
     send = arrived[0].shape[0]
@@ -142,31 +155,30 @@
     far_end = mm(gather_far[...], far).astype(bf16)
     pre = near[...] + mm(far_end, edge_first[width : 2 * width])
     act, slope = silu_parts(pre)
-    normed, inverse = norm_parts(mm(act.astype(bf16), edge_second[...]))
+    normed, inverse = norm_centred(act.astype(bf16), second_centred[...])
     received = (received_inner[...] + add_rows(scatter_cut[...], normed)) * edge_gain[...]
 
     pre_node = mm(jnp.concatenate([x, received.astype(bf16)], 1), node_first[...])
     act_node, slope_node = silu_parts(pre_node)
-    normed_node, inverse_node = norm_parts(mm(act_node.astype(bf16), node_second[...]))
+    normed_node, inverse_node = norm_centred(act_node.astype(bf16), centred_parts(node_second[...]))
     updated[...] = (x.astype(f32) + normed_node * node_gain[...]).astype(bf16)
     upstream = cotangent[...].astype(f32)
     grad_out_node = norm_backward(upstream * node_gain[...], normed_node, inverse_node).astype(bf16)
     grad_pre_node = (mm_t(grad_out_node, node_second[...]) * slope_node).astype(bf16)
-    at_receiver = mm_t(grad_pre_node, node_first[width:]) * edge_gain[...]
-    parts = jnp.concatenate(split(at_receiver), 0)
-    twice = jnp.concatenate([gather_cut[...], gather_cut[...]], 1)
-    grad_out = norm_backward(mm(twice, parts), normed, inverse).astype(bf16)
+    gathered = mm(gather_cut[...], grad_pre_node).astype(bf16)
+    scaled = mm_t(gathered, node_first[width:]) * edge_gain[...]
+    grad_out = norm_backward(scaled, normed, inverse).astype(bf16)
     grad = (mm(grad_out, second_t[...]) * slope).astype(bf16)
     sums = mm(scatter_far[...], grad).astype(bf16)
     for r in range(ROUNDS):
         back[r][...] = sums[r * send : (r + 1) * send]
     grad_cut[...] = grad
-    gained[...] = parts
+    grad_nodes[...] = grad_pre_node
     base[...] = upstream + mm_t(grad_pre_node, node_first[:width])
 
 
 def outer_kernel(
-    node_count, gained, gather, normed, inverse, slope, first_t, second_t, scatter_receive, scatter_send, scatter_cut,
+    node_count, grad_nodes, node_first, edge_gain, gather, normed, inverse, slope, first_t, second_t, scatter_receive, scatter_send, scatter_cut,
     grad_cut, base, updated_in, updated, edge_gradient, cut_gradient, total,
 ):
     n, width = base.shape
@@ -174,8 +186,9 @@
     updated[...] = jnp.where(valid, updated_in[...].astype(f32), 0.0).astype(bf16)
     cut = grad_cut[...]
     cut_gradient[...] = mm(cut, first_t[:, 2 * width :]).astype(bf16)
-    twice = jnp.concatenate([gather[...], gather[...]], 1)
-    grad_out = norm_backward(mm(twice, gained[...]), normed[...], inverse[...]).astype(bf16)
+    gathered = mm(gather[...], grad_nodes[...]).astype(bf16)
+    scaled = mm_t(gathered, node_first[width:]) * edge_gain[...]
+    grad_out = norm_backward(scaled, normed[...], inverse[...]).astype(bf16)
     grad = (mm(grad_out, second_t[...]) * slope[...]).astype(bf16)
     edge_gradient[...] = mm(grad, first_t[:, 2 * width :]).astype(bf16)
     at_receiver = mm(scatter_receive[...], grad) + mm(scatter_cut[...], cut)
@@ -261,6 +274,7 @@
             kept((n, width), f32), kept((c, width), f32), kept((c, n), bf16), kept((c, all_slots), bf16),
             kept((n, e), bf16), kept((n, e), bf16), kept((n, c), bf16), kept((some, c), bf16),
             kept((n, slots), bf16), kept((width, 3 * width), bf16), kept((width, width), bf16),
+            kept((2 * width, width), bf16),
         ],
         (
             edge_count, nodes, edges, cuts, edge_sender, edge_receiver, slot, cut_targets, boundary, edge_first,
@@ -269,24 +283,24 @@
         LONG,
     )
     gather, normed, inverse, slope, received, near, gather_cut, gather_far = outs[:8]
-    scatter_receive, scatter_send, scatter_cut, scatter_far, scatter_boundary, first_t, second_t = outs[8:]
+    scatter_receive, scatter_send, scatter_cut, scatter_far, scatter_boundary, first_t, second_t, second_centred = outs[8:]
     outs = call(
         main_kernel,
-        [kept((n, width), bf16), kept((n, width), f32), kept((2 * n, width), bf16), kept((c, width), bf16)]
+        [kept((n, width), bf16), kept((n, width), f32), kept((n, width), bf16), kept((c, width), bf16)]
         + [kept((send, width), bf16)] * ROUNDS,
         (
-            nodes, node_cotangent[0], edge_first, edge_second, edge_gain, node_first, node_second, node_gain,
+            nodes, node_cotangent[0], edge_first, second_centred, edge_gain, node_first, node_second, node_gain,
             received, near, gather_cut, gather_far, scatter_cut, scatter_far, second_t, *arrived,
         ),
         2 * c * width * width * 6,
     )
-    updated, base, gained, grad_cut = outs[:4]
+    updated, base, grad_nodes, grad_cut = outs[:4]
     returned = exchange(outs[4:])
     updated, edge_gradient, cut_gradient, total = call(
         outer_kernel,
         [kept((n, width), bf16), kept((e, width), bf16), kept((c, width), bf16), kept((n, width), f32)],
         (
-            node_count, gained, gather, normed, inverse, slope, first_t, second_t, scatter_receive, scatter_send,
+            node_count, grad_nodes, node_first, edge_gain, gather, normed, inverse, slope, first_t, second_t, scatter_receive, scatter_send,
             scatter_cut, grad_cut, base, updated,
         ),
         0,

time: 20.9 us -> 20.8 us (level)
  no operation moved by 1% of the time
where the time goes in v7:
time: 20.8 us; the launch traced here: 20.6 us
  starting transfers between devices  11.5 us (55%)
  Pallas kernels  6.37 us (31%)
  between operations  2.1 us (10%)
  waiting for transfers between devices  0.58 us (3%)
    ppermute x10, starting transfers between devices, partner(): lax.ppermute(shard, axis, [(i, i ^ 1 << apart) for i in range(lax.axis_si...  11.5 us
    pallas_call x5, Pallas kernels, call(): pl.pallas_call(kernel, out_shape=out_shape, in_specs=[SMEM if a.ndim == 1...  6.37 us
    ppermute x10, waiting for transfers between devices, partner(): lax.ppermute(shard, axis, [(i, i ^ 1 << apart) for i in range(lax.axis_si...  0.58 us
  transfers between devices with their start and end apart: 10, of which 3 were waited for; matrix products, arithmetic and copies ran while one was open for 0% of the time, Pallas kernels for 10%

profile of v7, /device:TPU:0, one launch (start us, length us, event | category | flops | bytes accessed | tf_op | source)
XLA Modules:
  0.0 20.6 jit_solution(556312948669889655)
XLA Ops:
  0.6 0.0 copy-start.1
  0.6 0.0 copy-start.4
  0.7 0.0 copy-start.5
  0.7 0.0 copy-start.6
  0.7 1.2 %shard_map.192 = (s32[5,1,16]{2,1,0:T(1,128)S(1)}, bf16[128,256]{1,0:T(8,128)(2,1)S(1)}, s32[1,384]{1,0:T(1,128)S(1)}, s32[1,384]{1,0:T(1,128)S(1)}, s32[5,1,64]...) custom-call(s32[5,1,16]{2,1,0:T(1,128)} %bitcast.21, ...), custom_call_target="tpu_custom_call" | custom-call | flops 4000000000 | bytes 73536 | tf_op jit(solution)/shard_map/pallas_call | solution.py:224
  1.8 4.1 %collective-permute-start = (bf16[16,256]{1,0:T(8,128)(2,1)S(1)}, bf16[16,256]{1,0:T(8,128)(2,1)S(1)}, u32[]{:S(2)}, u32[]{:S(2)}) collective-permute-start(bf16[16,256]{1,0:T(8,128)(2,1)S(1)} %get-tuple-element.76), channel_id=1, source_target_pairs={{0,4},{1,5},{2,6},{3,7},{4,0},{5,1},{6,2},{7,3},{8,12},{9,13},{10,... | collective-permute-start | bytes 24584 | tf_op jit(solution)/shard_map/ppermute | solution.py:22
  5.9 1.6 %collective-permute-start.1 = (bf16[16,256]{1,0:T(8,128)(2,1)S(1)}, bf16[16,256]{1,0:T(8,128)(2,1)S(1)}, u32[]{:S(2)}, u32[]{:S(2)}) collective-permute-start(bf16[16,256]{1,0:T(8,128)(2,1)S(1)} %get-tuple-element.77), channel_id=1, source_target_pairs={{0,2},{1,3},{2,0},{3,1},{4,6},{5,7},{6,4},{7,5},{8,10},{9,11},{10,... | collective-permute-start | bytes 24584 | tf_op jit(solution)/shard_map/ppermute | solution.py:22
  7.5 1.5 %collective-permute-start.2 = (bf16[16,256]{1,0:T(8,128)(2,1)S(1)}, bf16[16,256]{1,0:T(8,128)(2,1)S(1)}, u32[]{:S(2)}, u32[]{:S(2)}) collective-permute-start(bf16[16,256]{1,0:T(8,128)(2,1)S(1)} %get-tuple-element.78), channel_id=1, source_target_pairs={{0,1},{1,0},{2,3},{3,2},{4,5},{5,4},{6,7},{7,6},{8,9},{9,8},{10,11... | collective-permute-start | bytes 24584 | tf_op jit(solution)/shard_map/ppermute | solution.py:22
  9.0 1.5 %collective-permute-start.3 = (bf16[16,256]{1,0:T(8,128)(2,1)S(1)}, bf16[16,256]{1,0:T(8,128)(2,1)S(1)}, u32[]{:S(2)}, u32[]{:S(2)}) collective-permute-start(bf16[16,256]{1,0:T(8,128)(2,1)S(1)} %get-tuple-element.79), channel_id=1, source_target_pairs={{0,16},{8,24},{16,0},{24,8},{1,17},{9,25},{17,1},{25,9},{2,18},{10... | collective-permute-start | bytes 24584 | tf_op jit(solution)/shard_map/ppermute | solution.py:22
  10.5 0.0 collective-permute-start.4
  11.2 0.0 copy-start
  11.2 0.0 copy-start.2
  11.2 0.0 copy-start.3
  11.3 1.2 %shard_map.193 = (bf16[384,128]{1,0:T(8,128)(2,1)S(1)}, f32[384,256]{1,0:T(8,128)S(1)}, f32[384,1]{1,0:T(8,128)S(1)}, f32[384,256]{1,0:T(8,128)S(1)}, f32[128,25...) custom-call(s32[1]{0:T(128)S(6)} %copy.22.edge_count, ...), custom_call_target="tpu_custom_call" | custom-call | flops 4000000000 | bytes 956228 | tf_op jit(solution)/shard_map/pallas_call | solution.py:224
  12.5 0.0 collective-permute-done.rest_4_
  12.5 0.0 collective-permute-done.1.rest_3_
  12.5 0.0 collective-permute-done.2.rest_2_
  12.5 0.2 collective-permute-done.3.rest_1_
  12.7 0.0 collective-permute-done.4.rest_0_
  12.7 2.1 %shard_map.194 = (bf16[128,256]{1,0:T(8,128)(2,1)S(1)}, f32[128,256]{1,0:T(8,128)S(1)}, bf16[128,256]{1,0:T(8,128)(2,1)S(1)}, bf16[320,256]{1,0:T(8,128)(2,1)S(1...) custom-call(bf16[128,256]{1,0:T(8,128)(2,1)S(1)} %get-tuple-element., ...), custom_call_target="tpu_custom_call" | custom-call | flops 251658240 | bytes 2119680 | tf_op jit(solution)/shard_map/pallas_call | solution.py:224
  14.8 0.4 %collective-permute-start.5 = (bf16[16,256]{1,0:T(8,128)(2,1)S(1)}, bf16[16,256]{1,0:T(8,128)(2,1)S(1)}, u32[]{:S(2)}, u32[]{:S(2)}) collective-permute-start(bf16[16,256]{1,0:T(8,128)(2,1)S(1)} %get-tuple-element.102), channel_id=1, source_target_pairs={{0,4},{1,5},{2,6},{3,7},{4,0},{5,1},{6,2},{7,3},{8,12},{9,13},{10,... | collective-permute-start | bytes 24584 | tf_op jit(solution)/shard_map/ppermute | solution.py:22
  15.2 0.4 %collective-permute-start.6 = (bf16[16,256]{1,0:T(8,128)(2,1)S(1)}, bf16[16,256]{1,0:T(8,128)(2,1)S(1)}, u32[]{:S(2)}, u32[]{:S(2)}) collective-permute-start(bf16[16,256]{1,0:T(8,128)(2,1)S(1)} %get-tuple-element.103), channel_id=1, source_target_pairs={{0,2},{1,3},{2,0},{3,1},{4,6},{5,7},{6,4},{7,5},{8,10},{9,11},{10,... | collective-permute-start | bytes 24584 | tf_op jit(solution)/shard_map/ppermute | solution.py:22
  15.7 0.3 %collective-permute-start.7 = (bf16[16,256]{1,0:T(8,128)(2,1)S(1)}, bf16[16,256]{1,0:T(8,128)(2,1)S(1)}, u32[]{:S(2)}, u32[]{:S(2)}) collective-permute-start(bf16[16,256]{1,0:T(8,128)(2,1)S(1)} %get-tuple-element.104), channel_id=1, source_target_pairs={{0,1},{1,0},{2,3},{3,2},{4,5},{5,4},{6,7},{7,6},{8,9},{9,8},{10,11... | collective-permute-start | bytes 24584 | tf_op jit(solution)/shard_map/ppermute | solution.py:22
  16.0 1.7 %collective-permute-start.8 = (bf16[16,256]{1,0:T(8,128)(2,1)S(1)}, bf16[16,256]{1,0:T(8,128)(2,1)S(1)}, u32[]{:S(2)}, u32[]{:S(2)}) collective-permute-start(bf16[16,256]{1,0:T(8,128)(2,1)S(1)} %get-tuple-element.105), channel_id=1, source_target_pairs={{0,16},{8,24},{16,0},{24,8},{1,17},{9,25},{17,1},{25,9},{2,18},{10... | collective-permute-start | bytes 24584 | tf_op jit(solution)/shard_map/ppermute | solution.py:22
  17.7 0.0 collective-permute-start.9
  18.3 1.0 %shard_map.195 = (bf16[128,256]{1,0:T(8,128)(2,1)S(1)}, bf16[384,256]{1,0:T(8,128)(2,1)S(1)}, bf16[320,256]{1,0:T(8,128)(2,1)S(1)}, f32[128,256]{1,0:T(8,128)S(1)}) custom-call(s32[1]{0:T(128)S(6)} %copy.21.node_count, bf16[128,256]{1,0:T(8,128)(2,1)S(1)} %get-tuple-element.86.grad_nodes, bf16[512,256]{1,0:T(8,128)(2,1)S(1)} %copy-done, ...), custom_call_target="tpu_custom_call" | custom-call | tf_op jit(solution)/shard_map/pallas_call | solution.py:224
  19.3 0.1 collective-permute-done.5.rest_4_
  19.4 0.0 collective-permute-done.6.rest_3_
  19.4 0.0 collective-permute-done.7.rest_2_
  19.4 0.2 %collective-permute-done.8.rest_1_ = bf16[16,256]{1,0:T(8,128)(2,1)S(1)} collective-permute-done((bf16[16,256]{1,0:T(8,128)(2,1)S(1)}, bf16[16,256]{1,0:T(8,128)(2,1)S(1)}, u32[]{:S(2)}, u32[]{:S(2)}) %collective-permute-start.8) | collective-permute-done | bytes 8224 | tf_op jit(solution)/shard_map/ppermute | solution.py:22
  19.7 0.0 collective-permute-done.9.rest_0_
  19.7 1.0 %shard_map.196 = (bf16[128,256]{1,0:T(8,128)(2,1)}, bf16[384,256]{1,0:T(8,128)(2,1)}, bf16[320,256]{1,0:T(8,128)(2,1)}, bf16[128,256]{1,0:T(8,128)(2,1)}) custom-call(f32[128,256]{1,0:T(8,128)S(1)} %get-tuple-element.97.total, bf16[128,80]{1,0:T(8,128)(2,1)S(1)} %get-tuple-element.98.scatter_boundary, bf16[256,768]{1,0:T(8,128)(2,1)S(1)} %get-tuple-element.91.first_t, ...), custom_call_target="tpu_custom_call" | custom-call | flops 33554432 | bytes 1011712 | tf_op jit(solution)/shard_map/pallas_call | solution.py:224
  (7 shorter events, 0.0 us)
Async XLA Ops:
  0.6 10.6 %copy-start.1 = (bf16[768,256]{1,0:T(8,128)(2,1)S(1)}, bf16[768,256]{1,0:T(8,128)(2,1)}, u32[]{:S(2)}) copy-start(bf16[768,256]{1,0:T(8,128)(2,1)} %edge_first.3) | copy-start | bytes 1179652
  0.6 10.6 %copy-start.4 = (bf16[1,384,256]{2,1,0:T(8,128)(2,1)S(1)}, bf16[1,384,256]{2,1,0:T(8,128)(2,1)}, u32[]{:S(2)}) copy-start(bf16[1,384,256]{2,1,0:T(8,128)(2,1)} %param.18) | copy-start | bytes 589828
  0.7 10.6 %copy-start.5 = (bf16[1,5,64,256]{3,2,1,0:T(8,128)(2,1)S(1)}, bf16[1,5,64,256]{3,2,1,0:T(8,128)(2,1)}, u32[]{:S(2)}) copy-start(bf16[1,5,64,256]{3,2,1,0:T(8,128)(2,1)} %param.19) | copy-start | bytes 491524
  0.7 10.6 %copy-start.6 = (bf16[256,256]{1,0:T(8,128)(2,1)S(1)}, bf16[256,256]{1,0:T(8,128)(2,1)}, u32[]{:S(2)}) copy-start(bf16[256,256]{1,0:T(8,128)(2,1)} %edge_second.1) | copy-start | bytes 393220
  1.8 10.6 %collective-permute-start = (bf16[16,256]{1,0:T(8,128)(2,1)S(1)}, bf16[16,256]{1,0:T(8,128)(2,1)S(1)}, u32[]{:S(2)}, u32[]{:S(2)}) collective-permute-start(bf16[16,256]{1,0:T(8,128)(2,1)S(1)} %get-tuple-element.76), channel_id=1, source_target_pairs={{0,4},{1,5},{2,6},{3,7},{4,0},{5,1},{6,2},{7,3},{8,12},{9,13},{10,... | collective-permute-start | bytes 24584 | tf_op jit(solution)/shard_map/ppermute | solution.py:22
  5.9 6.5 %collective-permute-start.1 = (bf16[16,256]{1,0:T(8,128)(2,1)S(1)}, bf16[16,256]{1,0:T(8,128)(2,1)S(1)}, u32[]{:S(2)}, u32[]{:S(2)}) collective-permute-start(bf16[16,256]{1,0:T(8,128)(2,1)S(1)} %get-tuple-element.77), channel_id=1, source_target_pairs={{0,2},{1,3},{2,0},{3,1},{4,6},{5,7},{6,4},{7,5},{8,10},{9,11},{10,... | collective-permute-start | bytes 24584 | tf_op jit(solution)/shard_map/ppermute | solution.py:22
  7.5 5.0 %collective-permute-start.2 = (bf16[16,256]{1,0:T(8,128)(2,1)S(1)}, bf16[16,256]{1,0:T(8,128)(2,1)S(1)}, u32[]{:S(2)}, u32[]{:S(2)}) collective-permute-start(bf16[16,256]{1,0:T(8,128)(2,1)S(1)} %get-tuple-element.78), channel_id=1, source_target_pairs={{0,1},{1,0},{2,3},{3,2},{4,5},{5,4},{6,7},{7,6},{8,9},{9,8},{10,11... | collective-permute-start | bytes 24584 | tf_op jit(solution)/shard_map/ppermute | solution.py:22
  9.0 3.7 %collective-permute-start.3 = (bf16[16,256]{1,0:T(8,128)(2,1)S(1)}, bf16[16,256]{1,0:T(8,128)(2,1)S(1)}, u32[]{:S(2)}, u32[]{:S(2)}) collective-permute-start(bf16[16,256]{1,0:T(8,128)(2,1)S(1)} %get-tuple-element.79), channel_id=1, source_target_pairs={{0,16},{8,24},{16,0},{24,8},{1,17},{9,25},{17,1},{25,9},{2,18},{10... | collective-permute-start | bytes 24584 | tf_op jit(solution)/shard_map/ppermute | solution.py:22
  10.5 2.2 %collective-permute-start.4 = (bf16[16,256]{1,0:T(8,128)(2,1)S(1)}, bf16[16,256]{1,0:T(8,128)(2,1)S(1)}, u32[]{:S(2)}, u32[]{:S(2)}) collective-permute-start(bf16[16,256]{1,0:T(8,128)(2,1)S(1)} %get-tuple-element.80), channel_id=1, source_target_pairs={{0,8},{8,0},{16,24},{24,16},{1,9},{9,1},{17,25},{25,17},{2,10},{10... | collective-permute-start | bytes 24584 | tf_op jit(solution)/shard_map/ppermute | solution.py:22
  11.2 1.5 %copy-start = (bf16[512,256]{1,0:T(8,128)(2,1)S(1)}, bf16[512,256]{1,0:T(8,128)(2,1)}, u32[]{:S(2)}) copy-start(bf16[512,256]{1,0:T(8,128)(2,1)} %node_first.3) | copy-start | bytes 786436
  11.2 1.5 %copy-start.2 = (bf16[256,256]{1,0:T(8,128)(2,1)S(1)}, bf16[256,256]{1,0:T(8,128)(2,1)}, u32[]{:S(2)}) copy-start(bf16[256,256]{1,0:T(8,128)(2,1)} %node_second.1) | copy-start | bytes 393220
  11.2 1.5 %copy-start.3 = (bf16[1,128,256]{2,1,0:T(8,128)(2,1)S(1)}, bf16[1,128,256]{2,1,0:T(8,128)(2,1)}, u32[]{:S(2)}) copy-start(bf16[1,128,256]{2,1,0:T(8,128)(2,1)} %param.20) | copy-start | bytes 196612
  14.8 4.6 %collective-permute-start.5 = (bf16[16,256]{1,0:T(8,128)(2,1)S(1)}, bf16[16,256]{1,0:T(8,128)(2,1)S(1)}, u32[]{:S(2)}, u32[]{:S(2)}) collective-permute-start(bf16[16,256]{1,0:T(8,128)(2,1)S(1)} %get-tuple-element.102), channel_id=1, source_target_pairs={{0,4},{1,5},{2,6},{3,7},{4,0},{5,1},{6,2},{7,3},{8,12},{9,13},{10,... | collective-permute-start | bytes 24584 | tf_op jit(solution)/shard_map/ppermute | solution.py:22
  15.2 4.2 %collective-permute-start.6 = (bf16[16,256]{1,0:T(8,128)(2,1)S(1)}, bf16[16,256]{1,0:T(8,128)(2,1)S(1)}, u32[]{:S(2)}, u32[]{:S(2)}) collective-permute-start(bf16[16,256]{1,0:T(8,128)(2,1)S(1)} %get-tuple-element.103), channel_id=1, source_target_pairs={{0,2},{1,3},{2,0},{3,1},{4,6},{5,7},{6,4},{7,5},{8,10},{9,11},{10,... | collective-permute-start | bytes 24584 | tf_op jit(solution)/shard_map/ppermute | solution.py:22
  15.7 3.8 %collective-permute-start.7 = (bf16[16,256]{1,0:T(8,128)(2,1)S(1)}, bf16[16,256]{1,0:T(8,128)(2,1)S(1)}, u32[]{:S(2)}, u32[]{:S(2)}) collective-permute-start(bf16[16,256]{1,0:T(8,128)(2,1)S(1)} %get-tuple-element.104), channel_id=1, source_target_pairs={{0,1},{1,0},{2,3},{3,2},{4,5},{5,4},{6,7},{7,6},{8,9},{9,8},{10,11... | collective-permute-start | bytes 24584 | tf_op jit(solution)/shard_map/ppermute | solution.py:22
  16.0 3.7 %collective-permute-start.8 = (bf16[16,256]{1,0:T(8,128)(2,1)S(1)}, bf16[16,256]{1,0:T(8,128)(2,1)S(1)}, u32[]{:S(2)}, u32[]{:S(2)}) collective-permute-start(bf16[16,256]{1,0:T(8,128)(2,1)S(1)} %get-tuple-element.105), channel_id=1, source_target_pairs={{0,16},{8,24},{16,0},{24,8},{1,17},{9,25},{17,1},{25,9},{2,18},{10... | collective-permute-start | bytes 24584 | tf_op jit(solution)/shard_map/ppermute | solution.py:22
  17.7 2.0 %collective-permute-start.9 = (bf16[16,256]{1,0:T(8,128)(2,1)S(1)}, bf16[16,256]{1,0:T(8,128)(2,1)S(1)}, u32[]{:S(2)}, u32[]{:S(2)}) collective-permute-start(bf16[16,256]{1,0:T(8,128)(2,1)S(1)} %get-tuple-element.106), channel_id=1, source_target_pairs={{0,8},{8,0},{16,24},{24,16},{1,9},{9,1},{17,25},{25,17},{2,10},{10... | collective-permute-start | bytes 24584 | tf_op jit(solution)/shard_map/ppermute | solution.py:22

commit v8 on v7

--- a/solution.py
+++ b/solution.py
@@ -145,8 +145,8 @@
     gather_cut, gather_far, scatter_cut, scatter_far, second_t, *rest,
 ):
     arrived = rest[:ROUNDS]
-    updated, base, grad_nodes, grad_cut = rest[ROUNDS : ROUNDS + 4]
-    back = rest[ROUNDS + 4 :]
+    updated, grad_nodes, grad_cut = rest[ROUNDS : ROUNDS + 3]
+    back = rest[ROUNDS + 3 :]
     n, width = nodes.shape
     send = arrived[0].shape[0]
     x = nodes[...]
@@ -174,14 +174,13 @@
         back[r][...] = sums[r * send : (r + 1) * send]
     grad_cut[...] = grad
     grad_nodes[...] = grad_pre_node
-    base[...] = upstream + mm_t(grad_pre_node, node_first[:width])
 
 
 def outer_kernel(
     node_count, grad_nodes, node_first, edge_gain, gather, normed, inverse, slope, first_t, second_t, scatter_receive, scatter_send, scatter_cut,
-    grad_cut, base, updated_in, updated, edge_gradient, cut_gradient, total,
+    grad_cut, cotangent, updated_in, updated, edge_gradient, cut_gradient, total,
 ):
-    n, width = base.shape
+    n, width = cotangent.shape
     valid = lax.broadcasted_iota(jnp.int32, (n, width), 0) < node_count[0]
     updated[...] = jnp.where(valid, updated_in[...].astype(f32), 0.0).astype(bf16)
     cut = grad_cut[...]
@@ -194,7 +193,7 @@
     at_receiver = mm(scatter_receive[...], grad) + mm(scatter_cut[...], cut)
     at_sender = mm(scatter_send[...], grad)
     total[...] = (
-        jnp.where(valid, base[...], 0.0)
+        jnp.where(valid, cotangent[...].astype(f32) + mm_t(grad_nodes[...], node_first[:width]), 0.0)
         + mm(at_receiver.astype(bf16), first_t[:, :width])
         + mm(at_sender.astype(bf16), first_t[:, width : 2 * width])
     )
@@ -286,7 +285,7 @@
     scatter_receive, scatter_send, scatter_cut, scatter_far, scatter_boundary, first_t, second_t, second_centred = outs[8:]
     outs = call(
         main_kernel,
-        [kept((n, width), bf16), kept((n, width), f32), kept((n, width), bf16), kept((c, width), bf16)]
+        [kept((n, width), bf16), kept((n, width), bf16), kept((c, width), bf16)]
         + [kept((send, width), bf16)] * ROUNDS,
         (
             nodes, node_cotangent[0], edge_first, second_centred, edge_gain, node_first, node_second, node_gain,
@@ -294,14 +293,14 @@
         ),
         2 * c * width * width * 6,
     )
-    updated, base, grad_nodes, grad_cut = outs[:4]
-    returned = exchange(outs[4:])
+    updated, grad_nodes, grad_cut = outs[:3]
+    returned = exchange(outs[3:])
     updated, edge_gradient, cut_gradient, total = call(
         outer_kernel,
         [kept((n, width), bf16), kept((e, width), bf16), kept((c, width), bf16), kept((n, width), f32)],
         (
             node_count, grad_nodes, node_first, edge_gain, gather, normed, inverse, slope, first_t, second_t, scatter_receive, scatter_send,
-            scatter_cut, grad_cut, base, updated,
+            scatter_cut, grad_cut, node_cotangent[0], updated,
         ),
         0,
     )

time: 20.8 us -> 20.8 us (level)
  no operation moved by 1% of the time
where the time goes in v8:
time: 20.8 us; the launch traced here: 20.6 us
  starting transfers between devices  11.5 us (55%)
  Pallas kernels  6.36 us (31%)
  between operations  2.1 us (10%)
  waiting for transfers between devices  0.58 us (3%)
    ppermute x10, starting transfers between devices, partner(): lax.ppermute(shard, axis, [(i, i ^ 1 << apart) for i in range(lax.axis_si...  11.5 us
    pallas_call x5, Pallas kernels, call(): pl.pallas_call(kernel, out_shape=out_shape, in_specs=[SMEM if a.ndim == 1...  6.36 us
    ppermute x10, waiting for transfers between devices, partner(): lax.ppermute(shard, axis, [(i, i ^ 1 << apart) for i in range(lax.axis_si...  0.58 us
  transfers between devices with their start and end apart: 10, of which 3 were waited for; matrix products, arithmetic and copies ran while one was open for 0% of the time, Pallas kernels for 10%

profile of v8, /device:TPU:0, one launch (start us, length us, event | category | flops | bytes accessed | tf_op | source)
XLA Modules:
  0.0 20.6 jit_solution(17924487831833715308)
XLA Ops:
  0.6 0.0 copy-start.1
  0.6 0.0 copy-start.4
  0.7 0.0 copy-start.5
  0.7 1.2 %shard_map.192 = (s32[5,1,16]{2,1,0:T(1,128)S(1)}, bf16[128,256]{1,0:T(8,128)(2,1)S(1)}, s32[1,384]{1,0:T(1,128)S(1)}, s32[1,384]{1,0:T(1,128)S(1)}, s32[5,1,64]...) custom-call(s32[5,1,16]{2,1,0:T(1,128)} %bitcast.22, ...), custom_call_target="tpu_custom_call" | custom-call | flops 4000000000 | bytes 73536 | tf_op jit(solution)/shard_map/pallas_call | solution.py:223
  1.8 4.1 %collective-permute-start = (bf16[16,256]{1,0:T(8,128)(2,1)S(1)}, bf16[16,256]{1,0:T(8,128)(2,1)S(1)}, u32[]{:S(2)}, u32[]{:S(2)}) collective-permute-start(bf16[16,256]{1,0:T(8,128)(2,1)S(1)} %get-tuple-element.75), channel_id=1, source_target_pairs={{0,4},{1,5},{2,6},{3,7},{4,0},{5,1},{6,2},{7,3},{8,12},{9,13},{10,... | collective-permute-start | bytes 24584 | tf_op jit(solution)/shard_map/ppermute | solution.py:22
  5.9 1.6 %collective-permute-start.1 = (bf16[16,256]{1,0:T(8,128)(2,1)S(1)}, bf16[16,256]{1,0:T(8,128)(2,1)S(1)}, u32[]{:S(2)}, u32[]{:S(2)}) collective-permute-start(bf16[16,256]{1,0:T(8,128)(2,1)S(1)} %get-tuple-element.76), channel_id=1, source_target_pairs={{0,2},{1,3},{2,0},{3,1},{4,6},{5,7},{6,4},{7,5},{8,10},{9,11},{10,... | collective-permute-start | bytes 24584 | tf_op jit(solution)/shard_map/ppermute | solution.py:22
  7.5 1.5 %collective-permute-start.2 = (bf16[16,256]{1,0:T(8,128)(2,1)S(1)}, bf16[16,256]{1,0:T(8,128)(2,1)S(1)}, u32[]{:S(2)}, u32[]{:S(2)}) collective-permute-start(bf16[16,256]{1,0:T(8,128)(2,1)S(1)} %get-tuple-element.77), channel_id=1, source_target_pairs={{0,1},{1,0},{2,3},{3,2},{4,5},{5,4},{6,7},{7,6},{8,9},{9,8},{10,11... | collective-permute-start | bytes 24584 | tf_op jit(solution)/shard_map/ppermute | solution.py:22
  9.0 1.5 %collective-permute-start.3 = (bf16[16,256]{1,0:T(8,128)(2,1)S(1)}, bf16[16,256]{1,0:T(8,128)(2,1)S(1)}, u32[]{:S(2)}, u32[]{:S(2)}) collective-permute-start(bf16[16,256]{1,0:T(8,128)(2,1)S(1)} %get-tuple-element.78), channel_id=1, source_target_pairs={{0,16},{8,24},{16,0},{24,8},{1,17},{9,25},{17,1},{25,9},{2,18},{10... | collective-permute-start | bytes 24584 | tf_op jit(solution)/shard_map/ppermute | solution.py:22
  10.5 0.0 collective-permute-start.4
  11.2 0.0 copy-start
  11.2 0.0 copy-start.2
  11.2 0.0 copy-start.3
  11.3 1.2 %shard_map.193 = (bf16[384,128]{1,0:T(8,128)(2,1)S(1)}, f32[384,256]{1,0:T(8,128)S(1)}, f32[384,1]{1,0:T(8,128)S(1)}, f32[384,256]{1,0:T(8,128)S(1)}, f32[128,25...) custom-call(s32[1]{0:T(128)S(6)} %copy.22.edge_count, ...), custom_call_target="tpu_custom_call" | custom-call | flops 4000000000 | bytes 956228 | tf_op jit(solution)/shard_map/pallas_call | solution.py:223
  12.5 0.0 collective-permute-done.rest_4_
  12.5 0.0 collective-permute-done.1.rest_3_
  12.5 0.0 collective-permute-done.2.rest_2_
  12.5 0.2 collective-permute-done.3.rest_1_
  12.7 0.0 collective-permute-done.4.rest_0_
  12.7 0.0 copy-done.3
  12.7 2.1 %shard_map.194 = (bf16[128,256]{1,0:T(8,128)(2,1)S(1)}, bf16[128,256]{1,0:T(8,128)(2,1)S(1)}, bf16[320,256]{1,0:T(8,128)(2,1)S(1)}, bf16[16,256]{1,0:T(8,128)(2,...) custom-call(bf16[128,256]{1,0:T(8,128)(2,1)S(1)} %get-tuple-element., ...), custom_call_target="tpu_custom_call" | custom-call | flops 251658240 | bytes 2119680 | tf_op jit(solution)/shard_map/pallas_call | solution.py:223
  14.8 0.4 %collective-permute-start.5 = (bf16[16,256]{1,0:T(8,128)(2,1)S(1)}, bf16[16,256]{1,0:T(8,128)(2,1)S(1)}, u32[]{:S(2)}, u32[]{:S(2)}) collective-permute-start(bf16[16,256]{1,0:T(8,128)(2,1)S(1)} %get-tuple-element.100), channel_id=1, source_target_pairs={{0,4},{1,5},{2,6},{3,7},{4,0},{5,1},{6,2},{7,3},{8,12},{9,13},{10,... | collective-permute-start | bytes 24584 | tf_op jit(solution)/shard_map/ppermute | solution.py:22
  15.2 0.5 %collective-permute-start.6 = (bf16[16,256]{1,0:T(8,128)(2,1)S(1)}, bf16[16,256]{1,0:T(8,128)(2,1)S(1)}, u32[]{:S(2)}, u32[]{:S(2)}) collective-permute-start(bf16[16,256]{1,0:T(8,128)(2,1)S(1)} %get-tuple-element.101), channel_id=1, source_target_pairs={{0,2},{1,3},{2,0},{3,1},{4,6},{5,7},{6,4},{7,5},{8,10},{9,11},{10,... | collective-permute-start | bytes 24584 | tf_op jit(solution)/shard_map/ppermute | solution.py:22
  15.7 0.3 %collective-permute-start.7 = (bf16[16,256]{1,0:T(8,128)(2,1)S(1)}, bf16[16,256]{1,0:T(8,128)(2,1)S(1)}, u32[]{:S(2)}, u32[]{:S(2)}) collective-permute-start(bf16[16,256]{1,0:T(8,128)(2,1)S(1)} %get-tuple-element.102), channel_id=1, source_target_pairs={{0,1},{1,0},{2,3},{3,2},{4,5},{5,4},{6,7},{7,6},{8,9},{9,8},{10,11... | collective-permute-start | bytes 24584 | tf_op jit(solution)/shard_map/ppermute | solution.py:22
  16.0 1.7 %collective-permute-start.8 = (bf16[16,256]{1,0:T(8,128)(2,1)S(1)}, bf16[16,256]{1,0:T(8,128)(2,1)S(1)}, u32[]{:S(2)}, u32[]{:S(2)}) collective-permute-start(bf16[16,256]{1,0:T(8,128)(2,1)S(1)} %get-tuple-element.103), channel_id=1, source_target_pairs={{0,16},{8,24},{16,0},{24,8},{1,17},{9,25},{17,1},{25,9},{2,18},{10... | collective-permute-start | bytes 24584 | tf_op jit(solution)/shard_map/ppermute | solution.py:22
  17.7 0.0 collective-permute-start.9
  18.3 1.0 %shard_map.195 = (bf16[128,256]{1,0:T(8,128)(2,1)S(1)}, bf16[384,256]{1,0:T(8,128)(2,1)S(1)}, bf16[320,256]{1,0:T(8,128)(2,1)S(1)}, f32[128,256]{1,0:T(8,128)S(1)}) custom-call(s32[1]{0:T(128)S(6)} %copy.21.node_count, bf16[128,256]{1,0:T(8,128)(2,1)S(1)} %get-tuple-element.85.grad_nodes, bf16[512,256]{1,0:T(8,128)(2,1)S(1)} %copy-done, ...), custom_call_target="tpu_custom_call" | custom-call | tf_op jit(solution)/shard_map/pallas_call | solution.py:223
  19.3 0.1 collective-permute-done.5.rest_4_
  19.4 0.0 collective-permute-done.6.rest_3_
  19.4 0.0 collective-permute-done.7.rest_2_
  19.4 0.2 %collective-permute-done.8.rest_1_ = bf16[16,256]{1,0:T(8,128)(2,1)S(1)} collective-permute-done((bf16[16,256]{1,0:T(8,128)(2,1)S(1)}, bf16[16,256]{1,0:T(8,128)(2,1)S(1)}, u32[]{:S(2)}, u32[]{:S(2)}) %collective-permute-start.8) | collective-permute-done | bytes 8224 | tf_op jit(solution)/shard_map/ppermute | solution.py:22
  19.7 0.0 collective-permute-done.9.rest_0_
  19.7 0.9 %shard_map.196 = (bf16[128,256]{1,0:T(8,128)(2,1)}, bf16[384,256]{1,0:T(8,128)(2,1)}, bf16[320,256]{1,0:T(8,128)(2,1)}, bf16[128,256]{1,0:T(8,128)(2,1)}) custom-call(f32[128,256]{1,0:T(8,128)S(1)} %get-tuple-element.95.total, bf16[128,80]{1,0:T(8,128)(2,1)S(1)} %get-tuple-element.96.scatter_boundary, bf16[256,768]{1,0:T(8,128)(2,1)S(1)} %get-tuple-element.90.first_t, ...), custom_call_target="tpu_custom_call" | custom-call | flops 33554432 | bytes 1011712 | tf_op jit(solution)/shard_map/pallas_call | solution.py:223
  (7 shorter events, 0.0 us)
Async XLA Ops:
  0.6 10.6 %copy-start.1 = (bf16[768,256]{1,0:T(8,128)(2,1)S(1)}, bf16[768,256]{1,0:T(8,128)(2,1)}, u32[]{:S(2)}) copy-start(bf16[768,256]{1,0:T(8,128)(2,1)} %edge_first.3) | copy-start | bytes 1179652
  0.6 10.6 %copy-start.4 = (bf16[1,384,256]{2,1,0:T(8,128)(2,1)S(1)}, bf16[1,384,256]{2,1,0:T(8,128)(2,1)}, u32[]{:S(2)}) copy-start(bf16[1,384,256]{2,1,0:T(8,128)(2,1)} %param.18) | copy-start | bytes 589828
  0.7 10.6 %copy-start.5 = (bf16[1,5,64,256]{3,2,1,0:T(8,128)(2,1)S(1)}, bf16[1,5,64,256]{3,2,1,0:T(8,128)(2,1)}, u32[]{:S(2)}) copy-start(bf16[1,5,64,256]{3,2,1,0:T(8,128)(2,1)} %param.19) | copy-start | bytes 491524
  0.7 10.6 %copy-start.6 = (bf16[256,256]{1,0:T(8,128)(2,1)S(1)}, bf16[256,256]{1,0:T(8,128)(2,1)}, u32[]{:S(2)}) copy-start(bf16[256,256]{1,0:T(8,128)(2,1)} %edge_second.1) | copy-start | bytes 393220
  1.8 10.6 %collective-permute-start = (bf16[16,256]{1,0:T(8,128)(2,1)S(1)}, bf16[16,256]{1,0:T(8,128)(2,1)S(1)}, u32[]{:S(2)}, u32[]{:S(2)}) collective-permute-start(bf16[16,256]{1,0:T(8,128)(2,1)S(1)} %get-tuple-element.75), channel_id=1, source_target_pairs={{0,4},{1,5},{2,6},{3,7},{4,0},{5,1},{6,2},{7,3},{8,12},{9,13},{10,... | collective-permute-start | bytes 24584 | tf_op jit(solution)/shard_map/ppermute | solution.py:22
  5.9 6.5 %collective-permute-start.1 = (bf16[16,256]{1,0:T(8,128)(2,1)S(1)}, bf16[16,256]{1,0:T(8,128)(2,1)S(1)}, u32[]{:S(2)}, u32[]{:S(2)}) collective-permute-start(bf16[16,256]{1,0:T(8,128)(2,1)S(1)} %get-tuple-element.76), channel_id=1, source_target_pairs={{0,2},{1,3},{2,0},{3,1},{4,6},{5,7},{6,4},{7,5},{8,10},{9,11},{10,... | collective-permute-start | bytes 24584 | tf_op jit(solution)/shard_map/ppermute | solution.py:22
  7.5 5.0 %collective-permute-start.2 = (bf16[16,256]{1,0:T(8,128)(2,1)S(1)}, bf16[16,256]{1,0:T(8,128)(2,1)S(1)}, u32[]{:S(2)}, u32[]{:S(2)}) collective-permute-start(bf16[16,256]{1,0:T(8,128)(2,1)S(1)} %get-tuple-element.77), channel_id=1, source_target_pairs={{0,1},{1,0},{2,3},{3,2},{4,5},{5,4},{6,7},{7,6},{8,9},{9,8},{10,11... | collective-permute-start | bytes 24584 | tf_op jit(solution)/shard_map/ppermute | solution.py:22
  9.0 3.7 %collective-permute-start.3 = (bf16[16,256]{1,0:T(8,128)(2,1)S(1)}, bf16[16,256]{1,0:T(8,128)(2,1)S(1)}, u32[]{:S(2)}, u32[]{:S(2)}) collective-permute-start(bf16[16,256]{1,0:T(8,128)(2,1)S(1)} %get-tuple-element.78), channel_id=1, source_target_pairs={{0,16},{8,24},{16,0},{24,8},{1,17},{9,25},{17,1},{25,9},{2,18},{10... | collective-permute-start | bytes 24584 | tf_op jit(solution)/shard_map/ppermute | solution.py:22
  10.5 2.2 %collective-permute-start.4 = (bf16[16,256]{1,0:T(8,128)(2,1)S(1)}, bf16[16,256]{1,0:T(8,128)(2,1)S(1)}, u32[]{:S(2)}, u32[]{:S(2)}) collective-permute-start(bf16[16,256]{1,0:T(8,128)(2,1)S(1)} %get-tuple-element.79), channel_id=1, source_target_pairs={{0,8},{8,0},{16,24},{24,16},{1,9},{9,1},{17,25},{25,17},{2,10},{10... | collective-permute-start | bytes 24584 | tf_op jit(solution)/shard_map/ppermute | solution.py:22
  11.2 1.5 %copy-start = (bf16[512,256]{1,0:T(8,128)(2,1)S(1)}, bf16[512,256]{1,0:T(8,128)(2,1)}, u32[]{:S(2)}) copy-start(bf16[512,256]{1,0:T(8,128)(2,1)} %node_first.3) | copy-start | bytes 786436
  11.2 1.5 %copy-start.2 = (bf16[1,128,256]{2,1,0:T(8,128)(2,1)S(1)}, bf16[1,128,256]{2,1,0:T(8,128)(2,1)}, u32[]{:S(2)}) copy-start(bf16[1,128,256]{2,1,0:T(8,128)(2,1)} %param.20) | copy-start | bytes 196612
  11.2 1.5 %copy-start.3 = (bf16[256,256]{1,0:T(8,128)(2,1)S(1)}, bf16[256,256]{1,0:T(8,128)(2,1)}, u32[]{:S(2)}) copy-start(bf16[256,256]{1,0:T(8,128)(2,1)} %node_second.1) | copy-start | bytes 393220
  14.8 4.6 %collective-permute-start.5 = (bf16[16,256]{1,0:T(8,128)(2,1)S(1)}, bf16[16,256]{1,0:T(8,128)(2,1)S(1)}, u32[]{:S(2)}, u32[]{:S(2)}) collective-permute-start(bf16[16,256]{1,0:T(8,128)(2,1)S(1)} %get-tuple-element.100), channel_id=1, source_target_pairs={{0,4},{1,5},{2,6},{3,7},{4,0},{5,1},{6,2},{7,3},{8,12},{9,13},{10,... | collective-permute-start | bytes 24584 | tf_op jit(solution)/shard_map/ppermute | solution.py:22
  15.2 4.2 %collective-permute-start.6 = (bf16[16,256]{1,0:T(8,128)(2,1)S(1)}, bf16[16,256]{1,0:T(8,128)(2,1)S(1)}, u32[]{:S(2)}, u32[]{:S(2)}) collective-permute-start(bf16[16,256]{1,0:T(8,128)(2,1)S(1)} %get-tuple-element.101), channel_id=1, source_target_pairs={{0,2},{1,3},{2,0},{3,1},{4,6},{5,7},{6,4},{7,5},{8,10},{9,11},{10,... | collective-permute-start | bytes 24584 | tf_op jit(solution)/shard_map/ppermute | solution.py:22
  15.7 3.8 %collective-permute-start.7 = (bf16[16,256]{1,0:T(8,128)(2,1)S(1)}, bf16[16,256]{1,0:T(8,128)(2,1)S(1)}, u32[]{:S(2)}, u32[]{:S(2)}) collective-permute-start(bf16[16,256]{1,0:T(8,128)(2,1)S(1)} %get-tuple-element.102), channel_id=1, source_target_pairs={{0,1},{1,0},{2,3},{3,2},{4,5},{5,4},{6,7},{7,6},{8,9},{9,8},{10,11... | collective-permute-start | bytes 24584 | tf_op jit(solution)/shard_map/ppermute | solution.py:22
  16.0 3.7 %collective-permute-start.8 = (bf16[16,256]{1,0:T(8,128)(2,1)S(1)}, bf16[16,256]{1,0:T(8,128)(2,1)S(1)}, u32[]{:S(2)}, u32[]{:S(2)}) collective-permute-start(bf16[16,256]{1,0:T(8,128)(2,1)S(1)} %get-tuple-element.103), channel_id=1, source_target_pairs={{0,16},{8,24},{16,0},{24,8},{1,17},{9,25},{17,1},{25,9},{2,18},{10... | collective-permute-start | bytes 24584 | tf_op jit(solution)/shard_map/ppermute | solution.py:22
  17.7 2.0 %collective-permute-start.9 = (bf16[16,256]{1,0:T(8,128)(2,1)S(1)}, bf16[16,256]{1,0:T(8,128)(2,1)S(1)}, u32[]{:S(2)}, u32[]{:S(2)}) collective-permute-start(bf16[16,256]{1,0:T(8,128)(2,1)S(1)} %get-tuple-element.104), channel_id=1, source_target_pairs={{0,8},{8,0},{16,24},{24,16},{1,9},{9,1},{17,25},{25,17},{2,10},{10... | collective-permute-start | bytes 24584 | tf_op jit(solution)/shard_map/ppermute | solution.py:22

commit v9 on v7

--- a/solution.py
+++ b/solution.py
@@ -265,7 +265,7 @@
     sent = outs[len(held) :]
     arrived = exchange(sent)
     slots = ROUNDS * send
-    some = -(-slots // 32) * 32
+    some = slots
     all_slots = -(-slots // 128) * 128
     outs = call(
         inner_kernel,

time: 20.8 us -> 20.8 us (level)
  no operation moved by 1% of the time
where the time goes in v9:
time: 20.8 us; the launch traced here: 20.6 us
  starting transfers between devices  11.5 us (55%)
  Pallas kernels  6.35 us (31%)
  between operations  2.1 us (10%)
  waiting for transfers between devices  0.59 us (3%)
    ppermute x10, starting transfers between devices, partner(): lax.ppermute(shard, axis, [(i, i ^ 1 << apart) for i in range(lax.axis_si...  11.5 us
    pallas_call x5, Pallas kernels, call(): pl.pallas_call(kernel, out_shape=out_shape, in_specs=[SMEM if a.ndim == 1...  6.35 us
    ppermute x10, waiting for transfers between devices, partner(): lax.ppermute(shard, axis, [(i, i ^ 1 << apart) for i in range(lax.axis_si...  0.59 us
  transfers between devices with their start and end apart: 10, of which 3 were waited for; matrix products, arithmetic and copies ran while one was open for 0% of the time, Pallas kernels for 10%

profile of v9, /device:TPU:0, one launch (start us, length us, event | category | flops | bytes accessed | tf_op | source)
XLA Modules:
  0.0 20.6 jit_solution(9630049019616026748)
XLA Ops:
  0.6 0.0 copy-start.1
  0.6 0.0 copy-start.4
  0.7 0.0 copy-start.5
  0.7 1.2 %shard_map.192 = (s32[5,1,16]{2,1,0:T(1,128)S(1)}, bf16[128,256]{1,0:T(8,128)(2,1)S(1)}, s32[1,384]{1,0:T(1,128)S(1)}, s32[1,384]{1,0:T(1,128)S(1)}, s32[5,1,64]...) custom-call(s32[5,1,16]{2,1,0:T(1,128)} %bitcast.21, ...), custom_call_target="tpu_custom_call" | custom-call | flops 4000000000 | bytes 73536 | tf_op jit(solution)/shard_map/pallas_call | solution.py:224
  1.8 4.1 %collective-permute-start = (bf16[16,256]{1,0:T(8,128)(2,1)S(1)}, bf16[16,256]{1,0:T(8,128)(2,1)S(1)}, u32[]{:S(2)}, u32[]{:S(2)}) collective-permute-start(bf16[16,256]{1,0:T(8,128)(2,1)S(1)} %get-tuple-element.76), channel_id=1, source_target_pairs={{0,4},{1,5},{2,6},{3,7},{4,0},{5,1},{6,2},{7,3},{8,12},{9,13},{10,... | collective-permute-start | bytes 24584 | tf_op jit(solution)/shard_map/ppermute | solution.py:22
  5.9 1.6 %collective-permute-start.1 = (bf16[16,256]{1,0:T(8,128)(2,1)S(1)}, bf16[16,256]{1,0:T(8,128)(2,1)S(1)}, u32[]{:S(2)}, u32[]{:S(2)}) collective-permute-start(bf16[16,256]{1,0:T(8,128)(2,1)S(1)} %get-tuple-element.77), channel_id=1, source_target_pairs={{0,2},{1,3},{2,0},{3,1},{4,6},{5,7},{6,4},{7,5},{8,10},{9,11},{10,... | collective-permute-start | bytes 24584 | tf_op jit(solution)/shard_map/ppermute | solution.py:22
  7.5 1.5 %collective-permute-start.2 = (bf16[16,256]{1,0:T(8,128)(2,1)S(1)}, bf16[16,256]{1,0:T(8,128)(2,1)S(1)}, u32[]{:S(2)}, u32[]{:S(2)}) collective-permute-start(bf16[16,256]{1,0:T(8,128)(2,1)S(1)} %get-tuple-element.78), channel_id=1, source_target_pairs={{0,1},{1,0},{2,3},{3,2},{4,5},{5,4},{6,7},{7,6},{8,9},{9,8},{10,11... | collective-permute-start | bytes 24584 | tf_op jit(solution)/shard_map/ppermute | solution.py:22
  9.0 1.5 %collective-permute-start.3 = (bf16[16,256]{1,0:T(8,128)(2,1)S(1)}, bf16[16,256]{1,0:T(8,128)(2,1)S(1)}, u32[]{:S(2)}, u32[]{:S(2)}) collective-permute-start(bf16[16,256]{1,0:T(8,128)(2,1)S(1)} %get-tuple-element.79), channel_id=1, source_target_pairs={{0,16},{8,24},{16,0},{24,8},{1,17},{9,25},{17,1},{25,9},{2,18},{10... | collective-permute-start | bytes 24584 | tf_op jit(solution)/shard_map/ppermute | solution.py:22
  10.5 0.0 collective-permute-start.4
  11.2 0.0 copy-start
  11.2 0.0 copy-start.2
  11.2 0.0 copy-start.3
  11.3 1.2 %shard_map.193 = (bf16[384,128]{1,0:T(8,128)(2,1)S(1)}, f32[384,256]{1,0:T(8,128)S(1)}, f32[384,1]{1,0:T(8,128)S(1)}, f32[384,256]{1,0:T(8,128)S(1)}, f32[128,25...) custom-call(s32[1]{0:T(128)S(6)} %copy.22.edge_count, ...), custom_call_target="tpu_custom_call" | custom-call | flops 4000000000 | bytes 956228 | tf_op jit(solution)/shard_map/pallas_call | solution.py:224
  12.5 0.0 collective-permute-done.rest_4_
  12.5 0.0 collective-permute-done.1.rest_3_
  12.5 0.0 collective-permute-done.2.rest_2_
  12.5 0.2 collective-permute-done.3.rest_1_
  12.7 0.0 collective-permute-done.4.rest_0_
  12.7 0.0 copy-done.3
  12.7 2.1 %shard_map.194 = (bf16[128,256]{1,0:T(8,128)(2,1)S(1)}, f32[128,256]{1,0:T(8,128)S(1)}, bf16[128,256]{1,0:T(8,128)(2,1)S(1)}, bf16[320,256]{1,0:T(8,128)(2,1)S(1...) custom-call(bf16[128,256]{1,0:T(8,128)(2,1)S(1)} %get-tuple-element., ...), custom_call_target="tpu_custom_call" | custom-call | flops 251658240 | bytes 2109440 | tf_op jit(solution)/shard_map/pallas_call | solution.py:224
  14.8 0.4 %collective-permute-start.5 = (bf16[16,256]{1,0:T(8,128)(2,1)S(1)}, bf16[16,256]{1,0:T(8,128)(2,1)S(1)}, u32[]{:S(2)}, u32[]{:S(2)}) collective-permute-start(bf16[16,256]{1,0:T(8,128)(2,1)S(1)} %get-tuple-element.102), channel_id=1, source_target_pairs={{0,4},{1,5},{2,6},{3,7},{4,0},{5,1},{6,2},{7,3},{8,12},{9,13},{10,... | collective-permute-start | bytes 24584 | tf_op jit(solution)/shard_map/ppermute | solution.py:22
  15.2 0.4 %collective-permute-start.6 = (bf16[16,256]{1,0:T(8,128)(2,1)S(1)}, bf16[16,256]{1,0:T(8,128)(2,1)S(1)}, u32[]{:S(2)}, u32[]{:S(2)}) collective-permute-start(bf16[16,256]{1,0:T(8,128)(2,1)S(1)} %get-tuple-element.103), channel_id=1, source_target_pairs={{0,2},{1,3},{2,0},{3,1},{4,6},{5,7},{6,4},{7,5},{8,10},{9,11},{10,... | collective-permute-start | bytes 24584 | tf_op jit(solution)/shard_map/ppermute | solution.py:22
  15.7 0.3 %collective-permute-start.7 = (bf16[16,256]{1,0:T(8,128)(2,1)S(1)}, bf16[16,256]{1,0:T(8,128)(2,1)S(1)}, u32[]{:S(2)}, u32[]{:S(2)}) collective-permute-start(bf16[16,256]{1,0:T(8,128)(2,1)S(1)} %get-tuple-element.104), channel_id=1, source_target_pairs={{0,1},{1,0},{2,3},{3,2},{4,5},{5,4},{6,7},{7,6},{8,9},{9,8},{10,11... | collective-permute-start | bytes 24584 | tf_op jit(solution)/shard_map/ppermute | solution.py:22
  16.0 1.7 %collective-permute-start.8 = (bf16[16,256]{1,0:T(8,128)(2,1)S(1)}, bf16[16,256]{1,0:T(8,128)(2,1)S(1)}, u32[]{:S(2)}, u32[]{:S(2)}) collective-permute-start(bf16[16,256]{1,0:T(8,128)(2,1)S(1)} %get-tuple-element.105), channel_id=1, source_target_pairs={{0,16},{8,24},{16,0},{24,8},{1,17},{9,25},{17,1},{25,9},{2,18},{10... | collective-permute-start | bytes 24584 | tf_op jit(solution)/shard_map/ppermute | solution.py:22
  17.7 0.0 collective-permute-start.9
  18.3 1.0 %shard_map.195 = (bf16[128,256]{1,0:T(8,128)(2,1)S(1)}, bf16[384,256]{1,0:T(8,128)(2,1)S(1)}, bf16[320,256]{1,0:T(8,128)(2,1)S(1)}, f32[128,256]{1,0:T(8,128)S(1)}) custom-call(s32[1]{0:T(128)S(6)} %copy.21.node_count, bf16[128,256]{1,0:T(8,128)(2,1)S(1)} %get-tuple-element.86.grad_nodes, bf16[512,256]{1,0:T(8,128)(2,1)S(1)} %copy-done, ...), custom_call_target="tpu_custom_call" | custom-call | tf_op jit(solution)/shard_map/pallas_call | solution.py:224
  19.3 0.1 collective-permute-done.5.rest_4_
  19.4 0.0 collective-permute-done.6.rest_3_
  19.4 0.0 collective-permute-done.7.rest_2_
  19.4 0.2 %collective-permute-done.8.rest_1_ = bf16[16,256]{1,0:T(8,128)(2,1)S(1)} collective-permute-done((bf16[16,256]{1,0:T(8,128)(2,1)S(1)}, bf16[16,256]{1,0:T(8,128)(2,1)S(1)}, u32[]{:S(2)}, u32[]{:S(2)}) %collective-permute-start.8) | collective-permute-done | bytes 8224 | tf_op jit(solution)/shard_map/ppermute | solution.py:22
  19.7 0.0 collective-permute-done.9.rest_0_
  19.7 0.9 %shard_map.196 = (bf16[128,256]{1,0:T(8,128)(2,1)}, bf16[384,256]{1,0:T(8,128)(2,1)}, bf16[320,256]{1,0:T(8,128)(2,1)}, bf16[128,256]{1,0:T(8,128)(2,1)}) custom-call(f32[128,256]{1,0:T(8,128)S(1)} %get-tuple-element.97.total, bf16[128,80]{1,0:T(8,128)(2,1)S(1)} %get-tuple-element.98.scatter_boundary, bf16[256,768]{1,0:T(8,128)(2,1)S(1)} %get-tuple-element.91.first_t, ...), custom_call_target="tpu_custom_call" | custom-call | flops 33554432 | bytes 1011712 | tf_op jit(solution)/shard_map/pallas_call | solution.py:224
  (7 shorter events, 0.0 us)
Async XLA Ops:
  0.6 10.6 %copy-start.1 = (bf16[768,256]{1,0:T(8,128)(2,1)S(1)}, bf16[768,256]{1,0:T(8,128)(2,1)}, u32[]{:S(2)}) copy-start(bf16[768,256]{1,0:T(8,128)(2,1)} %edge_first.3) | copy-start | bytes 1179652
  0.6 10.6 %copy-start.4 = (bf16[1,384,256]{2,1,0:T(8,128)(2,1)S(1)}, bf16[1,384,256]{2,1,0:T(8,128)(2,1)}, u32[]{:S(2)}) copy-start(bf16[1,384,256]{2,1,0:T(8,128)(2,1)} %param.18) | copy-start | bytes 589828
  0.7 10.6 %copy-start.5 = (bf16[1,5,64,256]{3,2,1,0:T(8,128)(2,1)S(1)}, bf16[1,5,64,256]{3,2,1,0:T(8,128)(2,1)}, u32[]{:S(2)}) copy-start(bf16[1,5,64,256]{3,2,1,0:T(8,128)(2,1)} %param.19) | copy-start | bytes 491524
  0.7 10.6 %copy-start.6 = (bf16[256,256]{1,0:T(8,128)(2,1)S(1)}, bf16[256,256]{1,0:T(8,128)(2,1)}, u32[]{:S(2)}) copy-start(bf16[256,256]{1,0:T(8,128)(2,1)} %edge_second.1) | copy-start | bytes 393220
  1.8 10.6 %collective-permute-start = (bf16[16,256]{1,0:T(8,128)(2,1)S(1)}, bf16[16,256]{1,0:T(8,128)(2,1)S(1)}, u32[]{:S(2)}, u32[]{:S(2)}) collective-permute-start(bf16[16,256]{1,0:T(8,128)(2,1)S(1)} %get-tuple-element.76), channel_id=1, source_target_pairs={{0,4},{1,5},{2,6},{3,7},{4,0},{5,1},{6,2},{7,3},{8,12},{9,13},{10,... | collective-permute-start | bytes 24584 | tf_op jit(solution)/shard_map/ppermute | solution.py:22
  5.9 6.5 %collective-permute-start.1 = (bf16[16,256]{1,0:T(8,128)(2,1)S(1)}, bf16[16,256]{1,0:T(8,128)(2,1)S(1)}, u32[]{:S(2)}, u32[]{:S(2)}) collective-permute-start(bf16[16,256]{1,0:T(8,128)(2,1)S(1)} %get-tuple-element.77), channel_id=1, source_target_pairs={{0,2},{1,3},{2,0},{3,1},{4,6},{5,7},{6,4},{7,5},{8,10},{9,11},{10,... | collective-permute-start | bytes 24584 | tf_op jit(solution)/shard_map/ppermute | solution.py:22
  7.5 5.0 %collective-permute-start.2 = (bf16[16,256]{1,0:T(8,128)(2,1)S(1)}, bf16[16,256]{1,0:T(8,128)(2,1)S(1)}, u32[]{:S(2)}, u32[]{:S(2)}) collective-permute-start(bf16[16,256]{1,0:T(8,128)(2,1)S(1)} %get-tuple-element.78), channel_id=1, source_target_pairs={{0,1},{1,0},{2,3},{3,2},{4,5},{5,4},{6,7},{7,6},{8,9},{9,8},{10,11... | collective-permute-start | bytes 24584 | tf_op jit(solution)/shard_map/ppermute | solution.py:22
  9.0 3.7 %collective-permute-start.3 = (bf16[16,256]{1,0:T(8,128)(2,1)S(1)}, bf16[16,256]{1,0:T(8,128)(2,1)S(1)}, u32[]{:S(2)}, u32[]{:S(2)}) collective-permute-start(bf16[16,256]{1,0:T(8,128)(2,1)S(1)} %get-tuple-element.79), channel_id=1, source_target_pairs={{0,16},{8,24},{16,0},{24,8},{1,17},{9,25},{17,1},{25,9},{2,18},{10... | collective-permute-start | bytes 24584 | tf_op jit(solution)/shard_map/ppermute | solution.py:22
  10.5 2.2 %collective-permute-start.4 = (bf16[16,256]{1,0:T(8,128)(2,1)S(1)}, bf16[16,256]{1,0:T(8,128)(2,1)S(1)}, u32[]{:S(2)}, u32[]{:S(2)}) collective-permute-start(bf16[16,256]{1,0:T(8,128)(2,1)S(1)} %get-tuple-element.80), channel_id=1, source_target_pairs={{0,8},{8,0},{16,24},{24,16},{1,9},{9,1},{17,25},{25,17},{2,10},{10... | collective-permute-start | bytes 24584 | tf_op jit(solution)/shard_map/ppermute | solution.py:22
  11.2 1.5 %copy-start = (bf16[512,256]{1,0:T(8,128)(2,1)S(1)}, bf16[512,256]{1,0:T(8,128)(2,1)}, u32[]{:S(2)}) copy-start(bf16[512,256]{1,0:T(8,128)(2,1)} %node_first.3) | copy-start | bytes 786436
  11.2 1.5 %copy-start.2 = (bf16[256,256]{1,0:T(8,128)(2,1)S(1)}, bf16[256,256]{1,0:T(8,128)(2,1)}, u32[]{:S(2)}) copy-start(bf16[256,256]{1,0:T(8,128)(2,1)} %node_second.1) | copy-start | bytes 393220
  11.2 1.5 %copy-start.3 = (bf16[1,128,256]{2,1,0:T(8,128)(2,1)S(1)}, bf16[1,128,256]{2,1,0:T(8,128)(2,1)}, u32[]{:S(2)}) copy-start(bf16[1,128,256]{2,1,0:T(8,128)(2,1)} %param.20) | copy-start | bytes 196612
  14.8 4.6 %collective-permute-start.5 = (bf16[16,256]{1,0:T(8,128)(2,1)S(1)}, bf16[16,256]{1,0:T(8,128)(2,1)S(1)}, u32[]{:S(2)}, u32[]{:S(2)}) collective-permute-start(bf16[16,256]{1,0:T(8,128)(2,1)S(1)} %get-tuple-element.102), channel_id=1, source_target_pairs={{0,4},{1,5},{2,6},{3,7},{4,0},{5,1},{6,2},{7,3},{8,12},{9,13},{10,... | collective-permute-start | bytes 24584 | tf_op jit(solution)/shard_map/ppermute | solution.py:22
  15.2 4.2 %collective-permute-start.6 = (bf16[16,256]{1,0:T(8,128)(2,1)S(1)}, bf16[16,256]{1,0:T(8,128)(2,1)S(1)}, u32[]{:S(2)}, u32[]{:S(2)}) collective-permute-start(bf16[16,256]{1,0:T(8,128)(2,1)S(1)} %get-tuple-element.103), channel_id=1, source_target_pairs={{0,2},{1,3},{2,0},{3,1},{4,6},{5,7},{6,4},{7,5},{8,10},{9,11},{10,... | collective-permute-start | bytes 24584 | tf_op jit(solution)/shard_map/ppermute | solution.py:22
  15.7 3.8 %collective-permute-start.7 = (bf16[16,256]{1,0:T(8,128)(2,1)S(1)}, bf16[16,256]{1,0:T(8,128)(2,1)S(1)}, u32[]{:S(2)}, u32[]{:S(2)}) collective-permute-start(bf16[16,256]{1,0:T(8,128)(2,1)S(1)} %get-tuple-element.104), channel_id=1, source_target_pairs={{0,1},{1,0},{2,3},{3,2},{4,5},{5,4},{6,7},{7,6},{8,9},{9,8},{10,11... | collective-permute-start | bytes 24584 | tf_op jit(solution)/shard_map/ppermute | solution.py:22
  16.0 3.7 %collective-permute-start.8 = (bf16[16,256]{1,0:T(8,128)(2,1)S(1)}, bf16[16,256]{1,0:T(8,128)(2,1)S(1)}, u32[]{:S(2)}, u32[]{:S(2)}) collective-permute-start(bf16[16,256]{1,0:T(8,128)(2,1)S(1)} %get-tuple-element.105), channel_id=1, source_target_pairs={{0,16},{8,24},{16,0},{24,8},{1,17},{9,25},{17,1},{25,9},{2,18},{10... | collective-permute-start | bytes 24584 | tf_op jit(solution)/shard_map/ppermute | solution.py:22
  17.7 2.0 %collective-permute-start.9 = (bf16[16,256]{1,0:T(8,128)(2,1)S(1)}, bf16[16,256]{1,0:T(8,128)(2,1)S(1)}, u32[]{:S(2)}, u32[]{:S(2)}) collective-permute-start(bf16[16,256]{1,0:T(8,128)(2,1)S(1)} %get-tuple-element.106), channel_id=1, source_target_pairs={{0,8},{8,0},{16,24},{24,16},{1,9},{9,1},{17,25},{25,17},{2,10},{10... | collective-permute-start | bytes 24584 | tf_op jit(solution)/shard_map/ppermute | solution.py:22
